TPU v7x, 32 devices: a whole 2x2x4 slice. The times are simulated.
32 devices in a mesh: dp: 8 (over z, y), rows: 4 (over x, core).
Axes of the slice: x: 2, y: 2, z: 4, core: 2. Of those that a mesh axis runs over, the one named last changes fastest.
Arguments:
- tokens: bfloat16 [32, 64, 64, 512], P('dp', 'rows'), may hold values from -6 to 6
- frame_level: int32 [32], P('dp'), may hold values from 0 to 2, as said below
- ln1_gain: bfloat16 [512], P(('dp', 'rows')), may hold values from 0.25 to 1.75
- ln1_bias: bfloat16 [512], P(('dp', 'rows')), may hold values from -1.5 to 1.5
- qkv_weight: bfloat16 [512, 1536], P(('dp', 'rows')), may hold values from -0.25 to 0.25
- qv_bias: bfloat16 [1024], P(('dp', 'rows')), may hold values from -2.5 to 2.5
- proj_weight: bfloat16 [512, 512], P(('dp', 'rows')), may hold values from -1 to 1
- proj_bias: bfloat16 [512], P(('dp', 'rows')), may hold values from -1.5 to 1.5
- ln2_gain: bfloat16 [512], P(('dp', 'rows')), may hold values from 0.25 to 1.75
- ln2_bias: bfloat16 [512], P(('dp', 'rows')), may hold values from -1.5 to 1.5
- fc1_weight: bfloat16 [512, 2048], P(('dp', 'rows')), may hold values from -0.25 to 0.25
- fc1_bias: bfloat16 [2048], P(('dp', 'rows')), may hold values from -2.5 to 2.5
- fc2_weight: bfloat16 [2048, 512], P(('dp', 'rows')), may hold values from -0.1875 to 0.1875
- fc2_bias: bfloat16 [512], P(('dp', 'rows')), may hold values from -1.5 to 1.5
- d_out: bfloat16 [32, 64, 64, 512], P('dp', 'rows'), may hold values from -6 to 6
Outputs:
- mixed: bfloat16 [32, 64, 64, 512], P('dp', 'rows')
- grad_tokens: bfloat16 [32, 64, 64, 512], P('dp', 'rows')
- grad_ln1_gain: float32 [512], P(('dp', 'rows'))
- grad_ln1_bias: float32 [512], P(('dp', 'rows'))
- grad_qkv_weight: float32 [512, 1536], P(('dp', 'rows'))
- grad_qv_bias: float32 [1024], P(('dp', 'rows'))
- grad_proj_weight: float32 [512, 512], P(('dp', 'rows'))
- grad_proj_bias: float32 [512], P(('dp', 'rows'))
- grad_ln2_gain: float32 [512], P(('dp', 'rows'))
- grad_ln2_bias: float32 [512], P(('dp', 'rows'))
- grad_fc1_weight: float32 [512, 2048], P(('dp', 'rows'))
- grad_fc1_bias: float32 [2048], P(('dp', 'rows'))
- grad_fc2_weight: float32 [2048, 512], P(('dp', 'rows'))
- grad_fc2_bias: float32 [512], P(('dp', 'rows'))
Inputs may be any that keep to these rules, and one draw needn't show every extreme that they name: `frame_level`: in each aligned block of 4 frames, at least one frame has level 2.
All inputs are finite; a program needn't handle non-finite values.
Results may differ from a plain program's by a relative error of at most 0.012.
Values may be sent and summed in bfloat16 or wider, within the bound.
No kernel may reach another device: no remote copies, remote signals or barrier semaphores. Data moves between devices by JAX's collectives and lax.ppermute only.
A program may use at most 256 MiB of HBM per device.

v0:
```python
import jax
import jax.numpy as jnp
from jax import lax
from jax.sharding import PartitionSpec as P

HEAD_DIM = 64
WIN = 8


EPSILON = 1e-05
INV_ROOT_TWO = 0.7071067811865476
INV_ROOT_TWO_PI = 0.3989422804014327


def from_behind(x, axis, by):
    devices = lax.axis_size(axis)
    return lax.ppermute(x, axis, [(i, (i + by) % devices) for i in range(devices)])


def normalize(values):
    center = values - jnp.mean(values, axis=-1, keepdims=True)
    inverse = lax.rsqrt(jnp.mean(center * center, axis=-1, keepdims=True) + EPSILON)
    return (center * inverse, inverse)


def norm_back(grad, normed, inverse):
    return inverse * (
        grad
        - jnp.mean(grad, axis=-1, keepdims=True)
        - normed * jnp.mean(grad * normed, axis=-1, keepdims=True)
    )


def to_windows(grid, window):
    leading, rows_here, columns, depth = grid.shape
    divided = grid.reshape(leading, rows_here // window, window, columns // window, window, depth)
    divided = divided.transpose(0, 1, 3, 2, 4, 5)
    return divided.reshape(
        leading, rows_here // window * (columns // window), window * window, depth
    )


def from_windows(blocks, window, rows_here, columns):
    leading = blocks.shape[0]
    depth = blocks.shape[-1]
    divided = blocks.reshape(leading, rows_here // window, columns // window, window, window, depth)
    return divided.transpose(0, 1, 3, 2, 4, 5).reshape(leading, rows_here, columns, depth)


def region_of(index, length, window):
    return (index >= length - window).astype(jnp.int32) + (index >= length - window // 2).astype(
        jnp.int32
    )


def window_mask(levels, row_index, window, rows_here, height, columns):
    half_win = window // 2
    rolled_rows = row_index * rows_here + jnp.arange(rows_here, dtype=jnp.int32)
    rolled_cols = jnp.arange(columns, dtype=jnp.int32)
    factor = 1 + (levels >= 1).astype(jnp.int32) + 2 * (levels >= 2).astype(jnp.int32)
    row_valid = (rolled_rows + half_win) % height < (height * factor // 4)[:, None]
    col_valid = (rolled_cols + half_win) % columns < (columns * factor // 4)[:, None]
    usable = (row_valid[:, :, None] & col_valid[:, None, :]).astype(jnp.int32)[..., None]
    regions = (
        region_of(rolled_rows, height, window)[:, None] * 3
        + region_of(rolled_cols, columns, window)[None, :]
    )[None, :, :, None]
    usable_win = to_windows(usable, window)[..., 0]
    region_win = to_windows(regions, window)[..., 0]
    allowed = (region_win[..., :, None] == region_win[..., None, :]) & (
        usable_win[..., None, :] > 0
    )
    return jnp.where(allowed, 0.0, -100.0).astype(jnp.float32)[:, :, None]


def per_device(
    tokens,
    frame_level,
    ln1_gain,
    ln1_bias,
    qkv_weight,
    qv_bias,
    proj_weight,
    proj_bias,
    ln2_gain,
    ln2_bias,
    fc1_weight,
    fc1_bias,
    fc2_weight,
    fc2_bias,
    d_out,
):
    frames, rows_here, columns, model_width = tokens.shape
    window = WIN
    half_win = window // 2
    keep_rows = rows_here - half_win
    height = rows_here * lax.axis_size("rows")
    window_cells = window * window
    block_count = rows_here // window * (columns // window)
    head_count = model_width // HEAD_DIM
    scale = HEAD_DIM ** (-0.5)
    (
        gain_one,
        bias_one,
        weight_qkv,
        bias_qv,
        weight_proj,
        bias_proj,
        gain_two,
        bias_two,
        weight_up,
        bias_up,
        weight_down,
        bias_down,
    ) = (
        lax.all_gather(ln1_gain, ("dp", "rows"), axis=0, tiled=True),
        lax.all_gather(ln1_bias, ("dp", "rows"), axis=0, tiled=True),
        lax.all_gather(qkv_weight, ("dp", "rows"), axis=0, tiled=True),
        lax.all_gather(qv_bias, ("dp", "rows"), axis=0, tiled=True),
        lax.all_gather(proj_weight, ("dp", "rows"), axis=0, tiled=True),
        lax.all_gather(proj_bias, ("dp", "rows"), axis=0, tiled=True),
        lax.all_gather(ln2_gain, ("dp", "rows"), axis=0, tiled=True),
        lax.all_gather(ln2_bias, ("dp", "rows"), axis=0, tiled=True),
        lax.all_gather(fc1_weight, ("dp", "rows"), axis=0, tiled=True),
        lax.all_gather(fc1_bias, ("dp", "rows"), axis=0, tiled=True),
        lax.all_gather(fc2_weight, ("dp", "rows"), axis=0, tiled=True),
        lax.all_gather(fc2_bias, ("dp", "rows"), axis=0, tiled=True),
    )
    inputs = tokens.astype(jnp.float32)
    normed_one, inverse_one = normalize(inputs)
    hidden_one = (normed_one * gain_one + bias_one).astype(jnp.bfloat16)
    incoming = from_behind(hidden_one[:, :half_win], "rows", -1)
    window_in = jnp.roll(
        jnp.concatenate([hidden_one[:, half_win:], incoming], axis=1), -half_win, axis=2
    )
    window_in = window_in.reshape(-1, model_width)
    projected = jnp.dot(window_in, weight_qkv, preferred_element_type=jnp.float32)
    query = (projected[:, :model_width] + bias_qv[:model_width]).astype(jnp.bfloat16)
    keys = projected[:, model_width : 2 * model_width].astype(jnp.bfloat16)
    values = (projected[:, 2 * model_width :] + bias_qv[model_width:]).astype(jnp.bfloat16)

    def split_heads(flat):
        grid = flat.reshape(frames, rows_here, columns, model_width)
        return to_windows(grid, window).reshape(
            frames, block_count, window_cells, head_count, HEAD_DIM
        )

    def merge_grid(heads_form):
        return from_windows(
            heads_form.reshape(frames, block_count, window_cells, model_width),
            window,
            rows_here,
            columns,
        )

    query_heads = split_heads(query)
    key_heads = split_heads(keys)
    value_heads = split_heads(values)
    mask_bias = window_mask(frame_level, lax.axis_index("rows"), window, rows_here, height, columns)

    def scores_of():
        raw = jnp.einsum(
            "fbqhd,fbkhd->fbhqk", query_heads, key_heads, preferred_element_type=jnp.float32
        )
        return raw * scale + mask_bias

    scores = scores_of()
    row_max = jnp.max(scores, axis=-1, keepdims=True)
    exponent = jnp.exp(scores - row_max)
    row_sum = jnp.sum(exponent, axis=-1, keepdims=True)
    probs = (exponent / row_sum).astype(jnp.bfloat16)
    log_total = row_max + jnp.log(row_sum)
    attended = jnp.einsum(
        "fbhqk,fbkhd->fbqhd", probs, value_heads, preferred_element_type=jnp.float32
    ).astype(jnp.bfloat16)
    att_grid = jnp.roll(merge_grid(attended), half_win, axis=2)
    returned = from_behind(att_grid[:, keep_rows:], "rows", 1)
    own_attended = jnp.concatenate([returned, att_grid[:, :keep_rows]], axis=1).reshape(
        -1, model_width
    )
    middle = (
        inputs.reshape(-1, model_width)
        + jnp.dot(own_attended, weight_proj, preferred_element_type=jnp.float32)
        + bias_proj
    )
    normed_two, inverse_two = normalize(middle)
    hidden_two = (normed_two * gain_two + bias_two).astype(jnp.bfloat16)
    upward = jnp.dot(hidden_two, weight_up, preferred_element_type=jnp.float32) + bias_up
    gelu_out = jax.nn.gelu(upward, approximate=False).astype(jnp.bfloat16)
    result = middle + jnp.dot(gelu_out, weight_down, preferred_element_type=jnp.float32) + bias_down
    mixed = result.astype(jnp.bfloat16).reshape(tokens.shape)
    gain_one, weight_qkv, weight_proj, gain_two, weight_up, weight_down = (
        lax.all_gather(ln1_gain, ("dp", "rows"), axis=0, tiled=True),
        lax.all_gather(qkv_weight, ("dp", "rows"), axis=0, tiled=True),
        lax.all_gather(proj_weight, ("dp", "rows"), axis=0, tiled=True),
        lax.all_gather(ln2_gain, ("dp", "rows"), axis=0, tiled=True),
        lax.all_gather(fc1_weight, ("dp", "rows"), axis=0, tiled=True),
        lax.all_gather(fc2_weight, ("dp", "rows"), axis=0, tiled=True),
    )
    cotangent = d_out.reshape(-1, model_width)
    cotangent_full = cotangent.astype(jnp.float32)
    grad_bias_down = jnp.sum(cotangent_full, axis=0)
    grad_weight_down = jnp.einsum(
        "tf,tc->fc", gelu_out, cotangent, preferred_element_type=jnp.float32
    )
    grad_gelu = jnp.einsum("tc,fc->tf", cotangent, weight_down, preferred_element_type=jnp.float32)
    slope = (
        0.5 * (1.0 + lax.erf(upward * INV_ROOT_TWO))
        + upward * jnp.exp(-0.5 * upward * upward) * INV_ROOT_TWO_PI
    )
    grad_upward = (grad_gelu * slope).astype(jnp.bfloat16)
    grad_bias_up = jnp.sum(grad_upward.astype(jnp.float32), axis=0)
    grad_weight_up = jnp.einsum(
        "tc,tf->cf", hidden_two, grad_upward, preferred_element_type=jnp.float32
    )
    grad_hidden_two = jnp.einsum(
        "tf,cf->tc", grad_upward, weight_up, preferred_element_type=jnp.float32
    )
    grad_gain_two = jnp.sum(grad_hidden_two * normed_two, axis=0)
    grad_bias_two = jnp.sum(grad_hidden_two, axis=0)
    grad_middle = cotangent_full + norm_back(grad_hidden_two * gain_two, normed_two, inverse_two)
    grad_branch = grad_middle.astype(jnp.bfloat16)
    grad_bias_proj = jnp.sum(grad_branch.astype(jnp.float32), axis=0)
    grad_weight_proj = jnp.einsum(
        "tc,te->ce", own_attended, grad_branch, preferred_element_type=jnp.float32
    )
    grad_own = jnp.einsum("te,ce->tc", grad_branch, weight_proj, preferred_element_type=jnp.float32)
    grad_own = grad_own.astype(jnp.bfloat16).reshape(frames, rows_here, columns, model_width)
    incoming_grad = from_behind(grad_own[:, :half_win], "rows", -1)
    grad_window = jnp.roll(
        jnp.concatenate([grad_own[:, half_win:], incoming_grad], axis=1), -half_win, axis=2
    )
    grad_heads = to_windows(grad_window, window).reshape(
        frames, block_count, window_cells, head_count, HEAD_DIM
    )
    probs_full = jnp.exp(scores_of() - log_total)
    probs_low = probs_full.astype(jnp.bfloat16)
    grad_values = jnp.einsum(
        "fbhqk,fbqhd->fbkhd", probs_low, grad_heads, preferred_element_type=jnp.float32
    )
    grad_probs = jnp.einsum(
        "fbqhd,fbkhd->fbhqk", grad_heads, value_heads, preferred_element_type=jnp.float32
    )
    grad_scores = probs_full * (
        grad_probs - jnp.sum(grad_probs * probs_full, axis=-1, keepdims=True)
    )
    grad_scores = grad_scores.astype(jnp.bfloat16)
    grad_query = jnp.einsum(
        "fbhqk,fbkhd->fbqhd", grad_scores, key_heads, preferred_element_type=jnp.float32
    )
    grad_keys = jnp.einsum(
        "fbhqk,fbqhd->fbkhd", grad_scores, query_heads, preferred_element_type=jnp.float32
    )
    grad_query = merge_grid((grad_query * scale).astype(jnp.bfloat16)).reshape(-1, model_width)
    grad_keys = merge_grid((grad_keys * scale).astype(jnp.bfloat16)).reshape(-1, model_width)
    grad_values = merge_grid(grad_values.astype(jnp.bfloat16)).reshape(-1, model_width)
    grad_projected = jnp.concatenate([grad_query, grad_keys, grad_values], axis=1)
    grad_bias_qv = jnp.concatenate(
        [
            jnp.sum(grad_query.astype(jnp.float32), axis=0),
            jnp.sum(grad_values.astype(jnp.float32), axis=0),
        ]
    )
    grad_weight_qkv = jnp.einsum(
        "tc,te->ce", window_in, grad_projected, preferred_element_type=jnp.float32
    )
    grad_hidden_win = jnp.einsum(
        "te,ce->tc", grad_projected, weight_qkv, preferred_element_type=jnp.float32
    )
    grad_hidden_win = jnp.roll(
        grad_hidden_win.reshape(frames, rows_here, columns, model_width), half_win, axis=2
    )
    back_grad = from_behind(grad_hidden_win[:, keep_rows:].astype(jnp.bfloat16), "rows", 1).astype(
        jnp.float32
    )
    grad_hidden_one = jnp.concatenate([back_grad, grad_hidden_win[:, :keep_rows]], axis=1)
    grad_gain_one = jnp.sum(grad_hidden_one * normed_one, axis=(0, 1, 2))
    grad_bias_one = jnp.sum(grad_hidden_one, axis=(0, 1, 2))
    grad_inputs = grad_middle.reshape(tokens.shape) + norm_back(
        grad_hidden_one * gain_one, normed_one, inverse_one
    )
    grad_tokens = grad_inputs.astype(jnp.bfloat16)
    summed = (
        lax.psum_scatter(grad_gain_one, ("dp", "rows"), scatter_dimension=0, tiled=True),
        lax.psum_scatter(grad_bias_one, ("dp", "rows"), scatter_dimension=0, tiled=True),
        lax.psum_scatter(grad_weight_qkv, ("dp", "rows"), scatter_dimension=0, tiled=True),
        lax.psum_scatter(grad_bias_qv, ("dp", "rows"), scatter_dimension=0, tiled=True),
        lax.psum_scatter(grad_weight_proj, ("dp", "rows"), scatter_dimension=0, tiled=True),
        lax.psum_scatter(grad_bias_proj, ("dp", "rows"), scatter_dimension=0, tiled=True),
        lax.psum_scatter(grad_gain_two, ("dp", "rows"), scatter_dimension=0, tiled=True),
        lax.psum_scatter(grad_bias_two, ("dp", "rows"), scatter_dimension=0, tiled=True),
        lax.psum_scatter(grad_weight_up, ("dp", "rows"), scatter_dimension=0, tiled=True),
        lax.psum_scatter(grad_bias_up, ("dp", "rows"), scatter_dimension=0, tiled=True),
        lax.psum_scatter(grad_weight_down, ("dp", "rows"), scatter_dimension=0, tiled=True),
        lax.psum_scatter(grad_bias_down, ("dp", "rows"), scatter_dimension=0, tiled=True),
    )
    return (
        mixed,
        grad_tokens,
        summed[0],
        summed[1],
        summed[2],
        summed[3],
        summed[4],
        summed[5],
        summed[6],
        summed[7],
        summed[8],
        summed[9],
        summed[10],
        summed[11],
    )


def solution(mesh):
    placed = (
        P("dp", "rows", None, None),
        P("dp"),
        P(("dp", "rows")),
        P(("dp", "rows")),
        P(("dp", "rows"), None),
        P(("dp", "rows")),
        P(("dp", "rows"), None),
        P(("dp", "rows")),
        P(("dp", "rows")),
        P(("dp", "rows")),
        P(("dp", "rows"), None),
        P(("dp", "rows")),
        P(("dp", "rows"), None),
        P(("dp", "rows")),
        P("dp", "rows", None, None),
    )
    return jax.shard_map(
        per_device,
        mesh=mesh,
        in_specs=placed,
        out_specs=(
            P("dp", "rows", None, None),
            P("dp", "rows", None, None),
            P(("dp", "rows")),
            P(("dp", "rows")),
            P(("dp", "rows"), None),
            P(("dp", "rows")),
            P(("dp", "rows"), None),
            P(("dp", "rows")),
            P(("dp", "rows")),
            P(("dp", "rows")),
            P(("dp", "rows"), None),
            P(("dp", "rows")),
            P(("dp", "rows"), None),
            P(("dp", "rows")),
        ),
        check_vma=False,
    )
```

profile of v0, /device:TPU:0, one launch (start us, length us, event | category | flops | bytes accessed | tf_op | source)
XLA Modules:
  0.0 1059.8 jit_solution(10885839428394119786)
XLA Ops:
  14.8 42.2 %all-reduce.17 = (bf16[512]{0:T(512)(128)(2,1)S(1)}, bf16[512]{0:T(512)(128)(2,1)S(1)}, bf16[1024]{0:T(1024)(128)(2,1)S(1)}, bf16[512]{0:T(512)(128)(2,1)S(1)}, ...) all-reduce(bf16[512]{0:T(512)(128)(2,1)S(1)} %dynamic-update-slice., ...), channel_id=1, replica_groups=mesh['dp'=8,'rows'=4] {'dp','rows'}, use_global_device_ids=true, to_apply=%add.1 | all-reduce | flops 6144 | bytes 24576
  73.6 8.1 collective-permute-done
  83.9 3.4 fusion.38
  87.3 13.7 %fusion.61 = f32[4096,1536]{1,0:T(8,128)} fusion(bf16[4096,512]{1,0:T(8,128)(2,1)} %bitcast.125, bf16[512,1536]{1,0:T(8,128)(2,1)} %all-gather.4.cloned.1.call-done), kind=kOutput, calls=%fused_computation.152 | convolution fusion | flops 6442450944 | bytes 30932992 | tf_op jit(solution)/shard_map/dot_general | solution.py:137
  101.0 3.9 slice.130
  104.9 6.6 fusion.21
  119.1 11.2 %reshape_reshape.43 = bf16[4,16,64,8,64]{4,3,2,1,0:T(8,128)(2,1)} reshape(bf16[4,2,8,8,8,512]{5,4,3,2,1,0:T(8,128)(2,1)} %bitcast.115) | data formatting | bytes 8388608 | tf_op jit(solution)/shard_map/reshape;reshape | solution.py:144
  130.4 11.2 %reshape_reshape.47 = bf16[4,16,64,8,64]{4,3,2,1,0:T(8,128)(2,1)} reshape(bf16[4,2,8,8,8,512]{5,4,3,2,1,0:T(8,128)(2,1)} %bitcast.116) | data formatting | bytes 8388608 | tf_op jit(solution)/shard_map/reshape;reshape | solution.py:144
  141.5 12.0 %copy.103 = bf16[4,16,64,8,64]{2,4,3,1,0:T(8,128)(2,1)} copy(bf16[4,16,64,8,64]{4,3,2,1,0:T(8,128)(2,1)} %reshape_reshape.47) | data formatting | bytes 8388608 | tf_op jit(solution)/shard_map/reshape;reshape | solution.py:144
  153.6 11.2 %reshape_reshape.45 = bf16[4,16,64,8,64]{4,3,2,1,0:T(8,128)(2,1)} reshape(bf16[4,2,8,8,8,512]{5,4,3,2,1,0:T(8,128)(2,1)} %bitcast.114) | data formatting | bytes 8388608 | tf_op jit(solution)/shard_map/reshape;reshape | solution.py:144
  164.7 12.1 %copy.108 = bf16[4,16,64,8,64]{2,4,3,1,0:T(8,128)(2,1)} copy(bf16[4,16,64,8,64]{4,3,2,1,0:T(8,128)(2,1)} %reshape_reshape.45) | data formatting | bytes 8388608 | tf_op jit(solution)/shard_map/reshape;reshape | solution.py:144
  176.9 11.8 %fusion.59 = (f32[4,16,8,64]{3,2,1,0:T(8,128)S(1)}, f32[4,16,8,64,64]{3,4,2,1,0:T(8,128)}) fusion(f32[4,16,64,64]{2,3,1,0:T(8,128)S(1)} %copy-done.15, bf16[4,16,64,8,64]{2,4,3,1,0:T(8,128)(2,1)} %copy.108, bf16[4,16,64,8,64]{2,4,3,1,0:T(8,128)(2,1)} %copy.103), kind=kOutput, calls=%fused_computation.150 | convolution fusion | flops 274694144 | bytes 17956864 | tf_op jit(solution)/shard_map/fbqhd,fbkhd->fbhqk/dot_general | solution.py:162
  188.7 10.9 %fusion.16 = f32[4,16,8,64]{3,2,1,0:T(8,128)S(1)} fusion(f32[4,16,8,64,64]{3,4,2,1,0:T(8,128)} %get-tuple-element.46, f32[4,16,8,64]{3,2,1,0:T(8,128)S(1)} %get-tuple-element.45), kind=kLoop, calls=%fused_computation.35 | loop fusion | flops 4161536 | bytes 8650752 | tf_op jit(solution)/shard_map/reduce_sum | solution.py:170
  199.6 13.2 %convert_bitcast_fusion.1 = bf16[4,16,64,8,64]{2,4,3,1,0:T(8,128)(2,1)} fusion(f32[4,16,8,64,64]{3,4,2,1,0:T(8,128)} %get-tuple-element.46, f32[4,16,8,64]{3,2,1,0:T(8,128)S(1)} %fusion.16, f32[4,16,8,64]{3,2,1,0:T(8,128)S(1)} %get-tuple-element.45, bf16[4,16,64,8,64]{4,3,2,1,0:T(8,128)(2,1)} %reshape_reshape.43), kind=kOutput, calls=%fused_computation.64 | convolution fusion | flops 276824064 | bytes 17039360 | tf_op jit(solution)/shard_map/fbhqk,fbkhd->fbqhd/dot_general | solution.py:173
  212.9 12.0 %copy.98 = bf16[4,16,64,8,64]{4,3,2,1,0:T(8,128)(2,1)} copy(bf16[4,16,64,8,64]{2,4,3,1,0:T(8,128)(2,1)} %convert_bitcast_fusion.1) | data formatting | bytes 8388608 | tf_op jit(solution)/shard_map/convert_element_type | solution.py:175
  224.8 11.8 %reshape_reshape.48 = bf16[4,2,8,8,8,512]{5,4,3,2,1,0:T(8,128)(2,1)} reshape(bf16[4,16,64,8,64]{4,3,2,1,0:T(8,128)(2,1)} %copy.98) | data formatting | bytes 8388608 | tf_op jit(solution)/shard_map/reshape;reshape | solution.py:46
  244.7 42.2 %all_gather.46 = bf16[512,512]{1,0:T(8,128)(2,1)S(1)} all-gather(bf16[16,512]{1,0:T(8,128)(2,1)S(1)} %copy-done.32), channel_id=1, replica_groups=mesh['dp'=8,'rows'=4] {'dp','rows'}, dimensions={0}, use_global_device_ids=true | all-gather | bytes 540672 | tf_op jit(solution)/shard_map/all_gather | solution.py:120
  286.9 3.5 fusion.37
  298.3 85.4 %fusion.2 = (bf16[4096,2048]{1,0:T(8,128)(2,1)}, f32[4096,2048]{1,0:T(8,128)}) fusion(f32[2048]{0:T(1024)S(1)} %convert_element_type.183, bf16[512,2048]{1,0:T(8,128)(2,1)} %all-gather.6.cloned.1.call-done, f32[4096,512]{1,0:T(8,128)} %copy-done.12, f32[512]{0:T(512)S(1)} %convert_element_type.181, f32[512]{0:T(512)S(1)} %convert_element_type.180, ...), kind=kOutput, calls=%fused_computation.4 | convolution fusion | flops 9154068480 | bytes 60862464 | tf_op jit(solution)/shard_map/dot_general | solution.py:188
  383.7 27.1 %convert_reduce_fusion = (f32[2048]{0:T(1024)}, bf16[4096,2048]{1,0:T(8,128)(2,1)}) fusion(f32[4096,2048]{1,0:T(8,128)} %get-tuple-element.50, f32[2048]{0:T(1024)S(1)} %convert_element_type.183, bf16[4096,512]{1,0:T(8,128)(2,1)} %bitcast.121, bf16[2048,512]{1,0:T(8,128)(2,1)} %all-gather.8.cloned.1.call-done), kind=kOutput, calls=%fused_computation.11 | convolution fusion | flops 8698984448 | bytes 56639488 | tf_op jit(solution)/shard_map/tc,fc->tf/dot_general | solution.py:206
  410.7 18.3 %multiply_reduce_fusion.1 = (f32[512]{0:T(512)}, f32[4096]{0:T(1024)S(1)}, f32[4096]{0:T(1024)S(1)}, f32[512]{0:T(512)}, f32[4096,512]{1,0:T(8,128)}) fusion(f32[4096,512]{1,0:T(8,128)S(1)} %copy-done.13, f32[4096]{0:T(1024)S(1)} %add_rsqrt_fusion.1, f32[4096]{0:T(1024)S(1)} %broadcast_multiply_fusion.5, f32[512]{0:T(512)S(1)} %convert_element_type.180, ...), kind=kOutput, calls=%fused_computation.50 | convolution fusion | flops 8608800768 | bytes 35723264 | tf_op jit(solution)/shard_map/tf,cf->tc/dot_general | solution.py:216
  429.1 8.6 convert_reduce_fusion.2
  443.2 3.4 fusion.53
  446.7 8.3 collective-permute-done.2
  461.8 11.2 %reshape_reshape.49 = bf16[4,16,64,8,64]{4,3,2,1,0:T(8,128)(2,1)} reshape(bf16[4,2,8,8,8,512]{5,4,3,2,1,0:T(8,128)(2,1)} %copy.100) | data formatting | bytes 8388608 | tf_op jit(solution)/shard_map/reshape;reshape | solution.py:233
  473.0 12.0 %copy.113 = bf16[4,16,64,8,64]{2,4,3,1,0:T(8,128)(2,1)} copy(bf16[4,16,64,8,64]{4,3,2,1,0:T(8,128)(2,1)} %reshape_reshape.49) | data formatting | bytes 8388608 | tf_op jit(solution)/shard_map/reshape;reshape | solution.py:233
  485.0 13.3 %convert_bitcast_fusion = bf16[4,16,64,8,64]{2,4,3,1,0:T(8,128)(2,1)} fusion(bf16[4,16,64,8,64]{2,4,3,1,0:T(8,128)(2,1)} %copy.113, f32[4,16,8,64,64]{3,4,2,1,0:T(8,128)} %get-tuple-element.46, f32[4,16,8,64]{3,2,1,0:T(8,128)S(1)} %log_add_fusion), kind=kOutput, calls=%fused_computation.57 | convolution fusion | flops 274726912 | bytes 16908288 | tf_op jit(solution)/shard_map/fbhqk,fbqhd->fbkhd/dot_general | solution.py:238
  498.4 19.2 %multiply_reduce_fusion = (f32[4,16,8,64]{3,2,1,0:T(8,128)S(1)}, f32[4,16,8,64,64]{3,4,2,1,0:T(8,128)}) fusion(f32[4,16,8,64,64]{3,4,2,1,0:T(8,128)} %get-tuple-element.46, f32[4,16,8,64]{3,2,1,0:T(8,128)S(1)} %log_add_fusion, bf16[4,16,64,8,64]{2,4,3,1,0:T(8,128)(2,1)} %copy.113, bf16[4,16,64,8,64]{4,3,2,1,0:T(8,128)(2,1)} %reshape_reshape.43), kind=kOutput, calls=%fused_computation.30 | convolution fusion | flops 274694144 | bytes 25427968 | tf_op jit(solution)/shard_map/fbqhd,fbkhd->fbhqk/dot_general | solution.py:241
  517.6 12.2 %multiply_convert_fusion.2 = bf16[4,16,8,64,64]{3,4,2,1,0:T(8,128)(2,1)S(1)} fusion(f32[4,16,8,64,64]{3,4,2,1,0:T(8,128)} %get-tuple-element.53, f32[4,16,8,64,64]{3,4,2,1,0:T(8,128)} %get-tuple-element.46, f32[4,16,8,64]{3,2,1,0:T(8,128)S(1)} %get-tuple-element.52, f32[4,16,8,64]{3,2,1,0:T(8,128)S(1)} %log_add_fusion), kind=kLoop, calls=%fused_computation.29 | loop fusion | flops 8388608 | bytes 21233664 | tf_op jit(solution)/shard_map/convert_element_type | solution.py:247
  533.0 8.8 fusion.33
  541.8 10.6 %fusion.32 = bf16[4,16,64,8,64]{4,2,3,1,0:T(8,128)(2,1)} fusion(bf16[4,16,64,8,64]{2,4,3,1,0:T(8,128)(2,1)} %copy.103, bf16[4,16,8,64,64]{3,4,2,1,0:T(8,128)(2,1)} %copy-done.4), kind=kOutput, calls=%fused_computation.78 | convolution fusion | flops 272629760 | bytes 12582912 | tf_op jit(solution)/shard_map/fbhqk,fbkhd->fbqhd/dot_general | solution.py:248
  552.4 12.0 %copy.115 = bf16[4,16,64,8,64]{4,3,2,1,0:T(8,128)(2,1)} copy(bf16[4,16,64,8,64]{2,4,3,1,0:T(8,128)(2,1)} %convert_bitcast_fusion) | data formatting | bytes 8388608 | tf_op jit(solution)/shard_map/convert_element_type | solution.py:256
  564.4 11.8 %reshape_reshape.54 = bf16[4,2,8,8,8,512]{5,4,3,2,1,0:T(8,128)(2,1)} reshape(bf16[4,16,64,8,64]{4,3,2,1,0:T(8,128)(2,1)} %copy.115) | data formatting | bytes 8388608 | tf_op jit(solution)/shard_map/reshape;reshape | solution.py:46
  576.2 23.6 %copy.106 = bf16[4,16,64,8,64]{4,3,2,1,0:T(8,128)(2,1)} copy(bf16[4,16,64,8,64]{4,2,3,1,0:T(8,128)(2,1)} %fusion.32) | data formatting | bytes 8388608 | tf_op jit(solution)/shard_map/convert_element_type | solution.py:254
  599.8 11.8 %reshape_reshape.50 = bf16[4,2,8,8,8,512]{5,4,3,2,1,0:T(8,128)(2,1)} reshape(bf16[4,16,64,8,64]{4,3,2,1,0:T(8,128)(2,1)} %copy.106) | data formatting | bytes 8388608 | tf_op jit(solution)/shard_map/reshape;reshape | solution.py:46
  611.6 23.8 %copy.111 = bf16[4,16,64,8,64]{4,3,2,1,0:T(8,128)(2,1)} copy(bf16[4,16,64,8,64]{4,2,3,1,0:T(8,128)(2,1)} %fusion.33) | data formatting | bytes 8388608 | tf_op jit(solution)/shard_map/convert_element_type | solution.py:255
  635.4 11.8 %reshape_reshape.52 = bf16[4,2,8,8,8,512]{5,4,3,2,1,0:T(8,128)(2,1)} reshape(bf16[4,16,64,8,64]{4,3,2,1,0:T(8,128)(2,1)} %copy.111) | data formatting | bytes 8388608 | tf_op jit(solution)/shard_map/reshape;reshape | solution.py:46
  657.0 11.0 %fusion.34 = f32[512,1536]{1,0:T(8,128)} fusion(bf16[4096,512]{1,0:T(8,128)(2,1)S(1)} %bitcast.126, bf16[4096,512]{1,0:T(8,128)(2,1)} %bitcast.133, bf16[4096,512]{1,0:T(8,128)(2,1)S(1)} %bitcast.129, bf16[4096,512]{1,0:T(8,128)(2,1)} %bitcast.131), kind=kOutput, calls=%fused_computation.80 | convolution fusion | flops 6480199680 | bytes 19922944 | tf_op jit(solution)/shard_map/tc,te->ce/dot_general | solution.py:264
  668.1 15.1 %fusion.62 = f32[2048,512]{1,0:T(8,128)} fusion(bf16[4096,2048]{1,0:T(8,128)(2,1)} %get-tuple-element.49, bf16[4096,512]{1,0:T(8,128)(2,1)} %bitcast.122), kind=kOutput, calls=%fused_computation.153 | convolution fusion | flops 8589934592 | bytes 25165824 | tf_op jit(solution)/shard_map/tf,tc->fc/dot_general | solution.py:203
  683.4 19.8 %fusion.56 = f32[512,2048]{1,0:T(8,128)} fusion(bf16[4096,2048]{1,0:T(8,128)(2,1)} %get-tuple-element.55, f32[4096,512]{1,0:T(8,128)} %copy-done.12, f32[512]{0:T(512)S(1)} %copy-done.38, f32[512]{0:T(512)S(1)} %convert_element_type.180, f32[4096]{0:T(1024)S(1)} %add_rsqrt_fusion.1, f32[4096]{0:T(1024)S(1)} %broadcast_multiply_fusion.5), kind=kOutput, calls=%fused_computation.147 | convolution fusion | flops 8600420352 | bytes 29396992 | tf_op jit(solution)/shard_map/tc,tf->cf/dot_general | solution.py:213
  706.3 9.6 fusion.35
  722.1 18.3 %add_convert_fusion.1 = bf16[4096,512]{1,0:T(8,128)(2,1)} fusion(f32[4096,512]{1,0:T(8,128)} %copy-done.12, bf16[4096,2048]{1,0:T(8,128)(2,1)} %get-tuple-element.49, bf16[2048,512]{1,0:T(8,128)(2,1)} %all-gather.8.cloned.1.call-done, f32[512]{0:T(512)S(1)} %convert_element_type.185), kind=kOutput, calls=%fused_computation.61 | convolution fusion | flops 8596226048 | bytes 31459328 | tf_op jit(solution)/shard_map/dot_general | solution.py:190
  741.8 4.4 fusion.58
  746.7 4.6 multiply_reduce_fusion.2
  751.4 37.2 %all-reduce.16 = (f32[512]{0:T(512)S(1)}, f32[512]{0:T(512)S(1)}, f32[1024]{0:T(1024)S(1)}, f32[512]{0:T(512)S(1)}, f32[512]{0:T(512)S(1)}, /*index=5*/f32[512]{0:T(512)S(1)}, f32[2048]{0:T(1024)S(1)}, f32[512]{0:T(512)S(1)}) all-reduce(f32[512]{0:T(512)S(1)} %get-tuple-element.16, ...), channel_id=2, replica_groups=mesh['dp'=8,'rows'=4] {'dp','rows'}, use_global_device_ids=true, to_apply=%region_12.13.clone | all-reduce | flops 6144 | bytes 49152
  793.3 9.6 add_convert_fusion
  802.9 110.0 %reduce-scatter.11.cloned.1.call-done = f32[64,512]{1,0:T(8,128)} async-done(((f32[2048,512]{1,0:T(8,128)}), f32[64,512]{1,0:T(8,128)}) %reduce-scatter.11.cloned.1.call-update) | async-done | bytes 131088 | tf_op jit(solution)/shard_map/reduce_scatter | solution.py:294
  912.8 139.9 %reduce-scatter.9.cloned.1.call-done = f32[16,2048]{1,0:T(8,128)} async-done(((f32[512,2048]{1,0:T(8,128)}), f32[16,2048]{1,0:T(8,128)}) %reduce-scatter.9.cloned.1.call-update) | async-done | bytes 131088 | tf_op jit(solution)/shard_map/reduce_scatter | solution.py:292
  (194 shorter events, 90.8 us)
Async XLA Ops:
  7.2 80.1 %all-gather.4.cloned.1.call-start = ((), (), s32[]{:S(2)}) async-start(), calls=%async_computation.4 | async-start | bytes 1622016 | tf_op jit(solution)/shard_map/all_gather | solution.py:118
  7.9 290.4 %all-gather.6.cloned.1.call-start = ((), (), s32[]{:S(2)}) async-start(), calls=%async_computation.5 | async-start | bytes 2162688 | tf_op jit(solution)/shard_map/all_gather | solution.py:124
  56.9 6.5 copy-start.1
  57.0 8.2 copy-start.30
  60.0 8.3 copy-start.26
  63.4 4.8 copy-start.28
  63.4 7.4 copy-start.41
  68.2 13.5 %collective-permute-start = (bf16[4,4,64,512]{3,2,1,0:T(8,128)(2,1)}, bf16[4,4,64,512]{3,2,1,0:T(8,128)(2,1)}, u32[]{:S(2)}, u32[]{:S(2)}) collective-permute-start(bf16[4,4,64,512]{3,2,1,0:T(8,128)(2,1)} %slice.93), channel_id=1, source_target_pairs={{0,3},{1,0},{2,1},{3,2},{4,7},{5,4},{6,5},{7,6},{8,11},{9,8},{10,9... | collective-permute-start | bytes 3145736 | tf_op jit(solution)/shard_map/ppermute | solution.py:17
  68.6 315.1 %all-gather.8.cloned.1.call-start = ((), (), s32[]{:S(2)}) async-start(), calls=%async_computation.6 | async-start | bytes 2162688 | tf_op jit(solution)/shard_map/all_gather | solution.py:126
  164.7 12.1 %copy-start.15 = (f32[4,16,64,64]{2,3,1,0:T(8,128)S(1)}, f32[4,16,64,64]{2,3,1,0:T(8,128)}, u32[]{:S(2)}) copy-start(f32[4,16,64,64]{2,3,1,0:T(8,128)} %and_select_fusion) | copy-start | bytes 3145732
  188.7 10.9 %copy-start.20 = (f32[4,16,8,64]{3,2,1,0:T(8,128)}, f32[4,16,8,64]{3,2,1,0:T(8,128)S(1)}, u32[]{:S(2)}) copy-start(f32[4,16,8,64]{3,2,1,0:T(8,128)S(1)} %get-tuple-element.45) | copy-start | bytes 393220
  199.6 13.2 %copy-start.24 = (f32[4,16,8,64]{3,2,1,0:T(8,128)}, f32[4,16,8,64]{3,2,1,0:T(8,128)S(1)}, u32[]{:S(2)}) copy-start(f32[4,16,8,64]{3,2,1,0:T(8,128)S(1)} %fusion.16) | copy-start | bytes 393220
  236.6 8.1 copy-start.32
  241.8 45.1 %collective-permute-start.1 = (bf16[4,4,64,512]{3,2,1,0:T(8,128)(2,1)S(1)}, bf16[4,4,64,512]{3,2,1,0:T(8,128)(2,1)S(1)}, u32[]{:S(2)}, u32[]{:S(2)}) collective-permute-start(bf16[4,4,64,512]{3,2,1,0:T(8,128)(2,1)S(1)} %pad_maximum_fusion.8), channel_id=1, source_target_pairs={{0,1},{1,2},{2,3},{3,0},{4,5},{5,6},{6,7},{7,4},{8,9},{9,10},{10,1... | collective-permute-start | bytes 3145736 | tf_op jit(solution)/shard_map/ppermute | solution.py:17
  244.5 558.3 %reduce-scatter.7.cloned.1.call-start = ((), (), s32[]{:S(2)}) async-start(), calls=%async_computation.8 | async-start | bytes 1081344 | tf_op jit(solution)/shard_map/reduce_scatter | solution.py:288
  244.6 45.9 %copy-start.2 = (bf16[4,16,64,512]{3,2,1,0:T(8,128)(2,1)S(1)}, bf16[4,16,64,512]{3,2,1,0:T(8,128)(2,1)}, u32[]{:S(2)}) copy-start(bf16[4,16,64,512]{3,2,1,0:T(8,128)(2,1)} %param.15) | copy-start | bytes 12582916
  244.6 53.7 %copy-start.37 = (f32[512]{0:T(512)}, f32[512]{0:T(512)S(1)}, u32[]{:S(2)}) copy-start(f32[512]{0:T(512)S(1)} %convert_element_type.181) | copy-start | bytes 6148
  286.9 6.5 copy-start.22
  293.4 3.2 copy-start.12
  383.7 27.1 %copy-start.13 = (f32[4096,512]{1,0:T(8,128)S(1)}, f32[4096,512]{1,0:T(8,128)}, u32[]{:S(2)}) copy-start(f32[4096,512]{1,0:T(8,128)} %copy-done.12) | copy-start | bytes 25165828
  429.1 8.6 copy-start.23
  437.6 4.3 copy-start
  437.6 4.0 copy-start.21
  437.6 4.0 copy-start.25
  441.3 13.7 %collective-permute-start.2 = (bf16[4,4,64,512]{3,2,1,0:T(8,128)(2,1)}, bf16[4,4,64,512]{3,2,1,0:T(8,128)(2,1)}, u32[]{:S(2)}, u32[]{:S(2)}) collective-permute-start(bf16[4,4,64,512]{3,2,1,0:T(8,128)(2,1)} %slice.102), channel_id=1, source_target_pairs={{0,3},{1,0},{2,1},{3,2},{4,7},{5,4},{6,5},{7,6},{8,11},{9,8},{10,9... | collective-permute-start | bytes 3145736 | tf_op jit(solution)/shard_map/ppermute | solution.py:17
  446.6 356.2 %reduce-scatter.5.cloned.1.call-start = ((), (), s32[]{:S(2)}) async-start(), calls=%async_computation.7 | async-start | bytes 3244032 | tf_op jit(solution)/shard_map/reduce_scatter | solution.py:286
  529.8 3.2 copy-start.4
  647.2 3.4 copy-start.9
  647.2 6.8 copy-start.7
  650.0 6.6 copy-start.19
  650.6 6.4 copy-start.16
  668.0 244.8 %reduce-scatter.11.cloned.1.call-start = ((), (), s32[]{:S(2)}) async-start(), calls=%async_computation.10 | async-start | bytes 4325376 | tf_op jit(solution)/shard_map/reduce_scatter | solution.py:294
  668.1 15.3 %copy-start.38 = (f32[512]{0:T(512)S(1)}, f32[512]{0:T(512)}, u32[]{:S(2)}) copy-start(f32[512]{0:T(512)} %copy-done.37) | copy-start | bytes 6148
  683.2 20.1 %copy-start.39 = (bf16[512]{0:T(512)(128)(2,1)S(1)}, bf16[512]{0:T(512)(128)(2,1)}, u32[]{:S(2)}) copy-start(bf16[512]{0:T(512)(128)(2,1)} %get-tuple-element.36) | copy-start | bytes 3076
  683.2 369.5 %reduce-scatter.9.cloned.1.call-start = ((), (), s32[]{:S(2)}) async-start(), calls=%async_computation.9 | async-start | bytes 4325376 | tf_op jit(solution)/shard_map/reduce_scatter | solution.py:292
  715.9 3.2 copy-start.11
  719.5 21.0 %copy-start.8 = (bf16[4,2,8,8,8,512]{5,4,3,2,1,0:T(8,128)(2,1)S(1)}, bf16[4,2,8,8,8,512]{5,4,3,2,1,0:T(8,128)(2,1)}, u32[]{:S(2)}) copy-start(bf16[4,2,8,8,8,512]{5,4,3,2,1,0:T(8,128)(2,1)} %reshape_reshape.54) | copy-start | bytes 12582916
  719.5 21.6 %copy-start.10 = (bf16[4,2,8,8,8,512]{5,4,3,2,1,0:T(8,128)(2,1)S(1)}, bf16[4,2,8,8,8,512]{5,4,3,2,1,0:T(8,128)(2,1)}, u32[]{:S(2)}) copy-start(bf16[4,2,8,8,8,512]{5,4,3,2,1,0:T(8,128)(2,1)} %reshape_reshape.50) | copy-start | bytes 12582916
  719.5 26.7 %collective-permute-start.3 = (bf16[4,4,64,512]{3,2,1,0:T(8,128)(2,1)S(1)}, bf16[4,4,64,512]{3,2,1,0:T(8,128)(2,1)S(1)}, u32[]{:S(2)}, u32[]{:S(2)}) collective-permute-start(bf16[4,4,64,512]{3,2,1,0:T(8,128)(2,1)S(1)} %fusion.40), channel_id=1, source_target_pairs={{0,1},{1,2},{2,3},{3,0},{4,5},{5,6},{6,7},{7,4},{8,9},{9,10},{10,1... | collective-permute-start | bytes 3145736 | tf_op jit(solution)/shard_map/ppermute | solution.py:17
  741.7 5.0 copy-start.3
  741.7 5.0 copy-start.27
  741.7 5.0 copy-start.29
  741.7 5.0 copy-start.31
  746.1 5.2 copy-start.5
  746.1 5.2 copy-start.33
  746.1 5.2 copy-start.34
  746.2 5.2 copy-start.35
  746.2 5.2 copy-start.36
  (5 other events, 13.1 us)
Sparse Core Ops, SparseCore 0:
  10.9 57.7 all-gather.3
  71.5 55.2 all-gather.5
  244.7 56.4 all-gather.7
  446.7 130.9 reduce-scatter.6
  668.2 101.7 reduce-scatter.4
  772.8 139.9 reduce-scatter.10
  915.8 136.8 reduce-scatter.8
where the time goes:
time: 1070 us; the launch traced here: 1060 us
  matrix products  304 us (28%)
  waiting for transfers between devices  267 us (25%)
  local copies, waits for them, and re-layouts  257 us (24%)
  blocking collectives  122 us (11%)
  other arithmetic  87.9 us (8%)
  between operations  15.2 us (1%)
    reduce_scatter x1, waiting for transfers between devices, per_device(): lax.psum_scatter(grad_weight_up, ('dp', 'rows'), scatter_dimension=0, til...  140 us
    reduce_scatter x1, waiting for transfers between devices, per_device(): lax.psum_scatter(grad_weight_down, ('dp', 'rows'), scatter_dimension=0, t...  110 us
    dot_general x1, matrix products, per_device(): jnp.dot(hidden_two, weight_up, preferred_element_type=jnp.float32) + bias_up  85.4 us
    unnamed x2, blocking collectives  79.4 us
    another operation x5, local copies, waits for them, and re-layouts, split_heads(): to_windows(grid, window)  57.7 us
    another operation x4, local copies, waits for them, and re-layouts, from_windows(): blocks.reshape(leading, rows_here // window, columns // window, window, w...  47.1 us
    all_gather x1, blocking collectives, per_device(): lax.all_gather(proj_weight, ('dp', 'rows'), axis=0, tiled=True)  42.2 us
    unnamed x108, local copies, waits for them, and re-layouts  27.8 us
  transfers between devices with their start and end apart: 11, of which 4 were waited for; matrix products, arithmetic and copies ran while one was open for 54% of the time, Pallas kernels for 0%

commit v1 on v0

v1 whole, which is shorter than its diff:
```python
import functools

import jax
import jax.numpy as jnp
from jax import lax
from jax.experimental import pallas as pl
from jax.experimental.pallas import tpu as pltpu
from jax.sharding import PartitionSpec as P

HEAD_DIM = 64
WIN = 8
HALF = WIN // 2
CELLS = WIN * WIN
LANES = 4 * HEAD_DIM
EPSILON = 1e-05
INV_ROOT_TWO = 0.7071067811865476
INV_ROOT_TWO_PI = 0.3989422804014327
F32 = jnp.float32
BF16 = jnp.bfloat16
VMEM_LIMIT = 60 * 1024 * 1024


def from_behind(x, axis, by):
    devices = lax.axis_size(axis)
    return lax.ppermute(x, axis, [(i, (i + by) % devices) for i in range(devices)])


def dot(a, b):
    return jnp.dot(a, b, preferred_element_type=F32)


def dot_t(a, b):
    return lax.dot_general(a, b, (((1,), (1,)), ((), ())), preferred_element_type=F32)


def to_window_order(x, columns):
    depth = x.shape[-1]
    grid = pltpu.roll(x.reshape(WIN, columns, depth), columns - HALF, 1)
    grid = grid.reshape(WIN, columns // WIN, WIN, depth).swapaxes(0, 1)
    return grid.reshape(WIN * columns, depth)


def from_window_order(x, columns):
    depth = x.shape[-1]
    grid = x.reshape(columns // WIN, WIN, WIN, depth).swapaxes(0, 1)
    grid = pltpu.roll(grid.reshape(WIN, columns, depth), HALF, 1)
    return grid.reshape(WIN * columns, depth)


def normalize(values):
    center = values - jnp.mean(values, axis=-1, keepdims=True)
    inverse = lax.rsqrt(jnp.mean(center * center, axis=-1, keepdims=True) + EPSILON)
    return center * inverse, inverse


def norm_back(grad, normed, inverse):
    return inverse * (
        grad
        - jnp.mean(grad, axis=-1, keepdims=True)
        - normed * jnp.mean(grad * normed, axis=-1, keepdims=True)
    )


def block_diag(x):
    lane_head = lax.broadcasted_iota(jnp.int32, x.shape, 1) // HEAD_DIM
    zero = jnp.zeros_like(x)
    return jnp.concatenate(
        [jnp.where(lane_head == head, x, zero) for head in range(LANES // HEAD_DIM)], axis=0
    )


def stacked_identity():
    row = lax.broadcasted_iota(jnp.int32, (CELLS, LANES), 0)
    lane = lax.broadcasted_iota(jnp.int32, (CELLS, LANES), 1)
    return jnp.where(row == lane % CELLS, 1.0, 0.0).astype(BF16)


def flip(x):
    return dot_t(stacked_identity(), block_diag(x)).astype(BF16)


def window_bias(info, frames, step, win, columns, height, rows_here):
    frame = lax.rem(step, frames)
    level = info[frame]
    factor = jnp.where(level >= 2, 4, jnp.where(level >= 1, 2, 1))
    base = info[frames] * rows_here + (step // frames) * WIN
    row_limit, col_limit = height * factor // 4, columns * factor // 4
    last_row = (base + WIN >= height).astype(jnp.int32)
    last_col = jnp.int32(win == columns // WIN - 1)
    key = lax.broadcasted_iota(jnp.int32, (CELLS, LANES), 0)
    query = lax.broadcasted_iota(jnp.int32, (CELLS, LANES), 1) % CELLS
    row = base + key // WIN + HALF
    col = win * WIN + key % WIN + HALF
    row = jnp.where(row >= height, row - height, row)
    col = jnp.where(col >= columns, col - columns, col)
    differ = key ^ query
    bad = (differ // (HALF * WIN) % 2) * last_row + (differ // HALF % 2) * last_col
    bad = bad + (row >= row_limit).astype(jnp.int32) + (col >= col_limit).astype(jnp.int32)
    return jnp.where(bad > 0, -100.0, 0.0)


def attend_kernel(
    frames, columns, height, rows_here,
    info, top, own, halo, weight, gain, bias, bias_q, bias_v,
    q_out, k_out, v_out, p_out, o_out, q_s, k_s, v_s,
):
    step = pl.program_id(0)
    width = top.shape[-1]
    bottom = jnp.where(step < frames, own[...], halo[...])
    x = jnp.concatenate([top[...], bottom], axis=0).astype(F32)
    normed, _ = normalize(to_window_order(x, columns))
    hidden = (normed * gain[...] + bias[...]).astype(BF16)
    q = (dot(hidden, weight[:, :width]) + bias_q[...]).astype(BF16) * 0.125
    k = dot(hidden, weight[:, width : 2 * width]).astype(BF16)
    v = (dot(hidden, weight[:, 2 * width :]) + bias_v[...]).astype(BF16)
    q_s[...] = q
    k_s[...] = k
    v_s[...] = v
    q_out[...] = q
    k_out[...] = k
    v_out[...] = v

    def one_window(win, carry):
        rows = pl.ds(pl.multiple_of(win * CELLS, CELLS), CELLS)
        mask = window_bias(info, frames, step, win, columns, height, rows_here)
        for group in range(width // LANES):
            lanes = slice(group * LANES, (group + 1) * LANES)
            scores = dot_t(k_s[rows, lanes], block_diag(q_s[rows, lanes])) + mask
            exponent = jnp.exp(scores - jnp.max(scores, axis=0, keepdims=True))
            probs = exponent * (1.0 / jnp.sum(exponent, axis=0, keepdims=True))
            probs = probs.astype(BF16)
            p_out[rows, lanes] = probs
            out = dot(flip(probs), block_diag(v_s[rows, lanes]))
            o_out[rows, lanes] = out.astype(BF16)
        return carry

    lax.fori_loop(0, columns // WIN, one_window, 0, unroll=2)


def middle_kernel(
    frames, columns, chunk,
    top, own, halo, dtop, down, dhalo, o_in, w_proj, w_up, w_down,
    b_proj, g_two, b_two, b_up, b_down,
    m_top, m_own, m_halo, dx_out, do_out, dw_proj, dw_up, dw_down_t, small,
):
    step = pl.program_id(0)
    width = top.shape[-1]
    hidden_width = w_up.shape[-1]

    @pl.when(step == 0)
    def _():
        dw_proj[...] = jnp.zeros_like(dw_proj)
        dw_up[...] = jnp.zeros_like(dw_up)
        dw_down_t[...] = jnp.zeros_like(dw_down_t)
        small[...] = jnp.zeros_like(small)

    bottom = jnp.where(step < frames, own[...], halo[...])
    dbottom = jnp.where(step < frames, down[...], dhalo[...])
    x = to_window_order(jnp.concatenate([top[...], bottom], axis=0).astype(F32), columns)
    dy = to_window_order(jnp.concatenate([dtop[...], dbottom], axis=0).astype(F32), columns)
    dy_low = dy.astype(BF16)
    x2 = x + dot(o_in[...], w_proj[...]) + b_proj[...]
    normed, inverse = normalize(x2)
    h2 = (normed * g_two[...] + b_two[...]).astype(BF16)
    h2_t = h2.T
    dy_t = dy_low.T
    total = x2 + b_down[...]
    dh2 = jnp.zeros_like(x2)
    for start in range(0, hidden_width, chunk):
        part = slice(start, start + chunk)
        u = dot(h2, w_up[:, part]) + b_up[:, part]
        dg = dot_t(dy_low, w_down[part, :])
        phi = 0.5 * (1.0 + lax.erf(u * INV_ROOT_TWO))
        g = (u * phi).astype(BF16)
        slope = phi + u * jnp.exp(-0.5 * u * u) * INV_ROOT_TWO_PI
        du_full = dg * slope
        du = du_full.astype(BF16)
        total += dot(g, w_down[part, :])
        dh2 += dot_t(du, w_up[:, part])
        dw_up[:, part] += dot(h2_t, du)
        dw_down_t[:, part] += dot(dy_t, g)
        small[0:1, part] += jnp.sum(du_full, axis=0, keepdims=True)
    mixed = from_window_order(total, columns).astype(BF16)
    half = mixed.shape[0] // 2
    m_top[...] = mixed[:half]

    @pl.when(step < frames)
    def _():
        m_own[...] = mixed[half:]

    @pl.when(step >= frames)
    def _():
        m_halo[...] = mixed[half:]

    small[1:2, :width] += jnp.sum(dy, axis=0, keepdims=True)
    small[2:3, :width] += jnp.sum(dh2 * normed, axis=0, keepdims=True)
    small[3:4, :width] += jnp.sum(dh2, axis=0, keepdims=True)
    dx2 = dy + norm_back(dh2 * g_two[...], normed, inverse)
    da = dx2.astype(BF16)
    small[4:5, :width] += jnp.sum(dx2, axis=0, keepdims=True)
    dx_out[...] = dx2
    dw_proj[...] += dot(o_in[...].T, da)
    do_out[...] = dot_t(da, w_proj[...]).astype(BF16)


def back_kernel(
    frames, columns,
    top, own, halo, q_in, k_in, v_in, p_in, do_in, dx_in, weight, gain, bias,
    g_top, g_own, g_halo, dw, small, d_s,
):
    step = pl.program_id(0)
    width = top.shape[-1]

    @pl.when(step == 0)
    def _():
        dw[...] = jnp.zeros_like(dw)
        small[...] = jnp.zeros_like(small)

    def one_window(win, carry):
        rows = pl.ds(pl.multiple_of(win * CELLS, CELLS), CELLS)
        for group in range(width // LANES):
            at = group * LANES
            lanes = slice(at, at + LANES)
            probs = p_in[rows, lanes]
            full = probs.astype(F32)
            do_diag = block_diag(do_in[rows, lanes])
            dv = dot(probs, do_diag)
            dp = dot_t(v_in[rows, lanes], do_diag)
            ds = full * (dp - jnp.sum(dp * full, axis=0, keepdims=True))
            ds = ds.astype(BF16)
            dk = dot(ds, block_diag(q_in[rows, lanes]))
            dq = dot(flip(ds), block_diag(k_in[rows, lanes])) * 0.125
            d_s[rows, at : at + LANES] = dq.astype(BF16)
            d_s[rows, width + at : width + at + LANES] = dk.astype(BF16)
            d_s[rows, 2 * width + at : 2 * width + at + LANES] = dv.astype(BF16)
        return carry

    lax.fori_loop(0, columns // WIN, one_window, 0, unroll=2)
    bottom = jnp.where(step < frames, own[...], halo[...])
    x = jnp.concatenate([top[...], bottom], axis=0).astype(F32)
    normed, inverse = normalize(to_window_order(x, columns))
    hidden = (normed * gain[...] + bias[...]).astype(BF16)
    d = d_s[...]
    dw[...] += dot(hidden.T, d)
    small[0:1, :] += jnp.sum(d.astype(F32), axis=0, keepdims=True)
    dh = dot_t(d, weight[...])
    small[1:2, :width] += jnp.sum(dh * normed, axis=0, keepdims=True)
    small[2:3, :width] += jnp.sum(dh, axis=0, keepdims=True)
    grad = dx_in[...] + norm_back(dh * gain[...], normed, inverse)
    grad = from_window_order(grad, columns).astype(BF16)
    half = grad.shape[0] // 2
    g_top[...] = grad[:half]

    @pl.when(step < frames)
    def _():
        g_own[...] = grad[half:]

    @pl.when(step >= frames)
    def _():
        g_halo[...] = grad[half:]


def whole(array):
    zeros = (0,) * array.ndim
    return pl.BlockSpec(array.shape, lambda s, *_: zeros, pipeline_mode=pl.Buffered(1))


def whole_out(shape):
    zeros = (0,) * len(shape)
    return pl.BlockSpec(shape, lambda s, *_: zeros)


def grid_specs(frames, cells, width):
    top = pl.BlockSpec((None, None, cells, width), lambda s, *_: (s % frames, 1 + 2 * (s // frames), 0, 0))
    own = pl.BlockSpec(
        (None, None, cells, width), lambda s, *_: (jnp.minimum(s, frames - 1), 2, 0, 0)
    )
    halo = pl.BlockSpec((None, cells, width), lambda s, *_: (jnp.maximum(s - frames, 0), 0, 0))
    return [top, own, halo]


def out_specs_of(frames, cells, width):
    top = pl.BlockSpec((None, None, cells, width), lambda s, *_: (s // frames, s % frames, 0, 0))
    own = pl.BlockSpec((None, cells, width), lambda s, *_: (jnp.minimum(s, frames - 1), 0, 0))
    halo = pl.BlockSpec((None, cells, width), lambda s, *_: (jnp.maximum(s - frames, 0), 0, 0))
    return [top, own, halo]


def params(name_vmem=VMEM_LIMIT):
    return pltpu.CompilerParams(vmem_limit_bytes=name_vmem, dimension_semantics=("arbitrary",))


def attend(info, tokens4, halo, weight, gain, bias, bias_q, bias_v, height, columns):
    frames, groups, cells, width = tokens4.shape
    steps, block = 2 * frames, 2 * cells
    row = pl.BlockSpec((None, block, width), lambda s, *_: (s, 0, 0))
    shape = jax.ShapeDtypeStruct((steps, block, width), BF16)
    vectors = (gain, bias, bias_q, bias_v)
    return pl.pallas_call(
        functools.partial(attend_kernel, frames, columns, height, groups * HALF),
        out_shape=[shape] * 5,
        grid_spec=pltpu.PrefetchScalarGridSpec(
            num_scalar_prefetch=1,
            grid=(steps,),
            in_specs=grid_specs(frames, cells, width) + [whole(weight)] + [whole(v) for v in vectors],
            out_specs=[row] * 5,
            scratch_shapes=[pltpu.VMEM((block, width), BF16)] * 3,
        ),
        compiler_params=params(),
        name="attend",
    )(info, tokens4, tokens4, halo, weight, *vectors)


def middle(tokens4, halo, d4, dhalo, o, w_proj, w_up, w_down, vectors, columns, chunk=512):
    frames, groups, cells, width = tokens4.shape
    steps, block = 2 * frames, 2 * cells
    hidden_width = w_up.shape[-1]
    row = pl.BlockSpec((None, block, width), lambda s, *_: (s, 0, 0))
    ins = grid_specs(frames, cells, width)
    return pl.pallas_call(
        functools.partial(middle_kernel, frames, columns, chunk),
        out_shape=[
            jax.ShapeDtypeStruct((2, frames, cells, width), BF16),
            jax.ShapeDtypeStruct((frames, cells, width), BF16),
            jax.ShapeDtypeStruct((frames, cells, width), BF16),
            jax.ShapeDtypeStruct((steps, block, width), F32),
            jax.ShapeDtypeStruct((steps, block, width), BF16),
            jax.ShapeDtypeStruct((width, width), F32),
            jax.ShapeDtypeStruct((width, hidden_width), F32),
            jax.ShapeDtypeStruct((width, hidden_width), F32),
            jax.ShapeDtypeStruct((8, hidden_width), F32),
        ],
        grid=(steps,),
        in_specs=ins + ins + [row] + [whole(w) for w in (w_proj, w_up, w_down)] + [whole(v) for v in vectors],
        out_specs=out_specs_of(frames, cells, width)
        + [row, row]
        + [
            whole_out((width, width)),
            whole_out((width, hidden_width)),
            whole_out((width, hidden_width)),
            whole_out((8, hidden_width)),
        ],
        compiler_params=params(),
        name="middle",
    )(tokens4, tokens4, halo, d4, d4, dhalo, o, w_proj, w_up, w_down, *vectors)


def back(tokens4, halo, q, k, v, p, do, dx, weight, gain, bias, columns):
    frames, groups, cells, width = tokens4.shape
    steps, block = 2 * frames, 2 * cells
    row = pl.BlockSpec((None, block, width), lambda s, *_: (s, 0, 0))
    return pl.pallas_call(
        functools.partial(back_kernel, frames, columns),
        out_shape=[
            jax.ShapeDtypeStruct((2, frames, cells, width), BF16),
            jax.ShapeDtypeStruct((frames, cells, width), BF16),
            jax.ShapeDtypeStruct((frames, cells, width), BF16),
            jax.ShapeDtypeStruct((width, 3 * width), F32),
            jax.ShapeDtypeStruct((8, 3 * width), F32),
        ],
        grid=(steps,),
        in_specs=grid_specs(frames, cells, width) + [row] * 6 + [whole(weight), whole(gain), whole(bias)],
        out_specs=out_specs_of(frames, cells, width)
        + [whole_out((width, 3 * width)), whole_out((8, 3 * width))],
        scratch_shapes=[pltpu.VMEM((block, 3 * width), BF16)],
        compiler_params=params(),
        name="back",
    )(tokens4, tokens4, halo, q, k, v, p, do, dx, weight, gain, bias)


def per_device(
    tokens, frame_level, ln1_gain, ln1_bias, qkv_weight, qv_bias, proj_weight, proj_bias,
    ln2_gain, ln2_bias, fc1_weight, fc1_bias, fc2_weight, fc2_bias, d_out,
):
    frames, rows_here, columns, width = tokens.shape
    height = rows_here * lax.axis_size("rows")
    axes = ("dp", "rows")
    cells = HALF * columns
    grouped = (frames, rows_here // HALF, cells, width)
    tokens4, d4 = tokens.reshape(grouped), d_out.reshape(grouped)
    halo = from_behind(tokens4[:, 0], "rows", -1)
    dhalo = from_behind(d4[:, 0], "rows", -1)
    gather = lambda w: lax.all_gather(w, axes, axis=0, tiled=True)
    w_qkv, w_proj, w_up, w_down = (gather(w) for w in (qkv_weight, proj_weight, fc1_weight, fc2_weight))
    vec = lambda v: gather(v).astype(F32)[None, :]
    gain_one, bias_one, bias_qv = vec(ln1_gain), vec(ln1_bias), vec(qv_bias)
    info = jnp.concatenate([frame_level, lax.axis_index("rows").astype(jnp.int32)[None]])
    q, k, v, p, o = attend(
        info, tokens4, halo, w_qkv, gain_one, bias_one, bias_qv[:, :width], bias_qv[:, width:],
        height, columns,
    )
    vectors = tuple(vec(v) for v in (proj_bias, ln2_gain, ln2_bias, fc1_bias, fc2_bias))
    m_top, m_own, m_halo, dx, do, dw_proj, dw_up, dw_down_t, small = middle(
        tokens4, halo, d4, dhalo, o, w_proj, w_up, w_down, vectors, columns
    )
    g_top, g_own, g_halo, dw_qkv, small_back = back(
        tokens4, halo, q, k, v, p, do, dx, w_qkv, gain_one, bias_one, columns
    )

    def assemble(top, own, back_rows):
        returned = from_behind(back_rows, "rows", 1)
        return jnp.stack([returned, top[0], own, top[1]], axis=1).reshape(tokens.shape)

    scatter = lambda g: lax.psum_scatter(g, axes, scatter_dimension=0, tiled=True)
    return (
        assemble(m_top, m_own, m_halo),
        assemble(g_top, g_own, g_halo),
        scatter(small_back[1, :width]),
        scatter(small_back[2, :width]),
        scatter(dw_qkv),
        scatter(jnp.concatenate([small_back[0, :width], small_back[0, 2 * width :]])),
        scatter(dw_proj),
        scatter(small[4, :width]),
        scatter(small[2, :width]),
        scatter(small[3, :width]),
        scatter(dw_up),
        scatter(small[0]),
        scatter(dw_down_t.T),
        scatter(small[1, :width]),
    )


def solution(mesh):
    both = ("dp", "rows")
    frame, vector, matrix = P("dp", "rows", None, None), P(both), P(both, None)
    return jax.shard_map(
        per_device,
        mesh=mesh,
        in_specs=(
            frame, P("dp"), vector, vector, matrix, vector, matrix, vector,
            vector, vector, matrix, vector, matrix, vector, frame,
        ),
        out_specs=(
            frame, frame, vector, vector, matrix, vector, matrix, vector,
            vector, vector, matrix, vector, matrix, vector,
        ),
        check_vma=False,
    )
```

time: 1070 us -> 799 us (0.75)
  matrix products: 304 us -> 0 us
  local copies, waits for them, and re-layouts: 257 us -> 27.6 us
  Pallas kernels: 0 us -> 218 us
  waiting for transfers between devices: 267 us -> 372 us
  other arithmetic: 87.9 us -> 6.84 us
  blocking collectives: 122 us -> 156 us
    dot_general x18 -> x0, matrix products: 304 us -> none  [the longest x1 85.4 us: per_device(): jnp.dot(hidden_two, weight_up, preferred_element_type=jnp.float32) + bias_up]
    pallas_call x0 -> x3, Pallas kernels: none -> 218 us  [the longest x1 82.7 us: middle(): pl.pallas_call(functools.partial(middle_kernel, frames, columns, chunk),...]
    unnamed x7 -> x8, waiting for transfers between devices: 0.78 us -> 146 us
    another operation x14 -> x4, local copies, waits for them, and re-layouts: 136 us -> 7.01 us  [assemble(): jnp.stack([returned, top[0], own, top[1]], axis=1).reshape(tokens.shape)]
    convert_element_type x4 -> x0, local copies, waits for them, and re-layouts: 71.4 us -> none  [the longest x1 23.8 us: per_device(): (grad_keys * scale).astype(jnp.bfloat16)]
    reduce_sum x12 -> x0, other arithmetic: 40.8 us -> none  [the longest x1 10.9 us: per_device(): row_sum = jnp.sum(exponent, axis=-1, keepdims=True)]
    unnamed x2, blocking collectives: 79.4 us -> 112 us
    convert_element_type x13 -> x0, other arithmetic: 30.4 us -> none  [the longest x1 12.2 us: per_device(): grad_scores = grad_scores.astype(jnp.bfloat16)]
  transfers between devices with their start and end apart: 11 -> 11, of which waited for: 4 -> 3; matrix products, arithmetic and copies ran while one was open for 54% -> 4% of each run, Pallas kernels for 0% -> 17%
where the time goes in v1:
time: 799 us; the launch traced here: 798 us
  waiting for transfers between devices  372 us (47%)
  Pallas kernels  218 us (27%)
  blocking collectives  156 us (20%)
  local copies, waits for them, and re-layouts  27.6 us (3%)
  between operations  14.4 us (2%)
    reduce_scatter x3, waiting for transfers between devices, per_device(): lax.psum_scatter(g, axes, scatter_dimension=0, tiled=True)  226 us
    unnamed x8, waiting for transfers between devices  146 us
    unnamed x2, blocking collectives  112 us
    pallas_call x1, Pallas kernels, middle(): pl.pallas_call(functools.partial(middle_kernel, frames, columns, chunk),...  82.7 us
    pallas_call x1, Pallas kernels, back(): pl.pallas_call(functools.partial(back_kernel, frames, columns), out_shape...  72.4 us
    pallas_call x1, Pallas kernels, attend(): pl.pallas_call(functools.partial(attend_kernel, frames, columns, height,...  62.6 us
    all_gather x1, blocking collectives, per_device(): gather = lambda w: lax.all_gather(w, axes, axis=0, tiled=True)  44.2 us
  transfers between devices with their start and end apart: 11, of which 3 were waited for; matrix products, arithmetic and copies ran while one was open for 4% of the time, Pallas kernels for 17%

profile of v1, /device:TPU:0, one launch (start us, length us, event | category | flops | bytes accessed | tf_op | source)
XLA Modules:
  0.0 798.1 jit_solution(15336260772387228935)
XLA Ops:
  7.3 0.7 all-gather.4.cloned.1.call-update
  8.1 0.7 all-gather.6.cloned.1.call-update
  8.8 0.7 all-gather.8.cloned.1.call-update
  9.5 2.3 slice_bitcast_fusion.1
  11.8 2.4 collective-permute-start
  14.2 1.3 slice_bitcast_fusion
  15.5 0.7 collective-permute-start.1
  17.7 0.2 dynamic-update-slice.6
  18.2 56.1 %all-reduce.17 = (bf16[512]{0:T(512)(128)(2,1)S(1)}, bf16[512]{0:T(512)(128)(2,1)S(1)}, bf16[1024]{0:T(1024)(128)(2,1)S(1)}, bf16[512]{0:T(512)(128)(2,1)S(1)}, ...) all-reduce(bf16[512]{0:T(512)(128)(2,1)S(1)} %dynamic-update-slice,, ...), channel_id=1, replica_groups=mesh['dp'=8,'rows'=4] {'dp','rows'}, use_global_device_ids=true, to_apply=%add | all-reduce | flops 6144 | bytes 24576
  74.3 0.6 broadcast_in_dim.61
  74.8 0.6 broadcast_in_dim.62
  75.4 0.6 broadcast_in_dim.67
  76.0 0.6 broadcast_in_dim.65
  76.6 0.6 broadcast_in_dim.66
  77.2 0.6 broadcast_in_dim.68
  77.8 0.6 broadcast_in_dim.64
  78.3 0.6 pad_add_fusion.info
  78.9 0.6 fusion.2
  79.5 44.2 %all_gather.40.w_proj = bf16[512,512]{1,0:T(8,128)(2,1)} all-gather(bf16[16,512]{1,0:T(8,128)(2,1)S(1)} %copy-done.5), channel_id=1, replica_groups=mesh['dp'=8,'rows'=4] {'dp','rows'}, dimensions={0}, use_global_device_ids=true | all-gather | bytes 540672 | tf_op jit(solution)/shard_map/all_gather | solution.py:383
  123.8 1.0 copy-done
  124.7 62.6 %attend.1 = (bf16[8,512,512]{2,1,0:T(8,128)(2,1)}, bf16[8,512,512]{2,1,0:T(8,128)(2,1)}, bf16[8,512,512]{2,1,0:T(8,128)(2,1)}, bf16[8,512,512]{2,1,0:T(8,128)(2,1)}, bf16[8,512,512]{2,1,0:T(8,128)(2,1)}) custom-call(s32[5]{0:T(128)} %pad_add_fusion.info, bf16[4,4,256,512]{3,2,1,0:T(8,128)(2,1)} %bitcast.45, bf16[4,4,256,512]{3,2,1,0:T(8,128)(2,1)} %bitcast.46, ...), custom_call_target="tpu_custom_call" | custom-call | tf_op jit(solution)/shard_map/attend/pallas_call | solution.py:299
  187.4 0.9 copy-done.2
  188.3 82.7 %middle.1 = (bf16[2,4,256,512]{3,2,1,0:T(8,128)(2,1)}, bf16[4,256,512]{2,1,0:T(8,128)(2,1)}, bf16[4,256,512]{2,1,0:T(8,128)(2,1)}, f32[8,512,512]{2,1,0:T(8,128)...) custom-call(bf16[4,4,256,512]{3,2,1,0:T(8,128)(2,1)} %bitcast.47, ...), custom_call_target="tpu_custom_call" | custom-call | tf_op jit(solution)/shard_map/middle/pallas_call | solution.py:320
  271.1 0.3 reduce-scatter.7.cloned.1.call-start
  271.3 72.4 %back.1 = (bf16[2,4,256,512]{3,2,1,0:T(8,128)(2,1)}, bf16[4,256,512]{2,1,0:T(8,128)(2,1)}, bf16[4,256,512]{2,1,0:T(8,128)(2,1)}, f32[512,1536]{1,0:T(8,128)}, f32[8,1536]{1,0:T(8,128)}) custom-call(bf16[4,4,256,512]{3,2,1,0:T(8,128)(2,1)} %bitcast.49, bf16[4,4,256,512]{3,2,1,0:T(8,128)(2,1)} %bitcast.50, bf16[4,256,512]{2,1,0:T(8,128)(2,1)} %copy-done, ...), custom_call_target="tpu_custom_call" | custom-call | tf_op jit(solution)/shard_map/back/pallas_call | solution.py:352
  343.8 5.4 copy.48
  349.3 0.7 reduce-scatter.11.cloned.1.call-update
  350.0 0.4 collective-permute-start.3
  350.4 0.9 fusion
  351.2 0.8 slice.66
  352.1 0.8 fusion.1
  352.9 55.5 %all-reduce.16 = (f32[512]{0:T(512)S(1)}, f32[512]{0:T(512)S(1)}, f32[1024]{0:T(1024)S(1)}, f32[512]{0:T(512)S(1)}, f32[512]{0:T(512)S(1)}, /*index=5*/f32[512]{0:T(512)S(1)}, f32[2048]{0:T(1024)S(1)}, f32[512]{0:T(512)S(1)}) all-reduce(f32[512]{0:T(512)S(1)} %bitcast.76, ...), channel_id=2, replica_groups=mesh['dp'=8,'rows'=4] {'dp','rows'}, use_global_device_ids=true, to_apply=%region_0.0.clone | all-reduce | flops 6144 | bytes 49152
  408.4 0.6 dynamic-slice
  409.0 0.6 dynamic-slice.1
  409.6 0.6 dynamic-slice.3
  410.1 0.6 dynamic-slice.4
  410.7 0.6 dynamic-slice.5
  411.3 0.6 dynamic-slice.7
  411.9 0.6 dynamic-slice.2
  412.5 0.6 dynamic-slice.6
  413.1 1.9 slice_bitcast_fusion.3
  415.2 1.6 pad_maximum_fusion.1
  416.9 2.4 copy.46
  419.3 0.6 pad_maximum_fusion
  419.9 2.4 copy.45
  422.3 85.9 %reduce-scatter.7.cloned.1.call-done = f32[16,1536]{1,0:T(8,128)} async-done(((f32[512,1536]{1,0:T(8,128)}), f32[16,1536]{1,0:T(8,128)}) %reduce-scatter.7.cloned.1.call-update) | async-done | bytes 98320 | tf_op jit(solution)/shard_map/reduce_scatter | solution.py:404
  508.2 142.9 %reduce-scatter.13.cloned.1.call-done = f32[64,512]{1,0:T(8,128)} async-done(((f32[2048,512]{1,0:T(8,128)}), f32[64,512]{1,0:T(8,128)}) %reduce-scatter.13.cloned.1.call-update) | async-done | bytes 131088
  651.1 140.1 %reduce-scatter.11.cloned.1.call-done = f32[16,2048]{1,0:T(8,128)} async-done(((f32[512,2048]{1,0:T(8,128)}), f32[16,2048]{1,0:T(8,128)}) %reduce-scatter.11.cloned.1.call-update) | async-done | bytes 131088 | tf_op jit(solution)/shard_map/reduce_scatter | solution.py:404
  (64 shorter events, 2.3 us)
Async XLA Ops:
  7.2 9.0 %copy-start.6 = (bf16[16]{0:T(256)(128)(2,1)S(1)}, bf16[16]{0:T(256)(128)(2,1)}, u32[]{:S(2)}) copy-start(bf16[16]{0:T(256)(128)(2,1)} %param.17) | copy-start | bytes 100
  7.2 9.2 %copy-start.7 = (bf16[16]{0:T(256)(128)(2,1)S(1)}, bf16[16]{0:T(256)(128)(2,1)}, u32[]{:S(2)}) copy-start(bf16[16]{0:T(256)(128)(2,1)} %param.18) | copy-start | bytes 100
  7.2 9.5 %copy-start.8 = (bf16[16]{0:T(256)(128)(2,1)S(1)}, bf16[16]{0:T(256)(128)(2,1)}, u32[]{:S(2)}) copy-start(bf16[16]{0:T(256)(128)(2,1)} %param.22) | copy-start | bytes 100
  7.2 9.7 %copy-start.9 = (bf16[16]{0:T(256)(128)(2,1)S(1)}, bf16[16]{0:T(256)(128)(2,1)}, u32[]{:S(2)}) copy-start(bf16[16]{0:T(256)(128)(2,1)} %param.23) | copy-start | bytes 100
  7.2 10.0 %copy-start.10 = (bf16[16]{0:T(256)(128)(2,1)S(1)}, bf16[16]{0:T(256)(128)(2,1)}, u32[]{:S(2)}) copy-start(bf16[16]{0:T(256)(128)(2,1)} %param.24) | copy-start | bytes 100
  7.2 10.2 %copy-start.11 = (bf16[16]{0:T(256)(128)(2,1)S(1)}, bf16[16]{0:T(256)(128)(2,1)}, u32[]{:S(2)}) copy-start(bf16[16]{0:T(256)(128)(2,1)} %param.28) | copy-start | bytes 100
  7.2 10.4 %copy-start.12 = (bf16[64]{0:T(256)(128)(2,1)S(1)}, bf16[64]{0:T(256)(128)(2,1)}, u32[]{:S(2)}) copy-start(bf16[64]{0:T(256)(128)(2,1)} %param.26) | copy-start | bytes 388
  7.3 10.7 %copy-start.13 = (bf16[32]{0:T(256)(128)(2,1)S(1)}, bf16[32]{0:T(256)(128)(2,1)}, u32[]{:S(2)}) copy-start(bf16[32]{0:T(256)(128)(2,1)} %param.20) | copy-start | bytes 196
  7.3 71.1 %copy-start.14 = (s32[4]{0:T(128)S(1)}, s32[4]{0:T(128)}, u32[]{:S(2)}) copy-start(s32[4]{0:T(128)} %param.16) | copy-start | bytes 52
  7.3 72.3 %copy-start.5 = (bf16[16,512]{1,0:T(8,128)(2,1)S(1)}, bf16[16,512]{1,0:T(8,128)(2,1)}, u32[]{:S(2)}) copy-start(bf16[16,512]{1,0:T(8,128)(2,1)} %param.21) | copy-start | bytes 49156
  7.3 116.5 %all-gather.4.cloned.1.call-start = ((), (), s32[]{:S(2)}) async-start(), calls=%async_computation.4 | async-start | bytes 1622016 | tf_op jit(solution)/shard_map/all_gather | solution.py:383
  8.0 179.4 %all-gather.6.cloned.1.call-start = ((), (), s32[]{:S(2)}) async-start(), calls=%async_computation.5 | async-start | bytes 2162688 | tf_op jit(solution)/shard_map/all_gather | solution.py:383
  8.8 178.6 %all-gather.8.cloned.1.call-start = ((), (), s32[]{:S(2)}) async-start(), calls=%async_computation.6 | async-start | bytes 2162688 | tf_op jit(solution)/shard_map/all_gather | solution.py:383
  9.5 412.8 %reduce-scatter.9.cloned.1.call-start = ((), (), s32[]{:S(2)}) async-start(), calls=%async_computation.8 | async-start | bytes 1081344 | tf_op jit(solution)/shard_map/reduce_scatter | solution.py:404
  11.8 112.0 %collective-permute-start = (bf16[4,256,512]{2,1,0:T(8,128)(2,1)}, bf16[4,256,512]{2,1,0:T(8,128)(2,1)S(1)}, u32[]{:S(2)}, u32[]{:S(2)}) collective-permute-start(bf16[4,256,512]{2,1,0:T(8,128)(2,1)} %slice_bitcast_fusion.1), channel_id=1, source_target_pairs={{0,3},{1,0},{2,1},{3,2},{4,7},{5,4},{6,5},{7,6},{8,11},{9,8},{10,9... | collective-permute-start | bytes 3145736 | tf_op jit(solution)/shard_map/ppermute | solution.py:25
  15.5 171.8 %collective-permute-start.1 = (bf16[4,256,512]{2,1,0:T(8,128)(2,1)S(1)}, bf16[4,256,512]{2,1,0:T(8,128)(2,1)S(1)}, u32[]{:S(2)}, u32[]{:S(2)}) collective-permute-start(bf16[4,256,512]{2,1,0:T(8,128)(2,1)S(1)} %slice_bitcast_fusion), channel_id=1, source_target_pairs={{0,3},{1,0},{2,1},{3,2},{4,7},{5,4},{6,5},{7,6},{8,11},{9,8},{10,9... | collective-permute-start | bytes 3145736 | tf_op jit(solution)/shard_map/ppermute | solution.py:25
  123.8 1.0 copy-start
  187.3 1.0 copy-start.2
  271.1 237.2 %reduce-scatter.7.cloned.1.call-start = ((), (), s32[]{:S(2)}) async-start(), calls=%async_computation.7 | async-start | bytes 3244032 | tf_op jit(solution)/shard_map/reduce_scatter | solution.py:404
  343.8 307.4 %reduce-scatter.13.cloned.1.call-start = ((), (), s32[]{:S(2)}) async-start(), calls=%async_computation.10 | async-start | bytes 4325376
  349.2 442.0 %reduce-scatter.11.cloned.1.call-start = ((), (), s32[]{:S(2)}) async-start(), calls=%async_computation.9 | async-start | bytes 4325376 | tf_op jit(solution)/shard_map/reduce_scatter | solution.py:404
  349.3 65.7 %copy-start.1 = (bf16[2,4,256,512]{3,2,1,0:T(8,128)(2,1)S(1)}, bf16[2,4,256,512]{3,2,1,0:T(8,128)(2,1)}, u32[]{:S(2)}) copy-start(bf16[2,4,256,512]{3,2,1,0:T(8,128)(2,1)} %get-tuple-element.35) | copy-start | bytes 6291460
  350.0 65.2 %collective-permute-start.3 = (bf16[4,256,512]{2,1,0:T(8,128)(2,1)}, bf16[4,256,512]{2,1,0:T(8,128)(2,1)}, u32[]{:S(2)}, u32[]{:S(2)}) collective-permute-start(bf16[4,256,512]{2,1,0:T(8,128)(2,1)} %get-tuple-element.43), channel_id=1, source_target_pairs={{0,1},{1,2},{2,3},{3,0},{4,5},{5,6},{6,7},{7,4},{8,9},{9,10},{10,1... | collective-permute-start | bytes 3145736 | tf_op jit(solution)/shard_map/ppermute | solution.py:25
  352.1 67.2 %collective-permute-start.2 = (bf16[4,256,512]{2,1,0:T(8,128)(2,1)}, bf16[4,256,512]{2,1,0:T(8,128)(2,1)S(1)}, u32[]{:S(2)}, u32[]{:S(2)}) collective-permute-start(bf16[4,256,512]{2,1,0:T(8,128)(2,1)} %get-tuple-element.34), channel_id=1, source_target_pairs={{0,1},{1,2},{2,3},{3,0},{4,5},{5,6},{6,7},{7,4},{8,9},{9,10},{10,1... | collective-permute-start | bytes 3145736 | tf_op jit(solution)/shard_map/ppermute | solution.py:25
  413.1 2.2 copy-start.4
  416.8 2.5 copy-start.3
Sparse Core Ops, SparseCore 0:
  11.0 57.8 all-gather.3
  71.7 55.9 all-gather.5
  130.5 55.7 all-gather.7
  271.2 132.7 reduce-scatter.8
  410.7 97.4 reduce-scatter.6
  511.0 140.0 reduce-scatter.12
  654.1 137.1 reduce-scatter.10

commit v2 on v1

--- a/solution.py
+++ b/solution.py
@@ -12,6 +12,8 @@
 HALF = WIN // 2
 CELLS = WIN * WIN
 LANES = 4 * HEAD_DIM
+LANE = 128
+ROWS = 16
 EPSILON = 1e-05
 INV_ROOT_TWO = 0.7071067811865476
 INV_ROOT_TWO_PI = 0.3989422804014327
@@ -99,13 +101,79 @@
     return jnp.where(bad > 0, -100.0, 0.0)
 
 
+def place(info, at, mine, theirs, targets, vec, sem, vec_sem):
+    copies = []
+    for core, source in enumerate((mine, theirs)):
+        for j in range(source.shape[0]):
+            block = info[at] ^ (bits_of(j) | core)
+            for lane, lanes, rows, target in targets:
+                for sub in range(rows // ROWS):
+                    row = pl.multiple_of(block * rows + sub * ROWS, ROWS)
+                    copies.append(
+                        pltpu.make_async_copy(
+                            source.at[j, :, pl.ds(lane + sub * lanes, lanes)],
+                            target.at[pl.ds(row, ROWS), :],
+                            sem,
+                        )
+                    )
+        lanes = vec.shape[-1]
+        blocks = source.shape[0]
+        copies.append(
+            pltpu.make_async_copy(
+                source.at[:, :, pl.ds(source.shape[-1] - lanes, lanes)],
+                vec.at[pl.ds(core * blocks, blocks)],
+                vec_sem,
+            )
+        )
+    for copy in copies:
+        copy.start()
+
+
+def wait_bytes(targets, sem):
+    for target in targets:
+        pltpu.make_async_copy(target, target, sem).wait()
+
+
+def bits_of(j):
+    return (j % 4) * 8 + (j // 8) * 4 + (j // 4 % 2) * 2
+
+
+def natural_rows(vec):
+    total = jnp.sum(vec[...].astype(F32), axis=0)
+    return [total[r : r + 1, :] for r in range(total.shape[0])]
+
+
+def hand_over(info, at, sources, tail, keep, send):
+    for core, out in enumerate((keep, send)):
+        for j in range(out.shape[0]):
+            block = info[at] ^ (bits_of(j) | core)
+            for lane, lanes, rows, source in sources:
+                for sub in range(rows // ROWS):
+                    row = pl.multiple_of(block * rows + sub * ROWS, ROWS)
+                    start = lane + sub * lanes
+                    out[j, :, start : start + lanes] = source[pl.ds(row, ROWS), :].astype(out.dtype)
+            out[j, :, out.shape[-1] - tail.shape[-1] :] = tail.astype(out.dtype)
+
+
 def attend_kernel(
-    frames, columns, height, rows_here,
-    info, top, own, halo, weight, gain, bias, bias_q, bias_v,
-    q_out, k_out, v_out, p_out, o_out, q_s, k_s, v_s,
+    frames, columns, height, rows_here, first,
+    info, top, own, halo, mine, theirs, *rest,
 ):
-    step = pl.program_id(0)
+    q_out, k_out, v_out, p_out, o_out, q_s, k_s, v_s, weight, vec, lines, sem = rest[-12:]
+    step = pl.program_id(0) + first
     width = top.shape[-1]
+
+    @pl.when(pl.program_id(0) == 0)
+    def _():
+        place(info, frames + 1, mine, theirs, [(0, 3 * width, ROWS, weight)], vec, sem.at[0], sem.at[1])
+        wait_bytes([weight], sem.at[0])
+        wait_bytes([vec], sem.at[1])
+        pieces = natural_rows(vec)
+        per = width // LANE
+        for line in range(lines.shape[0]):
+            lines[line : line + 1, :] = jnp.concatenate(pieces[line * per : (line + 1) * per], axis=1)
+
+    gain, bias, bias_q, bias_v = (lines.at[i : i + 1] for i in range(4))
     bottom = jnp.where(step < frames, own[...], halo[...])
     x = jnp.concatenate([top[...], bottom], axis=0).astype(F32)
     normed, _ = normalize(to_window_order(x, columns))
@@ -139,16 +207,30 @@
 
 def middle_kernel(
     frames, columns, chunk,
-    top, own, halo, dtop, down, dhalo, o_in, w_proj, w_up, w_down,
-    b_proj, g_two, b_two, b_up, b_down,
-    m_top, m_own, m_halo, dx_out, do_out, dw_proj, dw_up, dw_down_t, small,
+    info, top, own, halo, dtop, down, dhalo, o_in, mine, theirs,
+    m_top, m_own, m_halo, dx_out, do_out, keep, send,
+    w_proj, w_up, w_down, vec, lines, b_up, dw_proj, dw_up, dw_down_t, dw_down, small, sem,
 ):
     step = pl.program_id(0)
     width = top.shape[-1]
     hidden_width = w_up.shape[-1]
+    b_proj, g_two, b_two, b_down = (lines.at[i : i + 1] for i in range(4))
 
     @pl.when(step == 0)
     def _():
+        targets = [
+            (0, width, ROWS, w_proj),
+            (width, hidden_width, ROWS, w_up),
+            (width + hidden_width, width, w_down.shape[0] // 32, w_down),
+        ]
+        place(info, frames + 1, mine, theirs, targets, vec, sem.at[0], sem.at[1])
+        wait_bytes([w_proj, w_up, w_down], sem.at[0])
+        wait_bytes([vec], sem.at[1])
+        pieces = natural_rows(vec)
+        per = width // pieces[0].shape[-1]
+        for line in range(4):
+            lines[line : line + 1, :] = jnp.concatenate(pieces[line * per : (line + 1) * per], axis=1)
+        b_up[...] = jnp.concatenate(pieces[4 * per :], axis=1)
         dw_proj[...] = jnp.zeros_like(dw_proj)
         dw_up[...] = jnp.zeros_like(dw_up)
         dw_down_t[...] = jnp.zeros_like(dw_down_t)
@@ -202,17 +284,42 @@
     dw_proj[...] += dot(o_in[...].T, da)
     do_out[...] = dot_t(da, w_proj[...]).astype(BF16)
 
+    @pl.when(step == pl.num_programs(0) - 1)
+    def _():
+        for lane in range(0, hidden_width, LANE):
+            dw_down[lane : lane + LANE, :] = dw_down_t[:, lane : lane + LANE].T
+        order = (4, 2, 3, 1)
+        flat = jnp.concatenate([small[r : r + 1, :width] for r in order] + [small[0:1, :]], axis=1)
+        lines_of = keep.shape[-1] - width - 2 * hidden_width
+        tail = jnp.concatenate(
+            [flat[:, i * lines_of : (i + 1) * lines_of] for i in range(ROWS)], axis=0
+        )
+        sources = [
+            (0, width, ROWS, dw_proj),
+            (width, hidden_width, ROWS, dw_up),
+            (width + hidden_width, width, dw_down.shape[0] // 32, dw_down),
+        ]
+        hand_over(info, frames + 1, sources, tail, keep, send)
+
 
 def back_kernel(
     frames, columns,
-    top, own, halo, q_in, k_in, v_in, p_in, do_in, dx_in, weight, gain, bias,
-    g_top, g_own, g_halo, dw, small, d_s,
+    info, top, own, halo, q_in, k_in, v_in, p_in, do_in, dx_in, mine, theirs,
+    g_top, g_own, g_halo, keep, send, d_s, weight, vec, lines, dw, small, sem,
 ):
     step = pl.program_id(0)
     width = top.shape[-1]
+    gain, bias = (lines.at[i : i + 1] for i in range(2))
 
     @pl.when(step == 0)
     def _():
+        place(info, frames + 1, mine, theirs, [(0, 3 * width, ROWS, weight)], vec, sem.at[0], sem.at[1])
+        wait_bytes([weight], sem.at[0])
+        wait_bytes([vec], sem.at[1])
+        pieces = natural_rows(vec)
+        per = width // LANE
+        for line in range(lines.shape[0]):
+            lines[line : line + 1, :] = jnp.concatenate(pieces[line * per : (line + 1) * per], axis=1)
         dw[...] = jnp.zeros_like(dw)
         small[...] = jnp.zeros_like(small)
 
@@ -259,23 +366,25 @@
     def _():
         g_halo[...] = grad[half:]
 
-
-def whole(array):
-    zeros = (0,) * array.ndim
-    return pl.BlockSpec(array.shape, lambda s, *_: zeros, pipeline_mode=pl.Buffered(1))
-
-
-def whole_out(shape):
-    zeros = (0,) * len(shape)
-    return pl.BlockSpec(shape, lambda s, *_: zeros)
-
-
-def grid_specs(frames, cells, width):
-    top = pl.BlockSpec((None, None, cells, width), lambda s, *_: (s % frames, 1 + 2 * (s // frames), 0, 0))
+    @pl.when(step == pl.num_programs(0) - 1)
+    def _():
+        pieces = [small[1:2, :width], small[2:3, :width], small[0:1, :width], small[0:1, 2 * width :]]
+        flat = jnp.concatenate(pieces, axis=1)
+        tail = jnp.concatenate([flat[:, i * LANE : (i + 1) * LANE] for i in range(ROWS)], axis=0)
+        hand_over(info, frames + 1, [(0, 3 * width, ROWS, dw)], tail, keep, send)
+
+
+def grid_specs(frames, cells, width, first=0):
+    top = pl.BlockSpec(
+        (None, None, cells, width),
+        lambda s, *_: ((s + first) % frames, 1 + 2 * ((s + first) // frames), 0, 0),
+    )
     own = pl.BlockSpec(
-        (None, None, cells, width), lambda s, *_: (jnp.minimum(s, frames - 1), 2, 0, 0)
-    )
-    halo = pl.BlockSpec((None, cells, width), lambda s, *_: (jnp.maximum(s - frames, 0), 0, 0))
+        (None, None, cells, width), lambda s, *_: (jnp.minimum(s + first, frames - 1), 2, 0, 0)
+    )
+    halo = pl.BlockSpec(
+        (None, cells, width), lambda s, *_: (jnp.maximum(s + first - frames, 0), 0, 0)
+    )
     return [top, own, halo]
 
 
@@ -286,37 +395,53 @@
     return [top, own, halo]
 
 
-def params(name_vmem=VMEM_LIMIT):
-    return pltpu.CompilerParams(vmem_limit_bytes=name_vmem, dimension_semantics=("arbitrary",))
-
-
-def attend(info, tokens4, halo, weight, gain, bias, bias_q, bias_v, height, columns):
+def whole_out(shape):
+    zeros = (0,) * len(shape)
+    return pl.BlockSpec(shape, lambda s, *_: zeros, pipeline_mode=pl.Buffered(1))
+
+
+ANYWHERE = pl.BlockSpec(memory_space=pl.ANY)
+
+
+def params():
+    return pltpu.CompilerParams(vmem_limit_bytes=VMEM_LIMIT, dimension_semantics=("arbitrary",))
+
+
+def attend(info, tokens4, halo, blocks, previous, first, height, columns):
+    frames, groups, cells, width = tokens4.shape
+    steps, block = 2 * frames, 2 * cells
+    row = pl.BlockSpec((None, block, width), lambda s, *_: (s + first, 0, 0))
+    shape = jax.ShapeDtypeStruct((steps, block, width), BF16)
+    held = 6
+    return pl.pallas_call(
+        functools.partial(attend_kernel, frames, columns, height, groups * HALF, first),
+        out_shape=[shape] * 5,
+        grid_spec=pltpu.PrefetchScalarGridSpec(
+            num_scalar_prefetch=1,
+            grid=(frames,),
+            in_specs=grid_specs(frames, cells, width, first) + [ANYWHERE] * (2 + len(previous)),
+            out_specs=[row] * 5,
+            scratch_shapes=[pltpu.VMEM((block, width), BF16)] * 3
+            + [
+                pltpu.VMEM((width, 3 * width), BF16),
+                pltpu.VMEM((32, ROWS, LANE), BF16),
+                pltpu.VMEM((4, width), F32),
+                pltpu.SemaphoreType.DMA((2,)),
+            ],
+        ),
+        input_output_aliases={held + i: i for i in range(len(previous))},
+        compiler_params=params(),
+        cost_estimate=pl.CostEstimate(flops=3 * 10**10, bytes_accessed=2 * 10**7, transcendentals=10**6),
+        name="attend",
+    )(info, tokens4, tokens4, halo, *blocks, *previous)
+
+
+def middle(info, tokens4, halo, d4, dhalo, o, blocks, hidden_width, columns, chunk=512):
     frames, groups, cells, width = tokens4.shape
     steps, block = 2 * frames, 2 * cells
     row = pl.BlockSpec((None, block, width), lambda s, *_: (s, 0, 0))
-    shape = jax.ShapeDtypeStruct((steps, block, width), BF16)
-    vectors = (gain, bias, bias_q, bias_v)
-    return pl.pallas_call(
-        functools.partial(attend_kernel, frames, columns, height, groups * HALF),
-        out_shape=[shape] * 5,
-        grid_spec=pltpu.PrefetchScalarGridSpec(
-            num_scalar_prefetch=1,
-            grid=(steps,),
-            in_specs=grid_specs(frames, cells, width) + [whole(weight)] + [whole(v) for v in vectors],
-            out_specs=[row] * 5,
-            scratch_shapes=[pltpu.VMEM((block, width), BF16)] * 3,
-        ),
-        compiler_params=params(),
-        name="attend",
-    )(info, tokens4, tokens4, halo, weight, *vectors)
-
-
-def middle(tokens4, halo, d4, dhalo, o, w_proj, w_up, w_down, vectors, columns, chunk=512):
-    frames, groups, cells, width = tokens4.shape
-    steps, block = 2 * frames, 2 * cells
-    hidden_width = w_up.shape[-1]
-    row = pl.BlockSpec((None, block, width), lambda s, *_: (s, 0, 0))
     ins = grid_specs(frames, cells, width)
+    mine = blocks[0].shape
     return pl.pallas_call(
         functools.partial(middle_kernel, frames, columns, chunk),
         out_shape=[
@@ -325,47 +450,173 @@
             jax.ShapeDtypeStruct((frames, cells, width), BF16),
             jax.ShapeDtypeStruct((steps, block, width), F32),
             jax.ShapeDtypeStruct((steps, block, width), BF16),
-            jax.ShapeDtypeStruct((width, width), F32),
-            jax.ShapeDtypeStruct((width, hidden_width), F32),
-            jax.ShapeDtypeStruct((width, hidden_width), F32),
-            jax.ShapeDtypeStruct((8, hidden_width), F32),
+            jax.ShapeDtypeStruct(mine, F32),
+            jax.ShapeDtypeStruct(mine, BF16),
         ],
-        grid=(steps,),
-        in_specs=ins + ins + [row] + [whole(w) for w in (w_proj, w_up, w_down)] + [whole(v) for v in vectors],
-        out_specs=out_specs_of(frames, cells, width)
-        + [row, row]
-        + [
-            whole_out((width, width)),
-            whole_out((width, hidden_width)),
-            whole_out((width, hidden_width)),
-            whole_out((8, hidden_width)),
-        ],
+        grid_spec=pltpu.PrefetchScalarGridSpec(
+            num_scalar_prefetch=1,
+            grid=(steps,),
+            in_specs=ins + ins + [row, ANYWHERE, ANYWHERE],
+            out_specs=out_specs_of(frames, cells, width) + [row, row, whole_out(mine), whole_out(mine)],
+            scratch_shapes=[
+                pltpu.VMEM((width, width), BF16),
+                pltpu.VMEM((width, hidden_width), BF16),
+                pltpu.VMEM((hidden_width, width), BF16),
+                pltpu.VMEM((32, ROWS, 2 * LANE), BF16),
+                pltpu.VMEM((4, width), F32),
+                pltpu.VMEM((1, hidden_width), F32),
+                pltpu.VMEM((width, width), F32),
+                pltpu.VMEM((width, hidden_width), F32),
+                pltpu.VMEM((width, hidden_width), F32),
+                pltpu.VMEM((hidden_width, width), F32),
+                pltpu.VMEM((8, hidden_width), F32),
+                pltpu.SemaphoreType.DMA((2,)),
+            ],
+        ),
         compiler_params=params(),
+        cost_estimate=pl.CostEstimate(flops=8 * 10**10, bytes_accessed=4 * 10**7, transcendentals=10**7),
         name="middle",
-    )(tokens4, tokens4, halo, d4, d4, dhalo, o, w_proj, w_up, w_down, *vectors)
-
-
-def back(tokens4, halo, q, k, v, p, do, dx, weight, gain, bias, columns):
+    )(info, tokens4, tokens4, halo, d4, d4, dhalo, o, *blocks)
+
+
+def back(info, tokens4, halo, q, k, v, p, do, dx, blocks, columns):
     frames, groups, cells, width = tokens4.shape
     steps, block = 2 * frames, 2 * cells
     row = pl.BlockSpec((None, block, width), lambda s, *_: (s, 0, 0))
+    mine = blocks[0].shape
     return pl.pallas_call(
         functools.partial(back_kernel, frames, columns),
         out_shape=[
             jax.ShapeDtypeStruct((2, frames, cells, width), BF16),
             jax.ShapeDtypeStruct((frames, cells, width), BF16),
             jax.ShapeDtypeStruct((frames, cells, width), BF16),
-            jax.ShapeDtypeStruct((width, 3 * width), F32),
-            jax.ShapeDtypeStruct((8, 3 * width), F32),
+            jax.ShapeDtypeStruct(mine, F32),
+            jax.ShapeDtypeStruct(mine, BF16),
         ],
-        grid=(steps,),
-        in_specs=grid_specs(frames, cells, width) + [row] * 6 + [whole(weight), whole(gain), whole(bias)],
-        out_specs=out_specs_of(frames, cells, width)
-        + [whole_out((width, 3 * width)), whole_out((8, 3 * width))],
-        scratch_shapes=[pltpu.VMEM((block, 3 * width), BF16)],
+        grid_spec=pltpu.PrefetchScalarGridSpec(
+            num_scalar_prefetch=1,
+            grid=(steps,),
+            in_specs=grid_specs(frames, cells, width) + [row] * 6 + [ANYWHERE, ANYWHERE],
+            out_specs=out_specs_of(frames, cells, width) + [whole_out(mine), whole_out(mine)],
+            scratch_shapes=[
+                pltpu.VMEM((block, 3 * width), BF16),
+                pltpu.VMEM((width, 3 * width), BF16),
+                pltpu.VMEM((32, ROWS, LANE), BF16),
+                pltpu.VMEM((4, width), F32),
+                pltpu.VMEM((width, 3 * width), F32),
+                pltpu.VMEM((8, 3 * width), F32),
+                pltpu.SemaphoreType.DMA((2,)),
+            ],
+        ),
         compiler_params=params(),
+        cost_estimate=pl.CostEstimate(flops=4 * 10**10, bytes_accessed=4 * 10**7, transcendentals=10**6),
         name="back",
-    )(tokens4, tokens4, halo, q, k, v, p, do, dx, weight, gain, bias)
+    )(info, tokens4, tokens4, halo, q, k, v, p, do, dx, *blocks)
+
+
+AXES = ("dp", "rows")
+
+
+def flip_perm(axis, bits):
+    return [(i, i ^ bits) for i in range(lax.axis_size(axis))]
+
+
+def flipped(x, axis, bits):
+    return lax.ppermute(x, axis, flip_perm(axis, bits))
+
+
+def flipped_both(x, dp_bits, rows_bits):
+    dp, rows = lax.axis_size("dp"), lax.axis_size("rows")
+    pairs = [
+        (d * rows + r, (d ^ dp_bits) * rows + (r ^ rows_bits)) for d in range(dp) for r in range(rows)
+    ]
+    return lax.ppermute(x, AXES, pairs)
+
+
+def is_cube():
+    return lax.axis_size("dp") == 8 and lax.axis_size("rows") == 4
+
+
+def place_index():
+    return lax.axis_index("dp") * lax.axis_size("rows") + lax.axis_index("rows")
+
+
+def spread(shards):
+    index = place_index()
+    parts = []
+    for shard in shards:
+        count = shard.shape[0]
+        whole_size = count * lax.axis_size("dp") * lax.axis_size("rows")
+        zeros = jnp.zeros((whole_size,), shard.dtype)
+        parts.append(lax.dynamic_update_slice(zeros, shard, (index * count,)))
+    return jnp.concatenate(parts).reshape(ROWS, -1)
+
+
+def gather_blocks(matrices, vectors):
+    if is_cube():
+        pieces = []
+        for m in matrices:
+            pieces += [m[i : i + ROWS] for i in range(0, m.shape[0], ROWS)]
+        own = jnp.concatenate(pieces + [spread(vectors)], axis=1)
+        column = jnp.stack([own] + [flipped(own, "dp", 2 * z) for z in (1, 2, 3)])
+        plane = [column, flipped(column, "rows", 2), flipped(column, "dp", 1), flipped_both(column, 1, 2)]
+        mine = jnp.concatenate(plane)
+        return mine, flipped(mine, "rows", 1)
+    full = [lax.all_gather(m, AXES, axis=0, tiled=True) for m in matrices]
+    lanes = []
+    for m in full:
+        per = m.shape[0] // 32
+        blocks = m.reshape(32, per // ROWS, ROWS, m.shape[1]).transpose(0, 2, 1, 3)
+        lanes.append(blocks.reshape(32, ROWS, -1))
+    flat = jnp.concatenate([lax.all_gather(v, AXES, axis=0, tiled=True) for v in vectors])
+    tail = flat.reshape(1, ROWS, -1)
+    lanes.append(jnp.concatenate([tail, jnp.zeros((31,) + tail.shape[1:], tail.dtype)]))
+    natural = jnp.concatenate(lanes, axis=2)
+    relative = natural.reshape(4, 2, 2, 2, ROWS, -1).transpose(3, 1, 2, 0, 4, 5)
+    relative = relative.reshape(2, 16, ROWS, -1)
+    return relative[0], relative[1]
+
+
+def scatter_sums(keep, send, matrix_shapes, vector_sizes):
+    shards = lax.axis_size("dp") * lax.axis_size("rows")
+    matrices = []
+    if is_cube():
+        first = keep + flipped(send, "rows", 1).astype(F32)
+        low = first[4:].astype(BF16)
+        plane = (
+            first[:4]
+            + flipped(low[:4], "rows", 2).astype(F32)
+            + flipped(low[4:8], "dp", 1).astype(F32)
+            + flipped_both(low[8:], 1, 2).astype(F32)
+        )
+        low = plane[1:].astype(BF16)
+        total = plane[0]
+        for z in (1, 2, 3):
+            total += flipped(low[z - 1], "dp", 2 * z).astype(F32)
+        lane = 0
+        for rows, lanes in matrix_shapes:
+            per = rows // shards
+            pieces = [total[:, lane + i * lanes : lane + (i + 1) * lanes] for i in range(per // ROWS)]
+            matrices.append(jnp.concatenate(pieces, axis=0))
+            lane += per // ROWS * lanes
+        flat = total[:, lane:].reshape(-1)
+    else:
+        relative = jnp.stack([keep, send.astype(F32)]).reshape(2, 2, 2, 4, ROWS, -1)
+        natural = relative.transpose(3, 1, 2, 0, 4, 5).reshape(32, ROWS, -1)
+        lane = 0
+        for rows, lanes in matrix_shapes:
+            subs = rows // 32 // ROWS
+            piece = natural[:, :, lane : lane + subs * lanes].reshape(32, ROWS, subs, lanes)
+            whole_matrix = piece.transpose(0, 2, 1, 3).reshape(rows, lanes)
+            matrices.append(lax.psum_scatter(whole_matrix, AXES, scatter_dimension=0, tiled=True))
+            lane += subs * lanes
+        flat = lax.psum(natural[0, :, lane:], AXES).reshape(-1)
+    vectors, start = [], 0
+    for size in vector_sizes:
+        count = size // shards
+        vectors.append(lax.dynamic_slice(flat, (start + place_index() * count,), (count,)))
+        start += size
+    return matrices, vectors
 
 
 def per_device(
@@ -374,49 +625,46 @@
 ):
     frames, rows_here, columns, width = tokens.shape
     height = rows_here * lax.axis_size("rows")
-    axes = ("dp", "rows")
+    hidden_width = fc1_weight.shape[1]
     cells = HALF * columns
     grouped = (frames, rows_here // HALF, cells, width)
     tokens4, d4 = tokens.reshape(grouped), d_out.reshape(grouped)
+    attend_blocks = gather_blocks((qkv_weight,), (ln1_gain, ln1_bias, qv_bias))
     halo = from_behind(tokens4[:, 0], "rows", -1)
+    middle_blocks = gather_blocks(
+        (proj_weight, fc1_weight, fc2_weight), (proj_bias, ln2_gain, ln2_bias, fc2_bias, fc1_bias)
+    )
     dhalo = from_behind(d4[:, 0], "rows", -1)
-    gather = lambda w: lax.all_gather(w, axes, axis=0, tiled=True)
-    w_qkv, w_proj, w_up, w_down = (gather(w) for w in (qkv_weight, proj_weight, fc1_weight, fc2_weight))
-    vec = lambda v: gather(v).astype(F32)[None, :]
-    gain_one, bias_one, bias_qv = vec(ln1_gain), vec(ln1_bias), vec(qv_bias)
-    info = jnp.concatenate([frame_level, lax.axis_index("rows").astype(jnp.int32)[None]])
-    q, k, v, p, o = attend(
-        info, tokens4, halo, w_qkv, gain_one, bias_one, bias_qv[:, :width], bias_qv[:, width:],
-        height, columns,
-    )
-    vectors = tuple(vec(v) for v in (proj_bias, ln2_gain, ln2_bias, fc1_bias, fc2_bias))
-    m_top, m_own, m_halo, dx, do, dw_proj, dw_up, dw_down_t, small = middle(
-        tokens4, halo, d4, dhalo, o, w_proj, w_up, w_down, vectors, columns
-    )
-    g_top, g_own, g_halo, dw_qkv, small_back = back(
-        tokens4, halo, q, k, v, p, do, dx, w_qkv, gain_one, bias_one, columns
+    me = place_index() if is_cube() else 0
+    info = jnp.concatenate(
+        [frame_level, jnp.stack([lax.axis_index("rows"), jnp.int32(me)]).astype(jnp.int32)]
+    )
+    early = attend(info, tokens4, halo, attend_blocks, (), 0, height, columns)
+    q, k, v, p, o = attend(info, tokens4, halo, attend_blocks, early, frames, height, columns)
+    m_top, m_own, m_halo, dx, do, keep, send = middle(
+        info, tokens4, halo, d4, dhalo, o, middle_blocks, hidden_width, columns
+    )
+    (dw_proj, dw_up, dw_down), (db_proj, dg_two, db_two, db_down, db_up) = scatter_sums(
+        keep,
+        send,
+        ((width, width), (width, hidden_width), (hidden_width, width)),
+        (width, width, width, width, hidden_width),
+    )
+    g_top, g_own, g_halo, keep, send = back(
+        info, tokens4, halo, q, k, v, p, do, dx, attend_blocks, columns
+    )
+    (dw_qkv,), (dg_one, db_one, db_qv) = scatter_sums(
+        keep, send, ((width, 3 * width),), (width, width, 2 * width)
     )
 
     def assemble(top, own, back_rows):
         returned = from_behind(back_rows, "rows", 1)
         return jnp.stack([returned, top[0], own, top[1]], axis=1).reshape(tokens.shape)
 
-    scatter = lambda g: lax.psum_scatter(g, axes, scatter_dimension=0, tiled=True)
     return (
         assemble(m_top, m_own, m_halo),
         assemble(g_top, g_own, g_halo),
-        scatter(small_back[1, :width]),
-        scatter(small_back[2, :width]),
-        scatter(dw_qkv),
-        scatter(jnp.concatenate([small_back[0, :width], small_back[0, 2 * width :]])),
-        scatter(dw_proj),
-        scatter(small[4, :width]),
-        scatter(small[2, :width]),
-        scatter(small[3, :width]),
-        scatter(dw_up),
-        scatter(small[0]),
-        scatter(dw_down_t.T),
-        scatter(small[1, :width]),
+        dg_one, db_one, dw_qkv, db_qv, dw_proj, db_proj, dg_two, db_two, dw_up, db_up, dw_down, db_down,
     )
 
 

time: 799 us -> 400 us (0.50)
  waiting for transfers between devices: 372 us -> 90.9 us
  blocking collectives: 156 us -> 0 us
  starting transfers between devices: 3.98 us -> 38.5 us
  between operations: 14.4 us -> 1.05 us
  Pallas kernels: 218 us -> 230 us
    reduce_scatter x3 -> x0, waiting for transfers between devices: 226 us -> none  [per_device(): lax.psum_scatter(g, axes, scatter_dimension=0, tiled=True)]
    unnamed x8 -> x0, waiting for transfers between devices: 146 us -> none
    unnamed x2 -> x0, blocking collectives: 112 us -> none
    ppermute x0 -> x28, waiting for transfers between devices: none -> 80.8 us  [the longest x24 63.2 us: flipped(): return lax.ppermute(x, axis, flip_perm(axis, bits))]
    all_gather x1 -> x0, blocking collectives: 44.2 us -> none  [per_device(): gather = lambda w: lax.all_gather(w, axes, axis=0, tiled=True)]
    ppermute x0 -> x28, starting transfers between devices: none -> 35.2 us  [the longest x24 29.4 us: flipped(): return lax.ppermute(x, axis, flip_perm(axis, bits))]
    ppermute x4, waiting for transfers between devices: 0.01 us -> 10.1 us  [from_behind(): lax.ppermute(x, axis, [(i, (i + by) % devices) for i in range(devices)])]
    pallas_call x1 -> x2, Pallas kernels: 62.6 us -> 67.9 us  [attend(): pl.pallas_call(functools.partial(attend_kernel, frames, columns, height,...]
  transfers between devices with their start and end apart: 11 -> 32, of which waited for: 3 -> 14; matrix products, arithmetic and copies ran while one was open for 4% -> 6% of each run, Pallas kernels for 17% -> 17%
where the time goes in v2:
time: 400 us; the launch traced here: 394 us
  Pallas kernels  230 us (58%)
  waiting for transfers between devices  90.9 us (23%)
  starting transfers between devices  38.5 us (10%)
  local copies, waits for them, and re-layouts  27.3 us (7%)
  other arithmetic  5.64 us (1%)
    pallas_call x1, Pallas kernels, middle(): pl.pallas_call(functools.partial(middle_kernel, frames, columns, chunk),...  87.9 us
    pallas_call x1, Pallas kernels, back(): pl.pallas_call(functools.partial(back_kernel, frames, columns), out_shape...  74.3 us
    pallas_call x2, Pallas kernels, attend(): pl.pallas_call(functools.partial(attend_kernel, frames, columns, height,...  67.9 us
    ppermute x24, waiting for transfers between devices, flipped(): return lax.ppermute(x, axis, flip_perm(axis, bits))  63.2 us
    ppermute x24, starting transfers between devices, flipped(): return lax.ppermute(x, axis, flip_perm(axis, bits))  29.4 us
    ppermute x4, waiting for transfers between devices, flipped_both(): return lax.ppermute(x, AXES, pairs)  17.6 us
    ppermute x4, waiting for transfers between devices, from_behind(): lax.ppermute(x, axis, [(i, (i + by) % devices) for i in range(devices)])  10.1 us
  transfers between devices with their start and end apart: 32, of which 14 were waited for; matrix products, arithmetic and copies ran while one was open for 6% of the time, Pallas kernels for 17%

profile of v2, /device:TPU:0, one launch (start us, length us, event | category | flops | bytes accessed | tf_op | source)
XLA Modules:
  0.0 393.6 jit_solution(17470216450170446564)
XLA Ops:
  0.7 0.9 dynamic_update_slice.24
  1.5 0.8 dynamic_update_slice.25
  2.4 0.8 dynamic_update_slice.26
  4.0 3.0 collective-permute-start.2
  7.1 2.6 collective-permute-start.3
  9.7 0.8 dynamic_update_slice.27
  10.5 0.8 dynamic_update_slice.28
  11.4 0.8 dynamic_update_slice.29
  12.2 0.8 dynamic_update_slice.30
  13.9 0.8 dynamic_update_slice.31
  15.5 0.8 constant_dynamic-update-slice_fusion.12
  19.2 0.9 collective-permute-start.9
  20.1 3.5 collective-permute-start.10
  24.4 1.3 slice_bitcast_fusion.1
  25.7 1.3 slice_bitcast_fusion
  27.7 1.8 collective-permute-start.1
  30.1 1.7 collective-permute-start.6
  31.8 2.9 collective-permute-done.11
  34.7 2.4 collective-permute-start.7
  37.3 36.3 %collective-permute-done.5 = bf16[4,16,1664]{2,1,0:T(8,128)(2,1)S(1)} collective-permute-done((bf16[4,16,1664]{2,1,0:T(8,128)(2,1)S(1)}, bf16[4,16,1664]{2,1,0:T(8,128)(2,1)S(1)}, u32[]{:S(2)}, u32[]{:S(2)}) %collective-permute-start.5) | collective-permute-done | bytes 213024 | tf_op jit(solution)/shard_map/ppermute | solution.py:525
  73.9 1.8 collective-permute-start.13
  75.7 1.1 collective-permute-done.7
  77.3 6.5 %collective-permute-done.12 = bf16[4,16,4864]{2,1,0:T(8,128)(2,1)S(1)} collective-permute-done((bf16[4,16,4864]{2,1,0:T(8,128)(2,1)S(1)}, bf16[4,16,4864]{2,1,0:T(8,128)(2,1)S(1)}, u32[]{:S(2)}, u32[]{:S(2)}) %collective-permute-start.12) | collective-permute-done | bytes 622624 | tf_op jit(solution)/shard_map/ppermute | solution.py:525
  83.9 6.3 %collective-permute-done.13 = bf16[4,16,4864]{2,1,0:T(8,128)(2,1)S(1)} collective-permute-done((bf16[4,16,4864]{2,1,0:T(8,128)(2,1)S(1)}, bf16[4,16,4864]{2,1,0:T(8,128)(2,1)S(1)}, u32[]{:S(2)}, u32[]{:S(2)}) %collective-permute-start.13) | collective-permute-done | bytes 622624 | tf_op jit(solution)/shard_map/ppermute | solution.py:525
  90.2 1.2 collective-permute-done.14
  91.6 1.1 copy-done.7
  92.7 33.9 %attend.2 = (bf16[8,512,512]{2,1,0:T(8,128)(2,1)}, bf16[8,512,512]{2,1,0:T(8,128)(2,1)}, bf16[8,512,512]{2,1,0:T(8,128)(2,1)}, bf16[8,512,512]{2,1,0:T(8,128)(2,1)}, bf16[8,512,512]{2,1,0:T(8,128)(2,1)}) custom-call(s32[6]{0:T(128)} %pad_add_fusion.info, bf16[4,4,256,512]{3,2,1,0:T(8,128)(2,1)} %bitcast.94, bf16[4,4,256,512]{3,2,1,0:T(8,128)(2,1)} %bitcast.95, ...), custom_call_target="tpu_custom_call" | custom-call | flops 30000001024 | bytes 20000000 | tf_op jit(solution)/shard_map/attend/pallas_call | solution.py:416
  126.6 34.0 %attend.3 = (bf16[8,512,512]{2,1,0:T(8,128)(2,1)}, bf16[8,512,512]{2,1,0:T(8,128)(2,1)}, bf16[8,512,512]{2,1,0:T(8,128)(2,1)}, bf16[8,512,512]{2,1,0:T(8,128)(2,1)}, bf16[8,512,512]{2,1,0:T(8,128)(2,1)}) custom-call(s32[6]{0:T(128)} %pad_add_fusion.info, ...), custom_call_target="tpu_custom_call", output_to_operand_aliasing={{0}: (6, {}), {1}: (7, {}), {2}: (8, {}), {3}: (9, {}), {4}... | custom-call | flops 30000001024 | bytes 20000000 | tf_op jit(solution)/shard_map/attend/pallas_call | solution.py:416
  160.6 87.9 %middle.1 = (bf16[2,4,256,512]{3,2,1,0:T(8,128)(2,1)}, bf16[4,256,512]{2,1,0:T(8,128)(2,1)}, bf16[4,256,512]{2,1,0:T(8,128)(2,1)}, f32[8,512,512]{2,1,0:T(8,128)...) custom-call(s32[6]{0:T(128)} %pad_add_fusion.info, ...), custom_call_target="tpu_custom_call" | custom-call | flops 80000000000 | bytes 40000000 | tf_op jit(solution)/shard_map/middle/pallas_call | solution.py:445
  248.5 74.3 %back.1 = (bf16[2,4,256,512]{3,2,1,0:T(8,128)(2,1)}, bf16[4,256,512]{2,1,0:T(8,128)(2,1)}, bf16[4,256,512]{2,1,0:T(8,128)(2,1)}, f32[16,16,1664]{2,1,0:T(8,128)}, bf16[16,16,1664]{2,1,0:T(8,128)(2,1)}) custom-call(s32[6]{0:T(128)} %pad_add_fusion.info, bf16[4,4,256,512]{3,2,1,0:T(8,128)(2,1)} %bitcast.100, bf16[4,4,256,512]{3,2,1,0:T(8,128)(2,1)} %bitcast.101, ...), custom_call_target="tpu_custom_call" | custom-call | flops 40000000000 | bytes 40000000 | tf_op jit(solution)/shard_map/back/pallas_call | solution.py:487
  323.8 1.7 slice_bitcast_fusion.3
  325.8 1.0 collective-permute-start.16
  327.2 1.3 collective-permute-start.19
  328.5 1.5 collective-permute-start.20
  330.1 10.1 %collective-permute-done.17 = bf16[4,256,512]{2,1,0:T(8,128)(2,1)S(1)} collective-permute-done((bf16[4,256,512]{2,1,0:T(8,128)(2,1)}, bf16[4,256,512]{2,1,0:T(8,128)(2,1)S(1)}, u32[]{:S(2)}, u32[]{:S(2)}) %collective-permute-start.17) | collective-permute-done | bytes 1048608 | tf_op jit(solution)/shard_map/ppermute | solution.py:27
  340.2 2.2 collective-permute-start.21
  342.9 6.3 %collective-permute-done.21 = bf16[4,16,1664]{2,1,0:T(8,128)(2,1)S(1)} collective-permute-done((bf16[4,16,1664]{2,1,0:T(8,128)(2,1)S(1)}, bf16[4,16,1664]{2,1,0:T(8,128)(2,1)S(1)}, u32[]{:S(2)}, u32[]{:S(2)}) %collective-permute-start.21) | collective-permute-done | bytes 213024 | tf_op jit(solution)/shard_map/ppermute | solution.py:533
  349.8 3.8 collective-permute-start.23
  354.8 1.3 collective-permute-start.26
  356.1 1.5 collective-permute-start.27
  358.9 2.4 copy.47
  361.3 2.3 copy.46
  363.7 1.5 collective-permute-done.26
  365.1 4.3 %collective-permute-done.27 = bf16[4,16,4864]{2,1,0:T(8,128)(2,1)S(1)} collective-permute-done((bf16[4,16,4864]{2,1,0:T(8,128)(2,1)S(1)}, bf16[4,16,4864]{2,1,0:T(8,128)(2,1)S(1)}, u32[]{:S(2)}, u32[]{:S(2)}) %collective-permute-start.27) | collective-permute-done | bytes 622624 | tf_op jit(solution)/shard_map/ppermute | solution.py:525
  369.4 9.1 %collective-permute-done.28 = bf16[4,16,4864]{2,1,0:T(8,128)(2,1)S(1)} collective-permute-done((bf16[4,16,4864]{2,1,0:T(8,128)(2,1)S(1)}, bf16[4,16,4864]{2,1,0:T(8,128)(2,1)S(1)}, u32[]{:S(2)}, u32[]{:S(2)}) %collective-permute-start.28) | collective-permute-done | bytes 622624 | tf_op jit(solution)/shard_map/ppermute | solution.py:533
  379.1 4.1 %collective-permute-start.30 = (bf16[16,4864]{1,0:T(8,128)(2,1)S(1)}, bf16[16,4864]{1,0:T(8,128)(2,1)S(1)}, u32[]{:S(2)}, u32[]{:S(2)}) collective-permute-start(bf16[16,4864]{1,0:T(8,128)(2,1)S(1)} %get-tuple-element.78), channel_id=1, source_target_pairs={{0,16},{4,20},{8,24},{12,28},{16,0},{20,4},{24,8},{28,12},{1,17},{... | collective-permute-start | bytes 466952 | tf_op jit(solution)/shard_map/ppermute | solution.py:525
  385.1 2.9 collective-permute-done.30
  388.0 2.3 collective-permute-done.31
  (119 shorter events, 19.5 us)
Async XLA Ops:
  4.0 23.5 %collective-permute-start.2 = (bf16[16,1664]{1,0:T(8,128)(2,1)S(1)}, bf16[16,1664]{1,0:T(8,128)(2,1)S(1)}, u32[]{:S(2)}, u32[]{:S(2)}) collective-permute-start(bf16[16,1664]{1,0:T(8,128)(2,1)S(1)} %get-tuple-element.88), channel_id=1, source_target_pairs={{0,8},{4,12},{8,0},{12,4},{16,24},{20,28},{24,16},{28,20},{1,9},{5... | collective-permute-start | bytes 159752 | tf_op jit(solution)/shard_map/ppermute | solution.py:525
  7.1 20.6 %collective-permute-start.3 = (bf16[16,1664]{1,0:T(8,128)(2,1)S(1)}, bf16[16,1664]{1,0:T(8,128)(2,1)S(1)}, u32[]{:S(2)}, u32[]{:S(2)}) collective-permute-start(bf16[16,1664]{1,0:T(8,128)(2,1)S(1)} %get-tuple-element.88), channel_id=1, source_target_pairs={{0,16},{4,20},{8,24},{12,28},{16,0},{20,4},{24,8},{28,12},{1,17},{... | collective-permute-start | bytes 159752 | tf_op jit(solution)/shard_map/ppermute | solution.py:525
  9.6 18.0 %collective-permute-start.4 = (bf16[16,1664]{1,0:T(8,128)(2,1)S(1)}, bf16[16,1664]{1,0:T(8,128)(2,1)S(1)}, u32[]{:S(2)}, u32[]{:S(2)}) collective-permute-start(bf16[16,1664]{1,0:T(8,128)(2,1)S(1)} %get-tuple-element.88), channel_id=1, source_target_pairs={{0,24},{4,28},{8,16},{12,20},{16,8},{20,12},{24,0},{28,4},{1,25},{... | collective-permute-start | bytes 159752 | tf_op jit(solution)/shard_map/ppermute | solution.py:525
  13.3 13.7 %copy-start.6 = (s32[4]{0:T(128)S(1)}, s32[4]{0:T(128)}, u32[]{:S(2)}) copy-start(s32[4]{0:T(128)} %param.16) | copy-start | bytes 52
  19.2 10.4 %collective-permute-start.9 = (bf16[16,4864]{1,0:T(8,128)(2,1)S(1)}, bf16[16,4864]{1,0:T(8,128)(2,1)S(1)}, u32[]{:S(2)}, u32[]{:S(2)}) collective-permute-start(bf16[16,4864]{1,0:T(8,128)(2,1)S(1)} %constant_dynamic-update-slice_fusion.7), channel_id=1, source_target_pairs={{0,8},{4,12},{8,0},{12,4},{16,24},{20,28},{24,16},{28,20},{1,9},{5... | collective-permute-start | bytes 466952 | tf_op jit(solution)/shard_map/ppermute | solution.py:525
  20.1 10.0 %collective-permute-start.10 = (bf16[16,4864]{1,0:T(8,128)(2,1)S(1)}, bf16[16,4864]{1,0:T(8,128)(2,1)S(1)}, u32[]{:S(2)}, u32[]{:S(2)}) collective-permute-start(bf16[16,4864]{1,0:T(8,128)(2,1)S(1)} %constant_dynamic-update-slice_fusion.7), channel_id=1, source_target_pairs={{0,16},{4,20},{8,24},{12,28},{16,0},{20,4},{24,8},{28,12},{1,17},{... | collective-permute-start | bytes 466952 | tf_op jit(solution)/shard_map/ppermute | solution.py:525
  27.6 7.1 %collective-permute-start.11 = (bf16[16,4864]{1,0:T(8,128)(2,1)S(1)}, bf16[16,4864]{1,0:T(8,128)(2,1)S(1)}, u32[]{:S(2)}, u32[]{:S(2)}) collective-permute-start(bf16[16,4864]{1,0:T(8,128)(2,1)S(1)} %constant_dynamic-update-slice_fusion.7), channel_id=1, source_target_pairs={{0,24},{4,28},{8,16},{12,20},{16,8},{20,12},{24,0},{28,4},{1,25},{... | collective-permute-start | bytes 466952 | tf_op jit(solution)/shard_map/ppermute | solution.py:525
  27.6 64.0 %collective-permute-start = (bf16[4,256,512]{2,1,0:T(8,128)(2,1)S(1)}, bf16[4,256,512]{2,1,0:T(8,128)(2,1)S(1)}, u32[]{:S(2)}, u32[]{:S(2)}) collective-permute-start(bf16[4,256,512]{2,1,0:T(8,128)(2,1)S(1)} %slice_bitcast_fusion.1), channel_id=1, source_target_pairs={{0,3},{1,0},{2,1},{3,2},{4,7},{5,4},{6,5},{7,6},{8,11},{9,8},{10,9... | collective-permute-start | bytes 3145736 | tf_op jit(solution)/shard_map/ppermute | solution.py:27
  27.7 132.9 %collective-permute-start.1 = (bf16[4,256,512]{2,1,0:T(8,128)(2,1)S(1)}, bf16[4,256,512]{2,1,0:T(8,128)(2,1)}, u32[]{:S(2)}, u32[]{:S(2)}) collective-permute-start(bf16[4,256,512]{2,1,0:T(8,128)(2,1)S(1)} %slice_bitcast_fusion), channel_id=1, source_target_pairs={{0,3},{1,0},{2,1},{3,2},{4,7},{5,4},{6,5},{7,6},{8,11},{9,8},{10,9... | collective-permute-start | bytes 3145736 | tf_op jit(solution)/shard_map/ppermute | solution.py:27
  29.6 44.0 %collective-permute-start.5 = (bf16[4,16,1664]{2,1,0:T(8,128)(2,1)S(1)}, bf16[4,16,1664]{2,1,0:T(8,128)(2,1)S(1)}, u32[]{:S(2)}, u32[]{:S(2)}) collective-permute-start(bf16[4,16,1664]{2,1,0:T(8,128)(2,1)S(1)} %pad_maximum_fusion.3), channel_id=1, source_target_pairs={{0,2},{1,3},{2,0},{3,1},{4,6},{5,7},{6,4},{7,5},{8,10},{9,11},{10,... | collective-permute-start | bytes 638984 | tf_op jit(solution)/shard_map/ppermute | solution.py:525
  30.1 43.8 %collective-permute-start.6 = (bf16[4,16,1664]{2,1,0:T(8,128)(2,1)S(1)}, bf16[4,16,1664]{2,1,0:T(8,128)(2,1)S(1)}, u32[]{:S(2)}, u32[]{:S(2)}) collective-permute-start(bf16[4,16,1664]{2,1,0:T(8,128)(2,1)S(1)} %pad_maximum_fusion.3), channel_id=1, source_target_pairs={{0,4},{4,0},{8,12},{12,8},{16,20},{20,16},{24,28},{28,24},{1,5},{5... | collective-permute-start | bytes 638984 | tf_op jit(solution)/shard_map/ppermute | solution.py:525
  34.7 42.1 %collective-permute-start.7 = (bf16[4,16,1664]{2,1,0:T(8,128)(2,1)S(1)}, bf16[4,16,1664]{2,1,0:T(8,128)(2,1)S(1)}, u32[]{:S(2)}, u32[]{:S(2)}) collective-permute-start(bf16[4,16,1664]{2,1,0:T(8,128)(2,1)S(1)} %pad_maximum_fusion.3), channel_id=1, source_target_pairs={{0,6},{1,7},{2,4},{3,5},{4,2},{5,3},{6,0},{7,1},{8,14},{9,15},{10,... | collective-permute-start | bytes 638984 | tf_op jit(solution)/shard_map/ppermute | solution.py:533
  73.6 10.2 %collective-permute-start.12 = (bf16[4,16,4864]{2,1,0:T(8,128)(2,1)S(1)}, bf16[4,16,4864]{2,1,0:T(8,128)(2,1)S(1)}, u32[]{:S(2)}, u32[]{:S(2)}) collective-permute-start(bf16[4,16,4864]{2,1,0:T(8,128)(2,1)S(1)} %pad_maximum_fusion.2), channel_id=1, source_target_pairs={{0,2},{1,3},{2,0},{3,1},{4,6},{5,7},{6,4},{7,5},{8,10},{9,11},{10,... | collective-permute-start | bytes 1867784 | tf_op jit(solution)/shard_map/ppermute | solution.py:525
  73.9 16.3 %collective-permute-start.13 = (bf16[4,16,4864]{2,1,0:T(8,128)(2,1)S(1)}, bf16[4,16,4864]{2,1,0:T(8,128)(2,1)S(1)}, u32[]{:S(2)}, u32[]{:S(2)}) collective-permute-start(bf16[4,16,4864]{2,1,0:T(8,128)(2,1)S(1)} %pad_maximum_fusion.2), channel_id=1, source_target_pairs={{0,4},{4,0},{8,12},{12,8},{16,20},{20,16},{24,28},{28,24},{1,5},{5... | collective-permute-start | bytes 1867784 | tf_op jit(solution)/shard_map/ppermute | solution.py:525
  76.8 14.6 %collective-permute-start.14 = (bf16[4,16,4864]{2,1,0:T(8,128)(2,1)S(1)}, bf16[4,16,4864]{2,1,0:T(8,128)(2,1)S(1)}, u32[]{:S(2)}, u32[]{:S(2)}) collective-permute-start(bf16[4,16,4864]{2,1,0:T(8,128)(2,1)S(1)} %pad_maximum_fusion.2), channel_id=1, source_target_pairs={{0,6},{1,7},{2,4},{3,5},{4,2},{5,3},{6,0},{7,1},{8,14},{9,15},{10,... | collective-permute-start | bytes 1867784 | tf_op jit(solution)/shard_map/ppermute | solution.py:533
  77.3 14.3 %copy-start.5 = (bf16[16,16,1664]{2,1,0:T(8,128)(2,1)}, bf16[16,16,1664]{2,1,0:T(8,128)(2,1)S(1)}, u32[]{:S(2)}) copy-start(bf16[16,16,1664]{2,1,0:T(8,128)(2,1)S(1)} %constant_dynamic-update-slice_fusion.mine) | copy-start | bytes 2555908
  83.8 8.9 %collective-permute-start.8 = (bf16[16,16,1664]{2,1,0:T(8,128)(2,1)S(1)}, bf16[16,16,1664]{2,1,0:T(8,128)(2,1)}, u32[]{:S(2)}, u32[]{:S(2)}) collective-permute-start(bf16[16,16,1664]{2,1,0:T(8,128)(2,1)S(1)} %constant_dynamic-update-slice_fusion.mine), channel_id=1, source_target_pairs={{0,1},{1,0},{2,3},{3,2},{4,5},{5,4},{6,7},{7,6},{8,9},{9,8},{10,11... | collective-permute-start | bytes 2555912 | tf_op jit(solution)/shard_map/ppermute | solution.py:525
  91.5 35.1 %copy-start.4 = (bf16[16,16,4864]{2,1,0:T(8,128)(2,1)}, bf16[16,16,4864]{2,1,0:T(8,128)(2,1)S(1)}, u32[]{:S(2)}) copy-start(bf16[16,16,4864]{2,1,0:T(8,128)(2,1)S(1)} %constant_dynamic-update-slice_fusion.14.mine) | copy-start | bytes 7471108
  91.5 69.1 %collective-permute-start.15 = (bf16[16,16,4864]{2,1,0:T(8,128)(2,1)S(1)}, bf16[16,16,4864]{2,1,0:T(8,128)(2,1)}, u32[]{:S(2)}, u32[]{:S(2)}) collective-permute-start(bf16[16,16,4864]{2,1,0:T(8,128)(2,1)S(1)} %constant_dynamic-update-slice_fusion.14.mine), channel_id=1, source_target_pairs={{0,1},{1,0},{2,3},{3,2},{4,5},{5,4},{6,7},{7,6},{8,9},{9,8},{10,11... | collective-permute-start | bytes 7471112 | tf_op jit(solution)/shard_map/ppermute | solution.py:525
  91.6 1.1 copy-start.7
  322.9 2.7 copy-start
  322.9 3.9 collective-permute-start.18
  323.3 30.5 %collective-permute-start.25 = (bf16[16,16,4864]{2,1,0:T(8,128)(2,1)}, bf16[16,16,4864]{2,1,0:T(8,128)(2,1)S(1)}, u32[]{:S(2)}, u32[]{:S(2)}) collective-permute-start(bf16[16,16,4864]{2,1,0:T(8,128)(2,1)} %get-tuple-element.57), channel_id=1, source_target_pairs={{0,1},{1,0},{2,3},{3,2},{4,5},{5,4},{6,7},{7,6},{8,9},{9,8},{10,11... | collective-permute-start | bytes 7471112 | tf_op jit(solution)/shard_map/ppermute | solution.py:525
  323.4 16.7 %collective-permute-start.17 = (bf16[4,256,512]{2,1,0:T(8,128)(2,1)}, bf16[4,256,512]{2,1,0:T(8,128)(2,1)S(1)}, u32[]{:S(2)}, u32[]{:S(2)}) collective-permute-start(bf16[4,256,512]{2,1,0:T(8,128)(2,1)} %get-tuple-element.51), channel_id=1, source_target_pairs={{0,1},{1,2},{2,3},{3,0},{4,5},{5,6},{6,7},{7,4},{8,9},{9,10},{10,1... | collective-permute-start | bytes 3145736 | tf_op jit(solution)/shard_map/ppermute | solution.py:27
  325.5 1.5 copy-start.1
  325.8 30.4 %collective-permute-start.16 = (bf16[4,256,512]{2,1,0:T(8,128)(2,1)}, bf16[4,256,512]{2,1,0:T(8,128)(2,1)S(1)}, u32[]{:S(2)}, u32[]{:S(2)}) collective-permute-start(bf16[4,256,512]{2,1,0:T(8,128)(2,1)} %get-tuple-element.42), channel_id=1, source_target_pairs={{0,1},{1,2},{2,3},{3,0},{4,5},{5,6},{6,7},{7,4},{8,9},{9,10},{10,1... | collective-permute-start | bytes 3145736 | tf_op jit(solution)/shard_map/ppermute | solution.py:27
  327.0 15.4 %copy-start.3 = (bf16[4,256,512]{2,1,0:T(8,128)(2,1)S(1)}, bf16[4,256,512]{2,1,0:T(8,128)(2,1)}, u32[]{:S(2)}) copy-start(bf16[4,256,512]{2,1,0:T(8,128)(2,1)} %get-tuple-element.53) | copy-start | bytes 3145732
  327.2 15.7 %collective-permute-start.19 = (bf16[4,16,1664]{2,1,0:T(8,128)(2,1)S(1)}, bf16[4,16,1664]{2,1,0:T(8,128)(2,1)S(1)}, u32[]{:S(2)}, u32[]{:S(2)}) collective-permute-start(bf16[4,16,1664]{2,1,0:T(8,128)(2,1)S(1)} %get-tuple-element.73), channel_id=1, source_target_pairs={{0,2},{1,3},{2,0},{3,1},{4,6},{5,7},{6,4},{7,5},{8,10},{9,11},{10,... | collective-permute-start | bytes 638984 | tf_op jit(solution)/shard_map/ppermute | solution.py:525
  328.5 14.4 %collective-permute-start.20 = (bf16[4,16,1664]{2,1,0:T(8,128)(2,1)S(1)}, bf16[4,16,1664]{2,1,0:T(8,128)(2,1)S(1)}, u32[]{:S(2)}, u32[]{:S(2)}) collective-permute-start(bf16[4,16,1664]{2,1,0:T(8,128)(2,1)S(1)} %get-tuple-element.75), channel_id=1, source_target_pairs={{0,4},{4,0},{8,12},{12,8},{16,20},{20,16},{24,28},{28,24},{1,5},{5... | collective-permute-start | bytes 638984 | tf_op jit(solution)/shard_map/ppermute | solution.py:525
  340.2 9.1 %collective-permute-start.21 = (bf16[4,16,1664]{2,1,0:T(8,128)(2,1)S(1)}, bf16[4,16,1664]{2,1,0:T(8,128)(2,1)S(1)}, u32[]{:S(2)}, u32[]{:S(2)}) collective-permute-start(bf16[4,16,1664]{2,1,0:T(8,128)(2,1)S(1)} %get-tuple-element.74), channel_id=1, source_target_pairs={{0,6},{1,7},{2,4},{3,5},{4,2},{5,3},{6,0},{7,1},{8,14},{9,15},{10,... | collective-permute-start | bytes 638984 | tf_op jit(solution)/shard_map/ppermute | solution.py:533
  342.4 11.5 %slice-start = ((s8[4980736]{0:T(1024)(128)(4,1)}), s8[4194304]{0:T(1024)(128)(4,1)S(1)}, s32[]{:S(2)}) async-start(s8[4980736]{0:T(1024)(128)(4,1)} %bitcast.78), calls=%async_computation | async-start | bytes 8388608
  342.4 11.5 %slice-start.1 = ((s8[4980736]{0:T(1024)(128)(4,1)}), s8[786432]{0:T(1024)(128)(4,1)S(1)}, s32[]{:S(2)}) async-start(s8[4980736]{0:T(1024)(128)(4,1)} %bitcast.78), calls=%async_computation.1 | async-start | bytes 1572864
  349.4 8.2 %collective-permute-start.22 = (bf16[16,1664]{1,0:T(8,128)(2,1)S(1)}, bf16[16,1664]{1,0:T(8,128)(2,1)S(1)}, u32[]{:S(2)}, u32[]{:S(2)}) collective-permute-start(bf16[16,1664]{1,0:T(8,128)(2,1)S(1)} %get-tuple-element.84), channel_id=1, source_target_pairs={{0,8},{4,12},{8,0},{12,4},{16,24},{20,28},{24,16},{28,20},{1,9},{5... | collective-permute-start | bytes 159752 | tf_op jit(solution)/shard_map/ppermute | solution.py:525
  349.8 13.8 %collective-permute-start.23 = (bf16[16,1664]{1,0:T(8,128)(2,1)S(1)}, bf16[16,1664]{1,0:T(8,128)(2,1)S(1)}, u32[]{:S(2)}, u32[]{:S(2)}) collective-permute-start(bf16[16,1664]{1,0:T(8,128)(2,1)S(1)} %get-tuple-element.86), channel_id=1, source_target_pairs={{0,16},{4,20},{8,24},{12,28},{16,0},{20,4},{24,8},{28,12},{1,17},{... | collective-permute-start | bytes 159752 | tf_op jit(solution)/shard_map/ppermute | solution.py:525
  353.6 10.0 %collective-permute-start.24 = (bf16[16,1664]{1,0:T(8,128)(2,1)S(1)}, bf16[16,1664]{1,0:T(8,128)(2,1)S(1)}, u32[]{:S(2)}, u32[]{:S(2)}) collective-permute-start(bf16[16,1664]{1,0:T(8,128)(2,1)S(1)} %get-tuple-element.85), channel_id=1, source_target_pairs={{0,24},{4,28},{8,16},{12,20},{16,8},{20,12},{24,0},{28,4},{1,25},{... | collective-permute-start | bytes 159752 | tf_op jit(solution)/shard_map/ppermute | solution.py:525
  354.7 3.7 copy-start.2
  354.8 10.3 %collective-permute-start.26 = (bf16[4,16,4864]{2,1,0:T(8,128)(2,1)S(1)}, bf16[4,16,4864]{2,1,0:T(8,128)(2,1)S(1)}, u32[]{:S(2)}, u32[]{:S(2)}) collective-permute-start(bf16[4,16,4864]{2,1,0:T(8,128)(2,1)S(1)} %get-tuple-element.66), channel_id=1, source_target_pairs={{0,2},{1,3},{2,0},{3,1},{4,6},{5,7},{6,4},{7,5},{8,10},{9,11},{10,... | collective-permute-start | bytes 1867784 | tf_op jit(solution)/shard_map/ppermute | solution.py:525
  356.1 13.3 %collective-permute-start.27 = (bf16[4,16,4864]{2,1,0:T(8,128)(2,1)S(1)}, bf16[4,16,4864]{2,1,0:T(8,128)(2,1)S(1)}, u32[]{:S(2)}, u32[]{:S(2)}) collective-permute-start(bf16[4,16,4864]{2,1,0:T(8,128)(2,1)S(1)} %get-tuple-element.68), channel_id=1, source_target_pairs={{0,4},{4,0},{8,12},{12,8},{16,20},{20,16},{24,28},{28,24},{1,5},{5... | collective-permute-start | bytes 1867784 | tf_op jit(solution)/shard_map/ppermute | solution.py:525
  357.6 20.8 %collective-permute-start.28 = (bf16[4,16,4864]{2,1,0:T(8,128)(2,1)S(1)}, bf16[4,16,4864]{2,1,0:T(8,128)(2,1)S(1)}, u32[]{:S(2)}, u32[]{:S(2)}) collective-permute-start(bf16[4,16,4864]{2,1,0:T(8,128)(2,1)S(1)} %get-tuple-element.67), channel_id=1, source_target_pairs={{0,6},{1,7},{2,4},{3,5},{4,2},{5,3},{6,0},{7,1},{8,14},{9,15},{10,... | collective-permute-start | bytes 1867784 | tf_op jit(solution)/shard_map/ppermute | solution.py:533
  378.9 6.3 %collective-permute-start.29 = (bf16[16,4864]{1,0:T(8,128)(2,1)S(1)}, bf16[16,4864]{1,0:T(8,128)(2,1)S(1)}, u32[]{:S(2)}, u32[]{:S(2)}) collective-permute-start(bf16[16,4864]{1,0:T(8,128)(2,1)S(1)} %get-tuple-element.76), channel_id=1, source_target_pairs={{0,8},{4,12},{8,0},{12,4},{16,24},{20,28},{24,16},{28,20},{1,9},{5... | collective-permute-start | bytes 466952 | tf_op jit(solution)/shard_map/ppermute | solution.py:525
  379.1 9.0 %collective-permute-start.30 = (bf16[16,4864]{1,0:T(8,128)(2,1)S(1)}, bf16[16,4864]{1,0:T(8,128)(2,1)S(1)}, u32[]{:S(2)}, u32[]{:S(2)}) collective-permute-start(bf16[16,4864]{1,0:T(8,128)(2,1)S(1)} %get-tuple-element.78), channel_id=1, source_target_pairs={{0,16},{4,20},{8,24},{12,28},{16,0},{20,4},{24,8},{28,12},{1,17},{... | collective-permute-start | bytes 466952 | tf_op jit(solution)/shard_map/ppermute | solution.py:525
  383.2 7.2 %collective-permute-start.31 = (bf16[16,4864]{1,0:T(8,128)(2,1)S(1)}, bf16[16,4864]{1,0:T(8,128)(2,1)S(1)}, u32[]{:S(2)}, u32[]{:S(2)}) collective-permute-start(bf16[16,4864]{1,0:T(8,128)(2,1)S(1)} %get-tuple-element.77), channel_id=1, source_target_pairs={{0,24},{4,28},{8,16},{12,20},{16,8},{20,12},{24,0},{28,4},{1,25},{... | collective-permute-start | bytes 466952 | tf_op jit(solution)/shard_map/ppermute | solution.py:525

commit v3 on v2

--- a/solution.py
+++ b/solution.py
@@ -71,14 +71,19 @@
     )
 
 
-def stacked_identity():
-    row = lax.broadcasted_iota(jnp.int32, (CELLS, LANES), 0)
-    lane = lax.broadcasted_iota(jnp.int32, (CELLS, LANES), 1)
-    return jnp.where(row == lane % CELLS, 1.0, 0.0).astype(BF16)
-
-
-def flip(x):
-    return dot_t(stacked_identity(), block_diag(x)).astype(BF16)
+def dot_down(a, b):
+    pair = 2 * HEAD_DIM
+    first = lax.broadcasted_iota(jnp.int32, (CELLS, pair), 1) < HEAD_DIM
+    out = []
+    for lane in range(0, LANES, pair):
+        both = lax.dot_general(
+            a[:, lane : lane + pair],
+            b[:, lane : lane + pair],
+            (((0,), (0,)), ((), ())),
+            preferred_element_type=F32,
+        )
+        out.append(jnp.where(first, both[:HEAD_DIM], both[HEAD_DIM:]))
+    return jnp.concatenate(out, axis=1)
 
 
 def window_bias(info, frames, step, win, columns, height, rows_here):
@@ -155,11 +160,46 @@
             out[j, :, out.shape[-1] - tail.shape[-1] :] = tail.astype(out.dtype)
 
 
+def store_rows(out, halo, held, sem, local, total, step, frames, value):
+    slot = lax.rem(local, 2)
+    half = value.shape[0] // 2
+
+    def finish(slot):
+        for part in range(2):
+            rows = held.at[slot, pl.ds(part * half, half)]
+            pltpu.make_async_copy(rows, rows, sem.at[slot, part]).wait()
+
+    @pl.when(local >= 2)
+    def _():
+        finish(slot)
+
+    held[slot] = value
+    frame, window_row = lax.rem(step, frames), step // frames
+    top, bottom = (held.at[slot, pl.ds(part * half, half)] for part in range(2))
+    pltpu.make_async_copy(top, out.at[frame, 1 + 2 * window_row], sem.at[slot, 0]).start()
+
+    @pl.when(step < frames)
+    def _():
+        pltpu.make_async_copy(bottom, out.at[frame, 2], sem.at[slot, 1]).start()
+
+    if halo is not None:
+
+        @pl.when(step >= frames)
+        def _():
+            pltpu.make_async_copy(bottom, halo.at[frame], sem.at[slot, 1]).start()
+
+    @pl.when(local == total - 1)
+    def _():
+        finish(slot)
+        if total > 1:
+            finish(1 - slot)
+
+
 def attend_kernel(
     frames, columns, height, rows_here, first,
     info, top, own, halo, mine, theirs, *rest,
 ):
-    q_out, k_out, v_out, p_out, o_out, q_s, k_s, v_s, weight, vec, lines, sem = rest[-12:]
+    q_out, k_out, v_out, p_out, o_out, weight, vec, lines, sem = rest[-9:]
     step = pl.program_id(0) + first
     width = top.shape[-1]
 
@@ -178,38 +218,31 @@
     x = jnp.concatenate([top[...], bottom], axis=0).astype(F32)
     normed, _ = normalize(to_window_order(x, columns))
     hidden = (normed * gain[...] + bias[...]).astype(BF16)
-    q = (dot(hidden, weight[:, :width]) + bias_q[...]).astype(BF16) * 0.125
-    k = dot(hidden, weight[:, width : 2 * width]).astype(BF16)
-    v = (dot(hidden, weight[:, 2 * width :]) + bias_v[...]).astype(BF16)
-    q_s[...] = q
-    k_s[...] = k
-    v_s[...] = v
-    q_out[...] = q
-    k_out[...] = k
-    v_out[...] = v
-
-    def one_window(win, carry):
-        rows = pl.ds(pl.multiple_of(win * CELLS, CELLS), CELLS)
-        mask = window_bias(info, frames, step, win, columns, height, rows_here)
-        for group in range(width // LANES):
-            lanes = slice(group * LANES, (group + 1) * LANES)
-            scores = dot_t(k_s[rows, lanes], block_diag(q_s[rows, lanes])) + mask
-            exponent = jnp.exp(scores - jnp.max(scores, axis=0, keepdims=True))
-            probs = exponent * (1.0 / jnp.sum(exponent, axis=0, keepdims=True))
-            probs = probs.astype(BF16)
-            p_out[rows, lanes] = probs
-            out = dot(flip(probs), block_diag(v_s[rows, lanes]))
-            o_out[rows, lanes] = out.astype(BF16)
-        return carry
-
-    lax.fori_loop(0, columns // WIN, one_window, 0, unroll=2)
+    q_out[...] = (dot(hidden, weight[:, :width]) + bias_q[...]).astype(BF16) * 0.125
+    k_out[...] = dot(hidden, weight[:, width : 2 * width]).astype(BF16)
+    v_out[...] = (dot(hidden, weight[:, 2 * width :]) + bias_v[...]).astype(BF16)
+
+    wins, groups = range(columns // WIN), range(width // LANES)
+    items = [(w, slice(w * CELLS, (w + 1) * CELLS), slice(g * LANES, (g + 1) * LANES)) for w in wins for g in groups]
+    masks = [window_bias(info, frames, step, w, columns, height, rows_here) for w in wins]
+    scores = [dot_t(k_out[r, l], block_diag(q_out[r, l])) for _, r, l in items]
+    exponents = []
+    for (w, _, _), score in zip(items, scores):
+        score = score + masks[w]
+        exponents.append(jnp.exp(score - jnp.max(score, axis=0, keepdims=True)))
+    probs = [(e * (1.0 / jnp.sum(e, axis=0, keepdims=True))).astype(BF16) for e in exponents]
+    outs = [dot_down(p, v_out[r, l]).astype(BF16) for p, (_, r, l) in zip(probs, items)]
+    for (_, r, l), p, out in zip(items, probs, outs):
+        p_out[r, l] = p
+        o_out[r, l] = out
 
 
 def middle_kernel(
     frames, columns, chunk,
     info, top, own, halo, dtop, down, dhalo, o_in, mine, theirs,
-    m_top, m_own, m_halo, dx_out, do_out, keep, send,
-    w_proj, w_up, w_down, vec, lines, b_up, dw_proj, dw_up, dw_down_t, dw_down, small, sem,
+    m_out, m_halo, dx_out, do_out, keep, send,
+    w_proj, w_up, w_down, vec, lines, b_up, dw_proj, dw_up, dw_down_t, dw_down, small, g_s, du_s, held,
+    sem, out_sem,
 ):
     step = pl.program_id(0)
     width = top.shape[-1]
@@ -248,32 +281,30 @@
     dy_t = dy_low.T
     total = x2 + b_down[...]
     dh2 = jnp.zeros_like(x2)
-    for start in range(0, hidden_width, chunk):
-        part = slice(start, start + chunk)
-        u = dot(h2, w_up[:, part]) + b_up[:, part]
-        dg = dot_t(dy_low, w_down[part, :])
-        phi = 0.5 * (1.0 + lax.erf(u * INV_ROOT_TWO))
-        g = (u * phi).astype(BF16)
-        slope = phi + u * jnp.exp(-0.5 * u * u) * INV_ROOT_TWO_PI
-        du_full = dg * slope
-        du = du_full.astype(BF16)
-        total += dot(g, w_down[part, :])
-        dh2 += dot_t(du, w_up[:, part])
-        dw_up[:, part] += dot(h2_t, du)
-        dw_down_t[:, part] += dot(dy_t, g)
-        small[0:1, part] += jnp.sum(du_full, axis=0, keepdims=True)
+    parts = [slice(start, start + chunk) for start in range(0, hidden_width, chunk)]
+
+    def enter(part):
+        return dot(h2, w_up[:, part]) + b_up[:, part], dot_t(dy_low, w_down[part, :])
+
+    ahead = enter(parts[0])
+    for index, part in enumerate(parts + [None]):
+        if part is not None:
+            u, dg = ahead
+            if index + 1 < len(parts):
+                ahead = enter(parts[index + 1])
+            phi = 0.5 * (1.0 + lax.erf(u * INV_ROOT_TWO))
+            g_s[:, part] = (u * phi).astype(BF16)
+            du = dg * (phi + u * jnp.exp(-0.5 * u * u) * INV_ROOT_TWO_PI)
+            du_s[:, part] = du.astype(BF16)
+            small[0:1, part] += jnp.sum(du, axis=0, keepdims=True)
+        if index > 0:
+            old = parts[index - 1]
+            total += dot(g_s[:, old], w_down[old, :])
+            dh2 += dot_t(du_s[:, old], w_up[:, old])
+            dw_up[:, old] += dot(h2_t, du_s[:, old])
+            dw_down_t[:, old] += dot(dy_t, g_s[:, old])
     mixed = from_window_order(total, columns).astype(BF16)
-    half = mixed.shape[0] // 2
-    m_top[...] = mixed[:half]
-
-    @pl.when(step < frames)
-    def _():
-        m_own[...] = mixed[half:]
-
-    @pl.when(step >= frames)
-    def _():
-        m_halo[...] = mixed[half:]
-
+    store_rows(m_out, m_halo, held, out_sem, step, pl.num_programs(0), step, frames, mixed)
     small[1:2, :width] += jnp.sum(dy, axis=0, keepdims=True)
     small[2:3, :width] += jnp.sum(dh2 * normed, axis=0, keepdims=True)
     small[3:4, :width] += jnp.sum(dh2, axis=0, keepdims=True)
@@ -303,46 +334,58 @@
 
 
 def back_kernel(
-    frames, columns,
-    info, top, own, halo, q_in, k_in, v_in, p_in, do_in, dx_in, mine, theirs,
-    g_top, g_own, g_halo, keep, send, d_s, weight, vec, lines, dw, small, sem,
+    frames, columns, first, count, with_halo, starts, ends,
+    info, top, own, halo, q_in, k_in, v_in, p_in, do_in, dx_in, mine, theirs, *rest,
 ):
-    step = pl.program_id(0)
+    if not starts:
+        dw_before, small_before, *rest = rest[1 + with_halo :]
+    *outs, d_s, weight, vec, lines, held, sem, out_sem = rest
+    g_out, g_halo, dw, small = (outs[0], outs[1] if with_halo else None, outs[-2], outs[-1])
+    local = pl.program_id(0)
+    step = lax.rem(local + first, 2 * frames)
     width = top.shape[-1]
     gain, bias = (lines.at[i : i + 1] for i in range(2))
 
-    @pl.when(step == 0)
+    @pl.when(local == 0)
     def _():
         place(info, frames + 1, mine, theirs, [(0, 3 * width, ROWS, weight)], vec, sem.at[0], sem.at[1])
+        if starts:
+            dw[...] = jnp.zeros_like(dw)
+            small[...] = jnp.zeros_like(small)
+        else:
+            copies = [
+                pltpu.make_async_copy(dw_before, dw, sem.at[2]),
+                pltpu.make_async_copy(small_before, small, sem.at[3]),
+            ]
+            for copy in copies:
+                copy.start()
+            for copy in copies:
+                copy.wait()
         wait_bytes([weight], sem.at[0])
         wait_bytes([vec], sem.at[1])
         pieces = natural_rows(vec)
         per = width // LANE
         for line in range(lines.shape[0]):
             lines[line : line + 1, :] = jnp.concatenate(pieces[line * per : (line + 1) * per], axis=1)
-        dw[...] = jnp.zeros_like(dw)
-        small[...] = jnp.zeros_like(small)
-
-    def one_window(win, carry):
-        rows = pl.ds(pl.multiple_of(win * CELLS, CELLS), CELLS)
-        for group in range(width // LANES):
-            at = group * LANES
-            lanes = slice(at, at + LANES)
-            probs = p_in[rows, lanes]
-            full = probs.astype(F32)
-            do_diag = block_diag(do_in[rows, lanes])
-            dv = dot(probs, do_diag)
-            dp = dot_t(v_in[rows, lanes], do_diag)
-            ds = full * (dp - jnp.sum(dp * full, axis=0, keepdims=True))
-            ds = ds.astype(BF16)
-            dk = dot(ds, block_diag(q_in[rows, lanes]))
-            dq = dot(flip(ds), block_diag(k_in[rows, lanes])) * 0.125
-            d_s[rows, at : at + LANES] = dq.astype(BF16)
-            d_s[rows, width + at : width + at + LANES] = dk.astype(BF16)
-            d_s[rows, 2 * width + at : 2 * width + at + LANES] = dv.astype(BF16)
-        return carry
-
-    lax.fori_loop(0, columns // WIN, one_window, 0, unroll=2)
+
+    items = [
+        (slice(w * CELLS, (w + 1) * CELLS), g * LANES)
+        for w in range(columns // WIN)
+        for g in range(width // LANES)
+    ]
+    items = [(r, at, slice(at, at + LANES)) for r, at in items]
+    diags = [block_diag(do_in[r, l]) for r, _, l in items]
+    dps = [dot_t(v_in[r, l], diag) for (r, _, l), diag in zip(items, diags)]
+    dvs = [dot(p_in[r, l], diag).astype(BF16) for (r, _, l), diag in zip(items, diags)]
+    dss = []
+    for (r, _, l), dp in zip(items, dps):
+        full = p_in[r, l].astype(F32)
+        dss.append((full * (dp - jnp.sum(dp * full, axis=0, keepdims=True))).astype(BF16))
+    dks = [dot(ds, block_diag(q_in[r, l])).astype(BF16) for (r, _, l), ds in zip(items, dss)]
+    dqs = [(dot_down(ds, k_in[r, l]) * 0.125).astype(BF16) for (r, _, l), ds in zip(items, dss)]
+    for (r, at, _), dq, dk, dv in zip(items, dqs, dks, dvs):
+        for part, grad in enumerate((dq, dk, dv)):
+            d_s[r, part * width + at : part * width + at + LANES] = grad
     bottom = jnp.where(step < frames, own[...], halo[...])
     x = jnp.concatenate([top[...], bottom], axis=0).astype(F32)
     normed, inverse = normalize(to_window_order(x, columns))
@@ -355,43 +398,100 @@
     small[2:3, :width] += jnp.sum(dh, axis=0, keepdims=True)
     grad = dx_in[...] + norm_back(dh * gain[...], normed, inverse)
     grad = from_window_order(grad, columns).astype(BF16)
-    half = grad.shape[0] // 2
-    g_top[...] = grad[:half]
-
-    @pl.when(step < frames)
-    def _():
-        g_own[...] = grad[half:]
-
-    @pl.when(step >= frames)
-    def _():
-        g_halo[...] = grad[half:]
-
-    @pl.when(step == pl.num_programs(0) - 1)
-    def _():
-        pieces = [small[1:2, :width], small[2:3, :width], small[0:1, :width], small[0:1, 2 * width :]]
-        flat = jnp.concatenate(pieces, axis=1)
-        tail = jnp.concatenate([flat[:, i * LANE : (i + 1) * LANE] for i in range(ROWS)], axis=0)
-        hand_over(info, frames + 1, [(0, 3 * width, ROWS, dw)], tail, keep, send)
+    store_rows(g_out, g_halo, held, out_sem, local, count, step, frames, grad)
+
+    if ends:
+        keep, send = outs[1 + with_halo : 3 + with_halo]
+
+        @pl.when(local == count - 1)
+        def _():
+            pieces = [small[1:2, :width], small[2:3, :width], small[0:1, :width], small[0:1, 2 * width :]]
+            flat = jnp.concatenate(pieces, axis=1)
+            tail = jnp.concatenate([flat[:, i * LANE : (i + 1) * LANE] for i in range(ROWS)], axis=0)
+            hand_over(info, frames + 1, [(0, 3 * width, ROWS, dw)], tail, keep, send)
+
+
+def join_kernel(*refs):
+    out = refs[-1]
+    rows = refs[0].shape[0]
+    for index, ref in enumerate(refs[:-1]):
+        out[index * rows : (index + 1) * rows] = ref[...]
+
+
+def join(*parts):
+    shape = (len(parts) * parts[0].shape[0],) + parts[0].shape[1:]
+    vmem = pl.BlockSpec(memory_space=pltpu.VMEM)
+    return pl.pallas_call(
+        join_kernel,
+        out_shape=jax.ShapeDtypeStruct(shape, parts[0].dtype),
+        in_specs=[vmem] * len(parts),
+        out_specs=vmem,
+        compiler_params=pltpu.CompilerParams(vmem_limit_bytes=VMEM_LIMIT),
+        name="join",
+    )(*parts)
+
+
+def pack_kernel(index_ref, *refs):
+    vectors, (qkv, proj, up, down, a_out, b_out) = refs[:-6], refs[-6:]
+    index = index_ref[0]
+    wide = 2 * LANE
+
+    def spread_rows(sections, lanes):
+        row = lax.broadcasted_iota(jnp.int32, (ROWS, wide), 0)
+        total = jnp.zeros((ROWS, wide), F32)
+        for ref, base in sections:
+            count = ref.shape[0]
+            at = base + index * count
+            own = ref[...].astype(F32)[None, :]
+            own = jnp.concatenate([own, jnp.zeros((1, wide - count), F32)], axis=1)
+            moved = pltpu.roll(own, lax.rem(at, lanes), 1)
+            total = total + jnp.where(row == at // lanes, moved, 0.0)
+        return total[:, :lanes].astype(BF16)
+
+    width = proj.shape[1]
+    full = qkv.shape[1]
+    a_out[:, :full] = qkv[...]
+    sections = [(vectors[i], i * width) for i in range(3)]
+    a_out[:, full:] = spread_rows(sections, a_out.shape[1] - full)
+    hidden = up.shape[1]
+    b_out[:, :width] = proj[...]
+    b_out[:, width : width + hidden] = up[...]
+    for i in range(down.shape[0] // ROWS):
+        at = width + hidden + i * width
+        b_out[:, at : at + width] = down[i * ROWS : (i + 1) * ROWS]
+    full = width + 2 * hidden
+    sections = [(vectors[3 + i], i * width) for i in range(5)]
+    b_out[:, full:] = spread_rows(sections, b_out.shape[1] - full)
+
+
+def pack(index, vectors, qkv, proj, up, down):
+    lanes_a = qkv.shape[1] + LANE
+    lanes_b = proj.shape[1] + 2 * up.shape[1] + 2 * LANE
+    vmem = pl.BlockSpec(memory_space=pltpu.VMEM)
+    return pl.pallas_call(
+        pack_kernel,
+        out_shape=[
+            jax.ShapeDtypeStruct((ROWS, lanes_a), BF16),
+            jax.ShapeDtypeStruct((ROWS, lanes_b), BF16),
+        ],
+        in_specs=[pl.BlockSpec(memory_space=pltpu.SMEM)] + [vmem] * (len(vectors) + 4),
+        out_specs=[vmem, vmem],
+        name="pack",
+    )(index, *vectors, qkv, proj, up, down)
 
 
 def grid_specs(frames, cells, width, first=0):
     top = pl.BlockSpec(
         (None, None, cells, width),
-        lambda s, *_: ((s + first) % frames, 1 + 2 * ((s + first) // frames), 0, 0),
+        lambda s, *_: ((s + first) % frames, 1 + 2 * ((s + first) % (2 * frames) // frames), 0, 0),
     )
     own = pl.BlockSpec(
-        (None, None, cells, width), lambda s, *_: (jnp.minimum(s + first, frames - 1), 2, 0, 0)
+        (None, None, cells, width),
+        lambda s, *_: (jnp.minimum((s + first) % (2 * frames), frames - 1), 2, 0, 0),
     )
     halo = pl.BlockSpec(
-        (None, cells, width), lambda s, *_: (jnp.maximum(s + first - frames, 0), 0, 0)
-    )
-    return [top, own, halo]
-
-
-def out_specs_of(frames, cells, width):
-    top = pl.BlockSpec((None, None, cells, width), lambda s, *_: (s // frames, s % frames, 0, 0))
-    own = pl.BlockSpec((None, cells, width), lambda s, *_: (jnp.minimum(s, frames - 1), 0, 0))
-    halo = pl.BlockSpec((None, cells, width), lambda s, *_: (jnp.maximum(s - frames, 0), 0, 0))
+        (None, cells, width), lambda s, *_: (jnp.maximum((s + first) % (2 * frames) - frames, 0), 0, 0)
+    )
     return [top, own, halo]
 
 
@@ -421,8 +521,7 @@
             grid=(frames,),
             in_specs=grid_specs(frames, cells, width, first) + [ANYWHERE] * (2 + len(previous)),
             out_specs=[row] * 5,
-            scratch_shapes=[pltpu.VMEM((block, width), BF16)] * 3
-            + [
+            scratch_shapes=[
                 pltpu.VMEM((width, 3 * width), BF16),
                 pltpu.VMEM((32, ROWS, LANE), BF16),
                 pltpu.VMEM((4, width), F32),
@@ -436,7 +535,7 @@
     )(info, tokens4, tokens4, halo, *blocks, *previous)
 
 
-def middle(info, tokens4, halo, d4, dhalo, o, blocks, hidden_width, columns, chunk=512):
+def middle(info, tokens4, halo, d4, dhalo, o, blocks, hidden_width, columns, chunk=256):
     frames, groups, cells, width = tokens4.shape
     steps, block = 2 * frames, 2 * cells
     row = pl.BlockSpec((None, block, width), lambda s, *_: (s, 0, 0))
@@ -445,19 +544,18 @@
     return pl.pallas_call(
         functools.partial(middle_kernel, frames, columns, chunk),
         out_shape=[
-            jax.ShapeDtypeStruct((2, frames, cells, width), BF16),
-            jax.ShapeDtypeStruct((frames, cells, width), BF16),
-            jax.ShapeDtypeStruct((frames, cells, width), BF16),
+            jax.ShapeDtypeStruct(tokens4.shape, BF16),
+            jax.ShapeDtypeStruct(halo.shape, BF16),
             jax.ShapeDtypeStruct((steps, block, width), F32),
             jax.ShapeDtypeStruct((steps, block, width), BF16),
-            jax.ShapeDtypeStruct(mine, F32),
+            jax.ShapeDtypeStruct(mine, BF16),
             jax.ShapeDtypeStruct(mine, BF16),
         ],
         grid_spec=pltpu.PrefetchScalarGridSpec(
             num_scalar_prefetch=1,
             grid=(steps,),
             in_specs=ins + ins + [row, ANYWHERE, ANYWHERE],
-            out_specs=out_specs_of(frames, cells, width) + [row, row, whole_out(mine), whole_out(mine)],
+            out_specs=[ANYWHERE, ANYWHERE, row, row, whole_out(mine), whole_out(mine)],
             scratch_shapes=[
                 pltpu.VMEM((width, width), BF16),
                 pltpu.VMEM((width, hidden_width), BF16),
@@ -470,48 +568,64 @@
                 pltpu.VMEM((width, hidden_width), F32),
                 pltpu.VMEM((hidden_width, width), F32),
                 pltpu.VMEM((8, hidden_width), F32),
+                pltpu.VMEM((block, hidden_width), BF16),
+                pltpu.VMEM((block, hidden_width), BF16),
+                pltpu.VMEM((2, block, width), BF16),
                 pltpu.SemaphoreType.DMA((2,)),
+                pltpu.SemaphoreType.DMA((2, 2)),
             ],
         ),
         compiler_params=params(),
-        cost_estimate=pl.CostEstimate(flops=8 * 10**10, bytes_accessed=4 * 10**7, transcendentals=10**7),
+        cost_estimate=pl.CostEstimate(flops=9 * 10**10, bytes_accessed=4 * 10**7, transcendentals=10**7),
         name="middle",
     )(info, tokens4, tokens4, halo, d4, d4, dhalo, o, *blocks)
 
 
-def back(info, tokens4, halo, q, k, v, p, do, dx, blocks, columns):
+def back(info, tokens4, halo, q, k, v, p, do, dx, blocks, columns, before, first, count, ends):
     frames, groups, cells, width = tokens4.shape
     steps, block = 2 * frames, 2 * cells
-    row = pl.BlockSpec((None, block, width), lambda s, *_: (s, 0, 0))
+    row = pl.BlockSpec((None, block, width), lambda s, *_: ((s + first) % steps, 0, 0))
     mine = blocks[0].shape
+    dw, small = (width, 3 * width), (8, 3 * width)
+    handed = [jax.ShapeDtypeStruct(mine, BF16)] * 2
+    sums = [jax.ShapeDtypeStruct(dw, F32), jax.ShapeDtypeStruct(small, F32)]
+    held = 12
+    with_halo = first + count > frames
+    g_shapes = [jax.ShapeDtypeStruct(tokens4.shape, BF16), jax.ShapeDtypeStruct(halo.shape, BF16)]
+    g_shapes = g_shapes[: 1 + with_halo]
+    if before:
+        before = (before[0], *(before[1:2] if with_halo else ()), *before[-2:])
     return pl.pallas_call(
-        functools.partial(back_kernel, frames, columns),
-        out_shape=[
-            jax.ShapeDtypeStruct((2, frames, cells, width), BF16),
-            jax.ShapeDtypeStruct((frames, cells, width), BF16),
-            jax.ShapeDtypeStruct((frames, cells, width), BF16),
-            jax.ShapeDtypeStruct(mine, F32),
-            jax.ShapeDtypeStruct(mine, BF16),
-        ],
+        functools.partial(
+            back_kernel, frames, columns, first, count, with_halo, not before, ends
+        ),
+        out_shape=g_shapes + (handed if ends else sums),
         grid_spec=pltpu.PrefetchScalarGridSpec(
             num_scalar_prefetch=1,
-            grid=(steps,),
-            in_specs=grid_specs(frames, cells, width) + [row] * 6 + [ANYWHERE, ANYWHERE],
-            out_specs=out_specs_of(frames, cells, width) + [whole_out(mine), whole_out(mine)],
-            scratch_shapes=[
+            grid=(count,),
+            in_specs=grid_specs(frames, cells, width, first)
+            + [row] * 6
+            + [ANYWHERE] * (2 + len(before)),
+            out_specs=[ANYWHERE] * len(g_shapes)
+            + ([whole_out(mine)] * 2 if ends else [whole_out(dw), whole_out(small)]),
+            scratch_shapes=([pltpu.VMEM(dw, F32), pltpu.VMEM(small, F32)] if ends else [])
+            + [
                 pltpu.VMEM((block, 3 * width), BF16),
                 pltpu.VMEM((width, 3 * width), BF16),
                 pltpu.VMEM((32, ROWS, LANE), BF16),
                 pltpu.VMEM((4, width), F32),
-                pltpu.VMEM((width, 3 * width), F32),
-                pltpu.VMEM((8, 3 * width), F32),
-                pltpu.SemaphoreType.DMA((2,)),
+                pltpu.VMEM((2, block, width), BF16),
+                pltpu.SemaphoreType.DMA((4,)),
+                pltpu.SemaphoreType.DMA((2, 2)),
             ],
         ),
+        input_output_aliases={held + i: i for i in range(len(g_shapes))} if before else {},
         compiler_params=params(),
-        cost_estimate=pl.CostEstimate(flops=4 * 10**10, bytes_accessed=4 * 10**7, transcendentals=10**6),
+        cost_estimate=pl.CostEstimate(
+            flops=6 * 10**9 * count, bytes_accessed=5 * 10**6 * count, transcendentals=10**5
+        ),
         name="back",
-    )(info, tokens4, tokens4, halo, q, k, v, p, do, dx, *blocks)
+    )(info, tokens4, tokens4, halo, q, k, v, p, do, dx, *blocks, *before)
 
 
 AXES = ("dp", "rows")
@@ -541,27 +655,19 @@
     return lax.axis_index("dp") * lax.axis_size("rows") + lax.axis_index("rows")
 
 
-def spread(shards):
-    index = place_index()
-    parts = []
-    for shard in shards:
-        count = shard.shape[0]
-        whole_size = count * lax.axis_size("dp") * lax.axis_size("rows")
-        zeros = jnp.zeros((whole_size,), shard.dtype)
-        parts.append(lax.dynamic_update_slice(zeros, shard, (index * count,)))
-    return jnp.concatenate(parts).reshape(ROWS, -1)
+def after(value, *others):
+    return lax.optimization_barrier((value,) + others)[0]
+
+
+def along_z(own):
+    return [flipped(own, "dp", 2 * z) for z in (1, 2, 3)]
+
+
+def over_plane(column):
+    return [flipped(column, "rows", 2), flipped(column, "dp", 1), flipped_both(column, 1, 2)]
 
 
 def gather_blocks(matrices, vectors):
-    if is_cube():
-        pieces = []
-        for m in matrices:
-            pieces += [m[i : i + ROWS] for i in range(0, m.shape[0], ROWS)]
-        own = jnp.concatenate(pieces + [spread(vectors)], axis=1)
-        column = jnp.stack([own] + [flipped(own, "dp", 2 * z) for z in (1, 2, 3)])
-        plane = [column, flipped(column, "rows", 2), flipped(column, "dp", 1), flipped_both(column, 1, 2)]
-        mine = jnp.concatenate(plane)
-        return mine, flipped(mine, "rows", 1)
     full = [lax.all_gather(m, AXES, axis=0, tiled=True) for m in matrices]
     lanes = []
     for m in full:
@@ -577,46 +683,64 @@
     return relative[0], relative[1]
 
 
-def scatter_sums(keep, send, matrix_shapes, vector_sizes):
+def own_rows(total, matrix_shapes, shards):
+    matrices, lane = [], 0
+    for rows, lanes in matrix_shapes:
+        subs = rows // shards // ROWS
+        pieces = [total[:, lane + i * lanes : lane + (i + 1) * lanes] for i in range(subs)]
+        matrices.append(jnp.concatenate(pieces, axis=0))
+        lane += subs * lanes
+    return matrices, total[:, lane:].reshape(-1)
+
+
+def wide(x):
+    return x.astype(F32)
+
+
+def sum_cores(keep, send):
+    first = wide(keep) + wide(flipped(send, "rows", 1))
+    return first[:4], first[4:].astype(BF16)
+
+
+def sum_plane(kept, low):
+    plane = (
+        kept
+        + wide(flipped(low[:4], "rows", 2))
+        + wide(flipped(low[4:8], "dp", 1))
+        + wide(flipped_both(low[8:], 1, 2))
+    )
+    return plane[0], plane[1:].astype(BF16)
+
+
+def sum_line(kept, low):
+    for z in (1, 2, 3):
+        kept += wide(flipped(low[z - 1], "dp", 2 * z))
+    return kept
+
+
+def own_vectors(flat, vector_sizes):
     shards = lax.axis_size("dp") * lax.axis_size("rows")
-    matrices = []
-    if is_cube():
-        first = keep + flipped(send, "rows", 1).astype(F32)
-        low = first[4:].astype(BF16)
-        plane = (
-            first[:4]
-            + flipped(low[:4], "rows", 2).astype(F32)
-            + flipped(low[4:8], "dp", 1).astype(F32)
-            + flipped_both(low[8:], 1, 2).astype(F32)
-        )
-        low = plane[1:].astype(BF16)
-        total = plane[0]
-        for z in (1, 2, 3):
-            total += flipped(low[z - 1], "dp", 2 * z).astype(F32)
-        lane = 0
-        for rows, lanes in matrix_shapes:
-            per = rows // shards
-            pieces = [total[:, lane + i * lanes : lane + (i + 1) * lanes] for i in range(per // ROWS)]
-            matrices.append(jnp.concatenate(pieces, axis=0))
-            lane += per // ROWS * lanes
-        flat = total[:, lane:].reshape(-1)
-    else:
-        relative = jnp.stack([keep, send.astype(F32)]).reshape(2, 2, 2, 4, ROWS, -1)
-        natural = relative.transpose(3, 1, 2, 0, 4, 5).reshape(32, ROWS, -1)
-        lane = 0
-        for rows, lanes in matrix_shapes:
-            subs = rows // 32 // ROWS
-            piece = natural[:, :, lane : lane + subs * lanes].reshape(32, ROWS, subs, lanes)
-            whole_matrix = piece.transpose(0, 2, 1, 3).reshape(rows, lanes)
-            matrices.append(lax.psum_scatter(whole_matrix, AXES, scatter_dimension=0, tiled=True))
-            lane += subs * lanes
-        flat = lax.psum(natural[0, :, lane:], AXES).reshape(-1)
     vectors, start = [], 0
     for size in vector_sizes:
         count = size // shards
         vectors.append(lax.dynamic_slice(flat, (start + place_index() * count,), (count,)))
         start += size
-    return matrices, vectors
+    return vectors
+
+
+def scatter_sums(keep, send, matrix_shapes):
+    matrices = []
+    relative = jnp.stack([wide(keep), wide(send)]).reshape(2, 2, 2, 4, ROWS, -1)
+    natural = relative.transpose(3, 1, 2, 0, 4, 5).reshape(32, ROWS, -1)
+    lane = 0
+    for rows, lanes in matrix_shapes:
+        subs = rows // 32 // ROWS
+        piece = natural[:, :, lane : lane + subs * lanes].reshape(32, ROWS, subs, lanes)
+        whole_matrix = piece.transpose(0, 2, 1, 3).reshape(rows, lanes)
+        matrices.append(lax.psum_scatter(whole_matrix, AXES, scatter_dimension=0, tiled=True))
+        lane += subs * lanes
+    flat = lax.psum(natural[0, :, lane:], AXES).reshape(-1)
+    return matrices, flat
 
 
 def per_device(
@@ -629,41 +753,75 @@
     cells = HALF * columns
     grouped = (frames, rows_here // HALF, cells, width)
     tokens4, d4 = tokens.reshape(grouped), d_out.reshape(grouped)
-    attend_blocks = gather_blocks((qkv_weight,), (ln1_gain, ln1_bias, qv_bias))
-    halo = from_behind(tokens4[:, 0], "rows", -1)
-    middle_blocks = gather_blocks(
-        (proj_weight, fc1_weight, fc2_weight), (proj_bias, ln2_gain, ln2_bias, fc2_bias, fc1_bias)
-    )
-    dhalo = from_behind(d4[:, 0], "rows", -1)
-    me = place_index() if is_cube() else 0
-    info = jnp.concatenate(
-        [frame_level, jnp.stack([lax.axis_index("rows"), jnp.int32(me)]).astype(jnp.int32)]
-    )
+    if is_cube():
+        me = place_index().astype(jnp.int32)
+        vectors = (
+            ln1_gain, ln1_bias, qv_bias, proj_bias, ln2_gain, ln2_bias, fc2_bias, fc1_bias
+        )
+        own_a, own_b = pack(me[None], vectors, qkv_weight, proj_weight, fc1_weight, fc2_weight)
+        z_a = along_z(own_a)
+        own_b = after(own_b, *z_a)
+        z_b = along_z(own_b)
+        column_a = join(own_a[None], *(z[None] for z in z_a))
+        halo = from_behind(after(tokens4[:, 0], column_a), "rows", -1)
+        plane_a = over_plane(column_a)
+        mine_a = join(column_a, *plane_a)
+        attend_blocks = (mine_a, flipped(mine_a, "rows", 1))
+        column_b = join(own_b[None], *(z[None] for z in z_b))
+        column_b = after(column_b, mine_a)
+        plane_b = over_plane(column_b)
+        dhalo = from_behind(after(d4[:, 0], mine_a), "rows", -1)
+    else:
+        me = jnp.int32(0)
+        attend_blocks = gather_blocks((qkv_weight,), (ln1_gain, ln1_bias, qv_bias))
+        middle_blocks = gather_blocks(
+            (proj_weight, fc1_weight, fc2_weight), (proj_bias, ln2_gain, ln2_bias, fc2_bias, fc1_bias)
+        )
+        halo = from_behind(tokens4[:, 0], "rows", -1)
+        dhalo = from_behind(d4[:, 0], "rows", -1)
+    info = jnp.concatenate([frame_level, jnp.stack([lax.axis_index("rows").astype(jnp.int32), me])])
     early = attend(info, tokens4, halo, attend_blocks, (), 0, height, columns)
+    if is_cube():
+        plane_b = lax.optimization_barrier((*plane_b, early[0]))[:3]
+        mine_b = join(column_b, *plane_b)
+        middle_blocks = (mine_b, flipped(mine_b, "rows", 1))
     q, k, v, p, o = attend(info, tokens4, halo, attend_blocks, early, frames, height, columns)
-    m_top, m_own, m_halo, dx, do, keep, send = middle(
+    m_out, m_halo, dx, do, keep, send = middle(
         info, tokens4, halo, d4, dhalo, o, middle_blocks, hidden_width, columns
     )
-    (dw_proj, dw_up, dw_down), (db_proj, dg_two, db_two, db_down, db_up) = scatter_sums(
-        keep,
-        send,
-        ((width, width), (width, hidden_width), (hidden_width, width)),
-        (width, width, width, width, hidden_width),
-    )
-    g_top, g_own, g_halo, keep, send = back(
-        info, tokens4, halo, q, k, v, p, do, dx, attend_blocks, columns
-    )
-    (dw_qkv,), (dg_one, db_one, db_qv) = scatter_sums(
-        keep, send, ((width, 3 * width),), (width, width, 2 * width)
-    )
-
-    def assemble(top, own, back_rows):
-        returned = from_behind(back_rows, "rows", 1)
-        return jnp.stack([returned, top[0], own, top[1]], axis=1).reshape(tokens.shape)
-
+    m_back = from_behind(m_halo, "rows", 1)
+    states = (info, tokens4, halo, q, k, v, p, do, dx, attend_blocks, columns)
+    shapes_b = ((width, width), (width, hidden_width), (hidden_width, width))
+    shapes_a = ((width, 3 * width),)
+    if is_cube():
+        shards = lax.axis_size("dp") * lax.axis_size("rows")
+        cores_b = sum_cores(keep, send)
+        before = back(*states, (), frames, 2, False)
+        *before, cores_b, m_back = lax.optimization_barrier((*before, cores_b, m_back))
+        plane_b = sum_plane(*cores_b)
+        before = back(*states, before, frames + 2, frames, False)
+        g_back = from_behind(before[1], "rows", 1)
+        g_out, keep, send = back(*states, before, 2, frames - 2, True)
+        plane_b, send = lax.optimization_barrier((plane_b, send))
+        cores_a = sum_cores(keep, send)
+        sums_b, flat_b = own_rows(sum_line(*plane_b), shapes_b, shards)
+        cores_a, g_back = lax.optimization_barrier((cores_a, g_back))
+        sums_a, flat_a = own_rows(sum_line(*sum_plane(*cores_a)), shapes_a, shards)
+    else:
+        sums_b, flat_b = scatter_sums(keep, send, shapes_b)
+        before = back(*states, (), frames, frames, False)
+        g_back = from_behind(before[1], "rows", 1)
+        g_out, keep, send = back(*states, before, 0, frames, True)
+        sums_a, flat_a = scatter_sums(keep, send, shapes_a)
+    dw_proj, dw_up, dw_down = sums_b
+    db_proj, dg_two, db_two, db_down, db_up = own_vectors(
+        flat_b, (width, width, width, width, hidden_width)
+    )
+    (dw_qkv,) = sums_a
+    dg_one, db_one, db_qv = own_vectors(flat_a, (width, width, 2 * width))
     return (
-        assemble(m_top, m_own, m_halo),
-        assemble(g_top, g_own, g_halo),
+        m_out.at[:, 0].set(m_back).reshape(tokens.shape),
+        g_out.at[:, 0].set(g_back).reshape(tokens.shape),
         dg_one, db_one, dw_qkv, db_qv, dw_proj, db_proj, dg_two, db_two, dw_up, db_up, dw_down, db_down,
     )
 

time: 400 us -> 294 us (0.73); the launches traced: 394 us -> 294 us
  Pallas kernels: 230 us -> 178 us
  waiting for transfers between devices: 90.9 us -> 59 us
  local copies, waits for them, and re-layouts: 27.3 us -> 17.1 us
  starting transfers between devices: 38.5 us -> 32.7 us
    pallas_call x2, Pallas kernels: 67.9 us -> 26.2 us  [attend(): pl.pallas_call(functools.partial(attend_kernel, frames, columns, height,...]
    ppermute x24, waiting for transfers between devices: 63.2 us -> 50.4 us  [flipped(): return lax.ppermute(x, axis, flip_perm(axis, bits))]
    ppermute x4, waiting for transfers between devices: 10.1 us -> 0.01 us  [from_behind(): lax.ppermute(x, axis, [(i, (i + by) % devices) for i in range(devices)])]
    ppermute x4, waiting for transfers between devices: 17.6 us -> 8.66 us  [flipped_both(): return lax.ppermute(x, AXES, pairs)]
    dynamic_update_slice x8 -> x0, local copies, waits for them, and re-layouts: 6.76 us -> none  [spread(): parts.append(lax.dynamic_update_slice(zeros, shard, (index * count,)))]
    another operation x10 -> x0, local copies, waits for them, and re-layouts: 6.6 us -> none  [the longest x4 6.58 us: assemble(): jnp.stack([returned, top[0], own, top[1]], axis=1).reshape(tokens.shape)]
    pallas_call x1, Pallas kernels: 87.9 us -> 82.6 us  [middle(): pl.pallas_call(functools.partial(middle_kernel, frames, columns, chunk),...]
    pallas_call x1 -> x8, Pallas kernels: 74.3 us -> 69.3 us  [the longest x3 58.5 us: back(): pl.pallas_call(functools.partial(back_kernel, frames, columns, first, cou...]
  transfers between devices with their start and end apart: 32 -> 32, of which waited for: 14 -> 18; matrix products, arithmetic and copies ran while one was open for 6% -> 4% of each run, Pallas kernels for 17% -> 31%
where the time goes in v3:
time: 294 us
  Pallas kernels  178 us (61%)
  waiting for transfers between devices  59 us (20%)
  starting transfers between devices  32.7 us (11%)
  local copies, waits for them, and re-layouts  17.1 us (6%)
  other arithmetic  5.73 us (2%)
    pallas_call x1, Pallas kernels, middle(): pl.pallas_call(functools.partial(middle_kernel, frames, columns, chunk),...  82.6 us
    pallas_call x3, Pallas kernels, back(): pl.pallas_call(functools.partial(back_kernel, frames, columns, first, cou...  58.5 us
    ppermute x24, waiting for transfers between devices, flipped(): return lax.ppermute(x, axis, flip_perm(axis, bits))  50.4 us
    pallas_call x2, Pallas kernels, attend(): pl.pallas_call(functools.partial(attend_kernel, frames, columns, height,...  26.2 us
    ppermute x24, starting transfers between devices, flipped(): return lax.ppermute(x, axis, flip_perm(axis, bits))  24.6 us
    pallas_call x4, Pallas kernels, join(): pl.pallas_call(join_kernel, out_shape=jax.ShapeDtypeStruct(shape, parts[0...  9.04 us
    ppermute x4, waiting for transfers between devices, flipped_both(): return lax.ppermute(x, AXES, pairs)  8.66 us
    ppermute x4, starting transfers between devices, flipped_both(): return lax.ppermute(x, AXES, pairs)  7.31 us
  transfers between devices with their start and end apart: 32, of which 18 were waited for; matrix products, arithmetic and copies ran while one was open for 4% of the time, Pallas kernels for 31%

profile of v3, /device:TPU:0, one launch (start us, length us, event | category | flops | bytes accessed | tf_op | source)
XLA Modules:
  0.0 293.6 jit_solution(6092732660523948754)
XLA Ops:
  0.7 1.8 pack.1
  2.5 5.0 %collective-permute-start.2 = (bf16[16,1664]{1,0:T(8,128)(2,1)}, bf16[16,1664]{1,0:T(8,128)(2,1)S(1)}, u32[]{:S(2)}, u32[]{:S(2)}) collective-permute-start(bf16[16,1664]{1,0:T(8,128)(2,1)} %get-tuple-element.87), channel_id=1, source_target_pairs={{0,24},{4,28},{8,16},{12,20},{16,8},{20,12},{24,0},{28,4},{1,25},{... | collective-permute-start | bytes 159752 | tf_op jit(solution)/shard_map/ppermute | solution.py:639
  8.2 1.9 collective-permute-done.2
  10.1 2.7 collective-permute-done.1
  13.4 1.6 join.4.refs_0_
  15.0 2.4 collective-permute-start.6
  18.5 1.3 slice_bitcast_fusion.1
  19.9 4.4 %collective-permute-done.6.refs_3_ = bf16[4,16,1664]{2,1,0:T(8,128)(2,1)S(1)} collective-permute-done((bf16[4,16,1664]{2,1,0:T(8,128)(2,1)}, bf16[4,16,1664]{2,1,0:T(8,128)(2,1)S(1)}, u32[]{:S(2)}, u32[]{:S(2)}) %collective-permute-start.6) | collective-permute-done | bytes 213024 | tf_op jit(solution)/shard_map/ppermute | solution.py:647
  24.3 2.5 collective-permute-done.5.refs_2_
  28.2 2.2 join.5.mine
  30.4 2.0 collective-permute-start.11
  32.5 2.3 collective-permute-start.9
  34.8 1.3 slice_bitcast_fusion
  36.7 2.5 collective-permute-done.11
  39.2 7.8 %collective-permute-done.10 = bf16[16,4864]{1,0:T(8,128)(2,1)S(1)} collective-permute-done((bf16[16,4864]{1,0:T(8,128)(2,1)S(1)}, bf16[16,4864]{1,0:T(8,128)(2,1)S(1)}, u32[]{:S(2)}, u32[]{:S(2)}) %collective-permute-start.10) | collective-permute-done | bytes 155680 | tf_op jit(solution)/shard_map/ppermute | solution.py:639
  47.7 2.0 join.6.refs_0_
  49.7 1.7 collective-permute-start.14
  51.4 1.2 collective-permute-start.13
  54.2 13.2 %attend.2 = (bf16[8,512,512]{2,1,0:T(8,128)(2,1)}, bf16[8,512,512]{2,1,0:T(8,128)(2,1)}, bf16[8,512,512]{2,1,0:T(8,128)(2,1)}, bf16[8,512,512]{2,1,0:T(8,128)(2,1)}, bf16[8,512,512]{2,1,0:T(8,128)(2,1)}) custom-call(s32[6]{0:T(128)} %pad_add_fusion.info, bf16[4,4,256,512]{3,2,1,0:T(8,128)(2,1)} %bitcast.56, bf16[4,4,256,512]{3,2,1,0:T(8,128)(2,1)} %bitcast.57, ...), custom_call_target="tpu_custom_call" | custom-call | flops 30000001024 | bytes 20000000 | tf_op jit(solution)/shard_map/attend/pallas_call | solution.py:516
  67.9 12.0 %collective-permute-done.13.refs_2_ = bf16[4,16,4864]{2,1,0:T(8,128)(2,1)} collective-permute-done((bf16[4,16,4864]{2,1,0:T(8,128)(2,1)}, bf16[4,16,4864]{2,1,0:T(8,128)(2,1)}, u32[]{:S(2)}, u32[]{:S(2)}) %collective-permute-start.13) | collective-permute-done | bytes 622624 | tf_op jit(solution)/shard_map/ppermute | solution.py:639
  80.0 3.2 %join.7.mine = bf16[16,16,4864]{2,1,0:T(8,128)(2,1)} custom-call(bf16[4,16,4864]{2,1,0:T(8,128)(2,1)} %join.6.refs_0_, bf16[4,16,4864]{2,1,0:T(8,128)(2,1)} %collective-permute-done.12.refs_1_, bf16[4,16,4864]{2,1,0:T(8,128)(2,1)} %collective-permute-done.13.refs_2_, bf16[4,16,4864]{2,1,0:T(8,128)(2,1)} %collective-permute-done.14.refs_3_), custom_call_target="tpu_custom_call" | custom-call | tf_op jit(solution)/shard_map/join/pallas_call | solution.py:424
  83.2 13.1 %attend.3 = (bf16[8,512,512]{2,1,0:T(8,128)(2,1)}, bf16[8,512,512]{2,1,0:T(8,128)(2,1)}, bf16[8,512,512]{2,1,0:T(8,128)(2,1)}, bf16[8,512,512]{2,1,0:T(8,128)(2,1)}, bf16[8,512,512]{2,1,0:T(8,128)(2,1)}) custom-call(s32[6]{0:T(128)} %pad_add_fusion.info, ...), custom_call_target="tpu_custom_call", output_to_operand_aliasing={{0}: (6, {}), {1}: (7, {}), {2}: (8, {}), {3}: (9, {}), {4}... | custom-call | flops 30000001024 | bytes 20000000 | tf_op jit(solution)/shard_map/attend/pallas_call | solution.py:516
  96.3 1.4 copy-done.15
  97.8 82.6 %middle.1 = (bf16[4,4,256,512]{3,2,1,0:T(8,128)(2,1)}, bf16[4,256,512]{2,1,0:T(8,128)(2,1)}, f32[8,512,512]{2,1,0:T(8,128)}, bf16[8,512,512]{2,1,0:T(8,128)(2,1)...) custom-call(s32[6]{0:T(128)} %pad_add_fusion.info, bf16[4,4,256,512]{3,2,1,0:T(8,128)(2,1)} %bitcast.60, ...), custom_call_target="tpu_custom_call" | custom-call | flops 89999998976 | bytes 40000000 | tf_op jit(solution)/shard_map/middle/pallas_call | solution.py:544
  181.0 16.1 %back.3 = (bf16[4,4,256,512]{3,2,1,0:T(8,128)(2,1)}, bf16[4,256,512]{2,1,0:T(8,128)(2,1)}, f32[512,1536]{1,0:T(8,128)}, f32[8,1536]{1,0:T(8,128)}) custom-call(s32[6]{0:T(128)} %pad_add_fusion.info, bf16[4,4,256,512]{3,2,1,0:T(8,128)(2,1)} %bitcast.62, bf16[4,4,256,512]{3,2,1,0:T(8,128)(2,1)} %bitcast.63, bf16[4,256,512]{2,1,0:T(8,128)(2,1)} %copy-done.2, ...), custom_call_target="tpu_custom_call" | custom-call | flops 12000000000 | bytes 10000000 | tf_op jit(solution)/shard_map/back/pallas_call | solution.py:598
  197.1 2.3 convert_add_fusion
  199.7 1.5 fusion.4
  201.1 1.1 copy-done
  202.2 1.4 collective-permute-start.18
  203.6 1.5 collective-permute-start.20
  205.7 25.4 %back.4 = (bf16[4,4,256,512]{3,2,1,0:T(8,128)(2,1)}, bf16[4,256,512]{2,1,0:T(8,128)(2,1)}, f32[512,1536]{1,0:T(8,128)}, f32[8,1536]{1,0:T(8,128)}) custom-call(s32[6]{0:T(128)} %pad_add_fusion.info, bf16[4,4,256,512]{3,2,1,0:T(8,128)(2,1)} %bitcast.64, bf16[4,4,256,512]{3,2,1,0:T(8,128)(2,1)} %bitcast.65, ...), custom_call_target="tpu_custom_call", output_to_operand_aliasing={{0}: (12, {}), {1}: (13, {})} | custom-call | flops 24000000000 | bytes 20000000 | tf_op jit(solution)/shard_map/back/pallas_call | solution.py:598
  231.8 17.0 %back.5 = (bf16[4,4,256,512]{3,2,1,0:T(8,128)(2,1)}, bf16[16,16,1664]{2,1,0:T(8,128)(2,1)}, bf16[16,16,1664]{2,1,0:T(8,128)(2,1)}) custom-call(s32[6]{0:T(128)} %pad_add_fusion.info, bf16[4,4,256,512]{3,2,1,0:T(8,128)(2,1)} %bitcast.66, bf16[4,4,256,512]{3,2,1,0:T(8,128)(2,1)} %bitcast.67, ...), custom_call_target="tpu_custom_call", output_to_operand_aliasing={{0}: (12, {})} | custom-call | flops 12000000000 | bytes 10000000 | tf_op jit(solution)/shard_map/back/pallas_call | solution.py:598
  248.8 1.8 convert_add_fusion.2
  250.8 2.0 collective-permute-start.31
  252.9 1.5 collective-permute-start.30
  254.3 1.0 bitcast_dynamic-update-slice_fusion
  255.4 2.5 collective-permute-done.29
  257.9 3.0 %collective-permute-done.31 = bf16[16,4864]{1,0:T(8,128)(2,1)S(1)} collective-permute-done((bf16[16,4864]{1,0:T(8,128)(2,1)S(1)}, bf16[16,4864]{1,0:T(8,128)(2,1)S(1)}, u32[]{:S(2)}, u32[]{:S(2)}) %collective-permute-start.31) | collective-permute-done | bytes 155680 | tf_op jit(solution)/shard_map/ppermute | solution.py:639
  260.9 8.0 %collective-permute-done.30 = bf16[16,4864]{1,0:T(8,128)(2,1)S(1)} collective-permute-done((bf16[16,4864]{1,0:T(8,128)(2,1)S(1)}, bf16[16,4864]{1,0:T(8,128)(2,1)S(1)}, u32[]{:S(2)}, u32[]{:S(2)}) %collective-permute-start.30) | collective-permute-done | bytes 155680 | tf_op jit(solution)/shard_map/ppermute | solution.py:639
  271.9 1.6 collective-permute-start.25
  273.5 1.2 collective-permute-start.24
  276.0 3.4 %collective-permute-done.23 = bf16[4,16,1664]{2,1,0:T(8,128)(2,1)S(1)} collective-permute-done((bf16[4,16,1664]{2,1,0:T(8,128)(2,1)S(1)}, bf16[4,16,1664]{2,1,0:T(8,128)(2,1)S(1)}, u32[]{:S(2)}, u32[]{:S(2)}) %collective-permute-start.23) | collective-permute-done | bytes 213024 | tf_op jit(solution)/shard_map/ppermute | solution.py:639
  279.4 3.7 %collective-permute-done.25 = bf16[4,16,1664]{2,1,0:T(8,128)(2,1)S(1)} collective-permute-done((bf16[4,16,1664]{2,1,0:T(8,128)(2,1)S(1)}, bf16[4,16,1664]{2,1,0:T(8,128)(2,1)S(1)}, u32[]{:S(2)}, u32[]{:S(2)}) %collective-permute-start.25) | collective-permute-done | bytes 213024 | tf_op jit(solution)/shard_map/ppermute | solution.py:647
  283.1 1.4 collective-permute-done.24
  284.7 2.0 collective-permute-start.28
  286.7 1.4 collective-permute-start.27
  288.2 1.0 bitcast_dynamic-update-slice_fusion.1
  289.2 1.6 collective-permute-done.28
  (94 shorter events, 16.9 us)
Async XLA Ops:
  0.7 35.5 %copy-start.14 = (s32[4]{0:T(128)S(1)}, s32[4]{0:T(128)}, u32[]{:S(2)}) copy-start(s32[4]{0:T(128)} %param.20) | copy-start | bytes 52
  2.5 27.9 %copy-start.7 = (bf16[16,4864]{1,0:T(8,128)(2,1)S(1)}, bf16[16,4864]{1,0:T(8,128)(2,1)}, u32[]{:S(2)}) copy-start(bf16[16,4864]{1,0:T(8,128)(2,1)} %get-tuple-element.97) | copy-start | bytes 466948
  2.5 7.6 %collective-permute-start.2 = (bf16[16,1664]{1,0:T(8,128)(2,1)}, bf16[16,1664]{1,0:T(8,128)(2,1)S(1)}, u32[]{:S(2)}, u32[]{:S(2)}) collective-permute-start(bf16[16,1664]{1,0:T(8,128)(2,1)} %get-tuple-element.87), channel_id=1, source_target_pairs={{0,24},{4,28},{8,16},{12,20},{16,8},{20,12},{24,0},{28,4},{1,25},{... | collective-permute-start | bytes 159752 | tf_op jit(solution)/shard_map/ppermute | solution.py:639
  7.5 5.2 %collective-permute-start.1 = (bf16[16,1664]{1,0:T(8,128)(2,1)}, bf16[16,1664]{1,0:T(8,128)(2,1)S(1)}, u32[]{:S(2)}, u32[]{:S(2)}) collective-permute-start(bf16[16,1664]{1,0:T(8,128)(2,1)} %get-tuple-element.87), channel_id=1, source_target_pairs={{0,16},{4,20},{8,24},{12,28},{16,0},{20,4},{24,8},{28,12},{1,17},{... | collective-permute-start | bytes 159752 | tf_op jit(solution)/shard_map/ppermute | solution.py:639
  7.5 5.2 %collective-permute-start = (bf16[16,1664]{1,0:T(8,128)(2,1)}, bf16[16,1664]{1,0:T(8,128)(2,1)S(1)}, u32[]{:S(2)}, u32[]{:S(2)}) collective-permute-start(bf16[16,1664]{1,0:T(8,128)(2,1)} %get-tuple-element.87), channel_id=1, source_target_pairs={{0,8},{4,12},{8,0},{12,4},{16,24},{20,28},{24,16},{28,20},{1,9},{5... | collective-permute-start | bytes 159752 | tf_op jit(solution)/shard_map/ppermute | solution.py:639
  10.1 2.7 copy-start.11
  15.0 9.3 %collective-permute-start.6 = (bf16[4,16,1664]{2,1,0:T(8,128)(2,1)}, bf16[4,16,1664]{2,1,0:T(8,128)(2,1)S(1)}, u32[]{:S(2)}, u32[]{:S(2)}) collective-permute-start(bf16[4,16,1664]{2,1,0:T(8,128)(2,1)} %join.4.refs_0_), channel_id=1, source_target_pairs={{0,6},{1,7},{2,4},{3,5},{4,2},{5,3},{6,0},{7,1},{8,14},{9,15},{10,... | collective-permute-start | bytes 638984 | tf_op jit(solution)/shard_map/ppermute | solution.py:647
  17.4 9.4 %collective-permute-start.5 = (bf16[4,16,1664]{2,1,0:T(8,128)(2,1)}, bf16[4,16,1664]{2,1,0:T(8,128)(2,1)S(1)}, u32[]{:S(2)}, u32[]{:S(2)}) collective-permute-start(bf16[4,16,1664]{2,1,0:T(8,128)(2,1)} %join.4.refs_0_), channel_id=1, source_target_pairs={{0,4},{4,0},{8,12},{12,8},{16,20},{20,16},{24,28},{28,24},{1,5},{5... | collective-permute-start | bytes 638984 | tf_op jit(solution)/shard_map/ppermute | solution.py:639
  18.0 9.0 %collective-permute-start.4 = (bf16[4,16,1664]{2,1,0:T(8,128)(2,1)}, bf16[4,16,1664]{2,1,0:T(8,128)(2,1)S(1)}, u32[]{:S(2)}, u32[]{:S(2)}) collective-permute-start(bf16[4,16,1664]{2,1,0:T(8,128)(2,1)} %join.4.refs_0_), channel_id=1, source_target_pairs={{0,2},{1,3},{2,0},{3,1},{4,6},{5,7},{6,4},{7,5},{8,10},{9,11},{10,... | collective-permute-start | bytes 638984 | tf_op jit(solution)/shard_map/ppermute | solution.py:639
  19.8 33.4 %collective-permute-start.3 = (bf16[4,256,512]{2,1,0:T(8,128)(2,1)S(1)}, bf16[4,256,512]{2,1,0:T(8,128)(2,1)S(1)}, u32[]{:S(2)}, u32[]{:S(2)}) collective-permute-start(bf16[4,256,512]{2,1,0:T(8,128)(2,1)S(1)} %slice_bitcast_fusion.1), channel_id=1, source_target_pairs={{0,3},{1,0},{2,1},{3,2},{4,7},{5,4},{6,5},{7,6},{8,11},{9,8},{10,9... | collective-permute-start | bytes 3145736 | tf_op jit(solution)/shard_map/ppermute | solution.py:27
  24.3 2.6 copy-start.4
  26.8 0.7 copy-start.5
  27.5 0.7 copy-start.6
  30.4 22.8 %collective-permute-start.8 = (bf16[16,16,1664]{2,1,0:T(8,128)(2,1)}, bf16[16,16,1664]{2,1,0:T(8,128)(2,1)}, u32[]{:S(2)}, u32[]{:S(2)}) collective-permute-start(bf16[16,16,1664]{2,1,0:T(8,128)(2,1)} %join.5.mine), channel_id=1, source_target_pairs={{0,1},{1,0},{2,3},{3,2},{4,5},{5,4},{6,7},{7,6},{8,9},{9,8},{10,11... | collective-permute-start | bytes 2555912 | tf_op jit(solution)/shard_map/ppermute | solution.py:639
  30.4 8.8 %collective-permute-start.11 = (bf16[16,4864]{1,0:T(8,128)(2,1)S(1)}, bf16[16,4864]{1,0:T(8,128)(2,1)S(1)}, u32[]{:S(2)}, u32[]{:S(2)}) collective-permute-start(bf16[16,4864]{1,0:T(8,128)(2,1)S(1)} %copy-done.7), channel_id=1, source_target_pairs={{0,24},{4,28},{8,16},{12,20},{16,8},{20,12},{24,0},{28,4},{1,25},{... | collective-permute-start | bytes 466952 | tf_op jit(solution)/shard_map/ppermute | solution.py:639
  32.4 14.6 %collective-permute-start.10 = (bf16[16,4864]{1,0:T(8,128)(2,1)S(1)}, bf16[16,4864]{1,0:T(8,128)(2,1)S(1)}, u32[]{:S(2)}, u32[]{:S(2)}) collective-permute-start(bf16[16,4864]{1,0:T(8,128)(2,1)S(1)} %copy-done.7), channel_id=1, source_target_pairs={{0,16},{4,20},{8,24},{12,28},{16,0},{20,4},{24,8},{28,12},{1,17},{... | collective-permute-start | bytes 466952 | tf_op jit(solution)/shard_map/ppermute | solution.py:639
  32.5 14.4 %collective-permute-start.9 = (bf16[16,4864]{1,0:T(8,128)(2,1)S(1)}, bf16[16,4864]{1,0:T(8,128)(2,1)S(1)}, u32[]{:S(2)}, u32[]{:S(2)}) collective-permute-start(bf16[16,4864]{1,0:T(8,128)(2,1)S(1)} %copy-done.7), channel_id=1, source_target_pairs={{0,8},{4,12},{8,0},{12,4},{16,24},{20,28},{24,16},{28,20},{1,9},{5... | collective-permute-start | bytes 466952 | tf_op jit(solution)/shard_map/ppermute | solution.py:639
  39.2 7.8 %copy-start.8 = (bf16[16,4864]{1,0:T(8,128)(2,1)}, bf16[16,4864]{1,0:T(8,128)(2,1)S(1)}, u32[]{:S(2)}) copy-start(bf16[16,4864]{1,0:T(8,128)(2,1)S(1)} %collective-permute-done.11) | copy-start | bytes 466948
  47.0 0.7 copy-start.9
  47.0 0.7 copy-start.10
  49.7 18.2 %collective-permute-start.14 = (bf16[4,16,4864]{2,1,0:T(8,128)(2,1)}, bf16[4,16,4864]{2,1,0:T(8,128)(2,1)}, u32[]{:S(2)}, u32[]{:S(2)}) collective-permute-start(bf16[4,16,4864]{2,1,0:T(8,128)(2,1)} %join.6.refs_0_), channel_id=1, source_target_pairs={{0,6},{1,7},{2,4},{3,5},{4,2},{5,3},{6,0},{7,1},{8,14},{9,15},{10,... | collective-permute-start | bytes 1867784 | tf_op jit(solution)/shard_map/ppermute | solution.py:647
  51.4 28.5 %collective-permute-start.13 = (bf16[4,16,4864]{2,1,0:T(8,128)(2,1)}, bf16[4,16,4864]{2,1,0:T(8,128)(2,1)}, u32[]{:S(2)}, u32[]{:S(2)}) collective-permute-start(bf16[4,16,4864]{2,1,0:T(8,128)(2,1)} %join.6.refs_0_), channel_id=1, source_target_pairs={{0,4},{4,0},{8,12},{12,8},{16,20},{20,16},{24,28},{28,24},{1,5},{5... | collective-permute-start | bytes 1867784 | tf_op jit(solution)/shard_map/ppermute | solution.py:639
  52.6 27.4 %collective-permute-start.12 = (bf16[4,16,4864]{2,1,0:T(8,128)(2,1)}, bf16[4,16,4864]{2,1,0:T(8,128)(2,1)}, u32[]{:S(2)}, u32[]{:S(2)}) collective-permute-start(bf16[4,16,4864]{2,1,0:T(8,128)(2,1)} %join.6.refs_0_), channel_id=1, source_target_pairs={{0,2},{1,3},{2,0},{3,1},{4,6},{5,7},{6,4},{7,5},{8,10},{9,11},{10,... | collective-permute-start | bytes 1867784 | tf_op jit(solution)/shard_map/ppermute | solution.py:639
  53.2 1.0 copy-start.2
  53.2 43.1 %collective-permute-start.7 = (bf16[4,256,512]{2,1,0:T(8,128)(2,1)S(1)}, bf16[4,256,512]{2,1,0:T(8,128)(2,1)}, u32[]{:S(2)}, u32[]{:S(2)}) collective-permute-start(bf16[4,256,512]{2,1,0:T(8,128)(2,1)S(1)} %slice_bitcast_fusion), channel_id=1, source_target_pairs={{0,3},{1,0},{2,1},{3,2},{4,7},{5,4},{6,5},{7,6},{8,11},{9,8},{10,9... | collective-permute-start | bytes 3145736 | tf_op jit(solution)/shard_map/ppermute | solution.py:27
  83.2 13.1 %collective-permute-start.15 = (bf16[16,16,4864]{2,1,0:T(8,128)(2,1)}, bf16[16,16,4864]{2,1,0:T(8,128)(2,1)S(1)}, u32[]{:S(2)}, u32[]{:S(2)}) collective-permute-start(bf16[16,16,4864]{2,1,0:T(8,128)(2,1)} %join.7.mine), channel_id=1, source_target_pairs={{0,1},{1,0},{2,3},{3,2},{4,5},{5,4},{6,7},{7,6},{8,9},{9,8},{10,11... | collective-permute-start | bytes 7471112 | tf_op jit(solution)/shard_map/ppermute | solution.py:639
  96.3 1.4 copy-start.15
  180.3 16.7 %collective-permute-start.16 = (bf16[16,16,4864]{2,1,0:T(8,128)(2,1)}, bf16[16,16,4864]{2,1,0:T(8,128)(2,1)}, u32[]{:S(2)}, u32[]{:S(2)}) collective-permute-start(bf16[16,16,4864]{2,1,0:T(8,128)(2,1)} %get-tuple-element.114), channel_id=1, source_target_pairs={{0,1},{1,0},{2,3},{3,2},{4,5},{5,4},{6,7},{7,6},{8,9},{9,8},{10,11... | collective-permute-start | bytes 7471112 | tf_op jit(solution)/shard_map/ppermute | solution.py:639
  180.9 18.7 %collective-permute-start.17 = (bf16[4,256,512]{2,1,0:T(8,128)(2,1)}, bf16[4,256,512]{2,1,0:T(8,128)(2,1)S(1)}, u32[]{:S(2)}, u32[]{:S(2)}) collective-permute-start(bf16[4,256,512]{2,1,0:T(8,128)(2,1)} %get-tuple-element.115), channel_id=1, source_target_pairs={{0,1},{1,2},{2,3},{3,0},{4,5},{5,6},{6,7},{7,4},{8,9},{9,10},{10,1... | collective-permute-start | bytes 3145736 | tf_op jit(solution)/shard_map/ppermute | solution.py:27
  181.0 16.1 %copy-start.1 = (bf16[16,16,4864]{2,1,0:T(8,128)(2,1)S(1)}, bf16[16,16,4864]{2,1,0:T(8,128)(2,1)}, u32[]{:S(2)}) copy-start(bf16[16,16,4864]{2,1,0:T(8,128)(2,1)} %get-tuple-element.113) | copy-start | bytes 7471108
  199.4 2.8 copy-start
  202.2 46.6 %collective-permute-start.18 = (bf16[4,16,4864]{2,1,0:T(8,128)(2,1)}, bf16[4,16,4864]{2,1,0:T(8,128)(2,1)}, u32[]{:S(2)}, u32[]{:S(2)}) collective-permute-start(bf16[4,16,4864]{2,1,0:T(8,128)(2,1)} %get-tuple-element.138), channel_id=1, source_target_pairs={{0,2},{1,3},{2,0},{3,1},{4,6},{5,7},{6,4},{7,5},{8,10},{9,11},{10,... | collective-permute-start | bytes 1867784 | tf_op jit(solution)/shard_map/ppermute | solution.py:639
  203.6 45.2 %collective-permute-start.20 = (bf16[4,16,4864]{2,1,0:T(8,128)(2,1)}, bf16[4,16,4864]{2,1,0:T(8,128)(2,1)}, u32[]{:S(2)}, u32[]{:S(2)}) collective-permute-start(bf16[4,16,4864]{2,1,0:T(8,128)(2,1)} %get-tuple-element.139), channel_id=1, source_target_pairs={{0,6},{1,7},{2,4},{3,5},{4,2},{5,3},{6,0},{7,1},{8,14},{9,15},{10,... | collective-permute-start | bytes 1867784 | tf_op jit(solution)/shard_map/ppermute | solution.py:647
  205.1 43.7 %collective-permute-start.19 = (bf16[4,16,4864]{2,1,0:T(8,128)(2,1)}, bf16[4,16,4864]{2,1,0:T(8,128)(2,1)}, u32[]{:S(2)}, u32[]{:S(2)}) collective-permute-start(bf16[4,16,4864]{2,1,0:T(8,128)(2,1)} %get-tuple-element.140), channel_id=1, source_target_pairs={{0,4},{4,0},{8,12},{12,8},{16,20},{20,16},{24,28},{28,24},{1,5},{5... | collective-permute-start | bytes 1867784 | tf_op jit(solution)/shard_map/ppermute | solution.py:639
  231.2 40.0 %collective-permute-start.22 = (bf16[4,256,512]{2,1,0:T(8,128)(2,1)}, bf16[4,256,512]{2,1,0:T(8,128)(2,1)S(1)}, u32[]{:S(2)}, u32[]{:S(2)}) collective-permute-start(bf16[4,256,512]{2,1,0:T(8,128)(2,1)} %get-tuple-element.130), channel_id=1, source_target_pairs={{0,1},{1,2},{2,3},{3,0},{4,5},{5,6},{6,7},{7,4},{8,9},{9,10},{10,1... | collective-permute-start | bytes 3145736 | tf_op jit(solution)/shard_map/ppermute | solution.py:27
  231.8 17.0 %slice-start = ((f32[16,16,4864]{2,1,0:T(8,128)}), f32[4,16,4864]{2,1,0:T(8,128)S(1)}, s32[]{:S(2)}) async-start(f32[16,16,4864]{2,1,0:T(8,128)} %copy-done), calls=%async_computation | async-start | bytes 2490368 | tf_op jit(solution)/shard_map/slice | solution.py:702
  248.8 6.6 %copy-start.16 = (bf16[16,16,1664]{2,1,0:T(8,128)(2,1)S(1)}, bf16[16,16,1664]{2,1,0:T(8,128)(2,1)}, u32[]{:S(2)}) copy-start(bf16[16,16,1664]{2,1,0:T(8,128)(2,1)} %get-tuple-element.129) | copy-start | bytes 2555908
  250.6 20.2 %copy-start.3 = (bf16[16,16,1664]{2,1,0:T(8,128)(2,1)S(1)}, bf16[16,16,1664]{2,1,0:T(8,128)(2,1)}, u32[]{:S(2)}) copy-start(bf16[16,16,1664]{2,1,0:T(8,128)(2,1)} %get-tuple-element.125) | copy-start | bytes 2555908
  250.8 7.2 %collective-permute-start.29 = (bf16[16,4864]{1,0:T(8,128)(2,1)S(1)}, bf16[16,4864]{1,0:T(8,128)(2,1)S(1)}, u32[]{:S(2)}, u32[]{:S(2)}) collective-permute-start(bf16[16,4864]{1,0:T(8,128)(2,1)S(1)} %get-tuple-element.144), channel_id=1, source_target_pairs={{0,8},{4,12},{8,0},{12,4},{16,24},{20,28},{24,16},{28,20},{1,9},{5... | collective-permute-start | bytes 466952 | tf_op jit(solution)/shard_map/ppermute | solution.py:639
  250.8 10.0 %collective-permute-start.31 = (bf16[16,4864]{1,0:T(8,128)(2,1)S(1)}, bf16[16,4864]{1,0:T(8,128)(2,1)S(1)}, u32[]{:S(2)}, u32[]{:S(2)}) collective-permute-start(bf16[16,4864]{1,0:T(8,128)(2,1)S(1)} %get-tuple-element.145), channel_id=1, source_target_pairs={{0,24},{4,28},{8,16},{12,20},{16,8},{20,12},{24,0},{28,4},{1,25},{... | collective-permute-start | bytes 466952 | tf_op jit(solution)/shard_map/ppermute | solution.py:639
  252.9 16.0 %collective-permute-start.30 = (bf16[16,4864]{1,0:T(8,128)(2,1)S(1)}, bf16[16,4864]{1,0:T(8,128)(2,1)S(1)}, u32[]{:S(2)}, u32[]{:S(2)}) collective-permute-start(bf16[16,4864]{1,0:T(8,128)(2,1)S(1)} %get-tuple-element.146), channel_id=1, source_target_pairs={{0,16},{4,20},{8,24},{12,28},{16,0},{20,4},{24,8},{28,12},{1,17},{... | collective-permute-start | bytes 466952 | tf_op jit(solution)/shard_map/ppermute | solution.py:639
  255.4 15.5 %collective-permute-start.21 = (bf16[16,16,1664]{2,1,0:T(8,128)(2,1)S(1)}, bf16[16,16,1664]{2,1,0:T(8,128)(2,1)S(1)}, u32[]{:S(2)}, u32[]{:S(2)}) collective-permute-start(bf16[16,16,1664]{2,1,0:T(8,128)(2,1)S(1)} %copy-done.16), channel_id=1, source_target_pairs={{0,1},{1,0},{2,3},{3,2},{4,5},{5,4},{6,7},{7,6},{8,9},{9,8},{10,11... | collective-permute-start | bytes 2555912 | tf_op jit(solution)/shard_map/ppermute | solution.py:639
  271.2 8.2 %collective-permute-start.23 = (bf16[4,16,1664]{2,1,0:T(8,128)(2,1)S(1)}, bf16[4,16,1664]{2,1,0:T(8,128)(2,1)S(1)}, u32[]{:S(2)}, u32[]{:S(2)}) collective-permute-start(bf16[4,16,1664]{2,1,0:T(8,128)(2,1)S(1)} %get-tuple-element.141), channel_id=1, source_target_pairs={{0,2},{1,3},{2,0},{3,1},{4,6},{5,7},{6,4},{7,5},{8,10},{9,11},{10,... | collective-permute-start | bytes 638984 | tf_op jit(solution)/shard_map/ppermute | solution.py:639
  271.9 11.2 %collective-permute-start.25 = (bf16[4,16,1664]{2,1,0:T(8,128)(2,1)S(1)}, bf16[4,16,1664]{2,1,0:T(8,128)(2,1)S(1)}, u32[]{:S(2)}, u32[]{:S(2)}) collective-permute-start(bf16[4,16,1664]{2,1,0:T(8,128)(2,1)S(1)} %get-tuple-element.142), channel_id=1, source_target_pairs={{0,6},{1,7},{2,4},{3,5},{4,2},{5,3},{6,0},{7,1},{8,14},{9,15},{10,... | collective-permute-start | bytes 638984 | tf_op jit(solution)/shard_map/ppermute | solution.py:647
  273.5 11.0 %collective-permute-start.24 = (bf16[4,16,1664]{2,1,0:T(8,128)(2,1)S(1)}, bf16[4,16,1664]{2,1,0:T(8,128)(2,1)S(1)}, u32[]{:S(2)}, u32[]{:S(2)}) collective-permute-start(bf16[4,16,1664]{2,1,0:T(8,128)(2,1)S(1)} %get-tuple-element.143), channel_id=1, source_target_pairs={{0,4},{4,0},{8,12},{12,8},{16,20},{20,16},{24,28},{28,24},{1,5},{5... | collective-permute-start | bytes 638984 | tf_op jit(solution)/shard_map/ppermute | solution.py:639
  284.6 4.6 %collective-permute-start.26 = (bf16[16,1664]{1,0:T(8,128)(2,1)S(1)}, bf16[16,1664]{1,0:T(8,128)(2,1)S(1)}, u32[]{:S(2)}, u32[]{:S(2)}) collective-permute-start(bf16[16,1664]{1,0:T(8,128)(2,1)S(1)} %get-tuple-element.152), channel_id=1, source_target_pairs={{0,8},{4,12},{8,0},{12,4},{16,24},{20,28},{24,16},{28,20},{1,9},{5... | collective-permute-start | bytes 159752 | tf_op jit(solution)/shard_map/ppermute | solution.py:639
  284.7 6.1 %collective-permute-start.28 = (bf16[16,1664]{1,0:T(8,128)(2,1)S(1)}, bf16[16,1664]{1,0:T(8,128)(2,1)S(1)}, u32[]{:S(2)}, u32[]{:S(2)}) collective-permute-start(bf16[16,1664]{1,0:T(8,128)(2,1)S(1)} %get-tuple-element.153), channel_id=1, source_target_pairs={{0,24},{4,28},{8,16},{12,20},{16,8},{20,12},{24,0},{28,4},{1,25},{... | collective-permute-start | bytes 159752 | tf_op jit(solution)/shard_map/ppermute | solution.py:639
  286.7 5.0 %collective-permute-start.27 = (bf16[16,1664]{1,0:T(8,128)(2,1)S(1)}, bf16[16,1664]{1,0:T(8,128)(2,1)S(1)}, u32[]{:S(2)}, u32[]{:S(2)}) collective-permute-start(bf16[16,1664]{1,0:T(8,128)(2,1)S(1)} %get-tuple-element.154), channel_id=1, source_target_pairs={{0,16},{4,20},{8,24},{12,28},{16,0},{20,4},{24,8},{28,12},{1,17},{... | collective-permute-start | bytes 159752 | tf_op jit(solution)/shard_map/ppermute | solution.py:639
  (2 other events, 1.3 us)

commit v4 on v3

--- a/solution.py
+++ b/solution.py
@@ -106,37 +106,36 @@
     return jnp.where(bad > 0, -100.0, 0.0)
 
 
-def place(info, at, mine, theirs, targets, vec, sem, vec_sem):
-    copies = []
-    for core, source in enumerate((mine, theirs)):
-        for j in range(source.shape[0]):
-            block = info[at] ^ (bits_of(j) | core)
-            for lane, lanes, rows, target in targets:
-                for sub in range(rows // ROWS):
-                    row = pl.multiple_of(block * rows + sub * ROWS, ROWS)
-                    copies.append(
-                        pltpu.make_async_copy(
-                            source.at[j, :, pl.ds(lane + sub * lanes, lanes)],
-                            target.at[pl.ds(row, ROWS), :],
-                            sem,
-                        )
-                    )
-        lanes = vec.shape[-1]
-        blocks = source.shape[0]
-        copies.append(
-            pltpu.make_async_copy(
-                source.at[:, :, pl.ds(source.shape[-1] - lanes, lanes)],
-                vec.at[pl.ds(core * blocks, blocks)],
-                vec_sem,
-            )
-        )
-    for copy in copies:
-        copy.start()
-
-
-def wait_bytes(targets, sem):
-    for target in targets:
-        pltpu.make_async_copy(target, target, sem).wait()
+def place(info, at, pieces, targets, vec, vec_sem):
+    blocks = [
+        (source, k, core, i)
+        for core, sources in enumerate(pieces)
+        for i, (source, k) in enumerate((s, k) for s in sources for k in range(s.shape[0]))
+    ]
+    lanes = vec.shape[-1]
+    start = 0
+    for sources in pieces:
+        for source in sources:
+            count = source.shape[0]
+            tail = source.at[:, :, pl.ds(source.shape[-1] - lanes, lanes)]
+            pltpu.make_async_copy(tail, vec.at[pl.ds(start, count)], vec_sem).start()
+            start += count
+    for lane, lanes, rows, target, sem in targets:
+        for source, k, core, i in blocks:
+            block = info[at] ^ (bits_of(i) | core)
+            for sub in range(rows // ROWS):
+                row = pl.multiple_of(block * rows + sub * ROWS, ROWS)
+                pltpu.make_async_copy(
+                    source.at[k, :, pl.ds(lane + sub * lanes, lanes)], target.at[pl.ds(row, ROWS), :], sem
+                ).start()
+
+
+def halves(pieces):
+    return pieces[: len(pieces) // 2], pieces[len(pieces) // 2 :]
+
+
+def wait_bytes(target, sem):
+    pltpu.make_async_copy(target, target, sem).wait()
 
 
 def bits_of(j):
@@ -196,18 +195,20 @@
 
 
 def attend_kernel(
-    frames, columns, height, rows_here, first,
-    info, top, own, halo, mine, theirs, *rest,
+    frames, columns, height, rows_here,
+    info, top, own, halo, *rest,
 ):
     q_out, k_out, v_out, p_out, o_out, weight, vec, lines, sem = rest[-9:]
-    step = pl.program_id(0) + first
+    step = pl.program_id(0)
     width = top.shape[-1]
 
-    @pl.when(pl.program_id(0) == 0)
+    @pl.when(step == 0)
     def _():
-        place(info, frames + 1, mine, theirs, [(0, 3 * width, ROWS, weight)], vec, sem.at[0], sem.at[1])
-        wait_bytes([weight], sem.at[0])
-        wait_bytes([vec], sem.at[1])
+        place(
+            info, frames + 1, halves(rest[:-9]), [(0, 3 * width, ROWS, weight, sem.at[0])], vec, sem.at[1]
+        )
+        wait_bytes(weight, sem.at[0])
+        wait_bytes(vec, sem.at[1])
         pieces = natural_rows(vec)
         per = width // LANE
         for line in range(lines.shape[0]):
@@ -239,11 +240,13 @@
 
 def middle_kernel(
     frames, columns, chunk,
-    info, top, own, halo, dtop, down, dhalo, o_in, mine, theirs,
-    m_out, m_halo, dx_out, do_out, keep, send,
-    w_proj, w_up, w_down, vec, lines, b_up, dw_proj, dw_up, dw_down_t, dw_down, small, g_s, du_s, held,
-    sem, out_sem,
+    info, top, own, halo, dtop, down, dhalo, o_in, *rest,
 ):
+    (
+        m_out, m_halo, dx_out, do_out, keep, send,
+        w_proj, w_up, w_down, vec, lines, b_up, dw_proj, dw_up, dw_down_t, dw_down, small, g_s, du_s, held,
+        sem, out_sem,
+    ) = rest[-22:]
     step = pl.program_id(0)
     width = top.shape[-1]
     hidden_width = w_up.shape[-1]
@@ -252,18 +255,19 @@
     @pl.when(step == 0)
     def _():
         targets = [
-            (0, width, ROWS, w_proj),
-            (width, hidden_width, ROWS, w_up),
-            (width + hidden_width, width, w_down.shape[0] // 32, w_down),
+            (0, width, ROWS, w_proj, sem.at[0]),
+            (width, hidden_width, ROWS, w_up, sem.at[1]),
+            (width + hidden_width, width, w_down.shape[0] // 32, w_down, sem.at[2]),
         ]
-        place(info, frames + 1, mine, theirs, targets, vec, sem.at[0], sem.at[1])
-        wait_bytes([w_proj, w_up, w_down], sem.at[0])
-        wait_bytes([vec], sem.at[1])
+        place(info, frames + 1, halves(rest[:-22]), targets, vec, sem.at[3])
+        wait_bytes(vec, sem.at[3])
         pieces = natural_rows(vec)
         per = width // pieces[0].shape[-1]
         for line in range(4):
             lines[line : line + 1, :] = jnp.concatenate(pieces[line * per : (line + 1) * per], axis=1)
         b_up[...] = jnp.concatenate(pieces[4 * per :], axis=1)
+        for target, copied in ((w_proj, sem.at[0]), (w_up, sem.at[1]), (w_down, sem.at[2])):
+            wait_bytes(target, copied)
         dw_proj[...] = jnp.zeros_like(dw_proj)
         dw_up[...] = jnp.zeros_like(dw_up)
         dw_down_t[...] = jnp.zeros_like(dw_down_t)
@@ -334,13 +338,17 @@
 
 
 def back_kernel(
-    frames, columns, first, count, with_halo, starts, ends,
-    info, top, own, halo, q_in, k_in, v_in, p_in, do_in, dx_in, mine, theirs, *rest,
+    frames, columns, first, count, with_halo, n_blocks, n_before, ends,
+    info, top, own, halo, q_in, k_in, v_in, p_in, do_in, dx_in, *rest,
 ):
-    if not starts:
-        dw_before, small_before, *rest = rest[1 + with_halo :]
-    *outs, d_s, weight, vec, lines, held, sem, out_sem = rest
-    g_out, g_halo, dw, small = (outs[0], outs[1] if with_halo else None, outs[-2], outs[-1])
+    blocks, rest = rest[:n_blocks], rest[n_blocks:]
+    earlier = rest[1 + with_halo : n_before] if n_before else ()
+    *outs, d_s, weight, vec, lines, held, sem, out_sem = rest[n_before:]
+    g_out, g_halo = outs[0], outs[1] if with_halo else None
+    if ends:
+        keep, send, dw, small, *loaded = outs[1 + with_halo :]
+    else:
+        dw, small = outs[1 + with_halo :]
     local = pl.program_id(0)
     step = lax.rem(local + first, 2 * frames)
     width = top.shape[-1]
@@ -348,25 +356,14 @@
 
     @pl.when(local == 0)
     def _():
-        place(info, frames + 1, mine, theirs, [(0, 3 * width, ROWS, weight)], vec, sem.at[0], sem.at[1])
-        if starts:
-            dw[...] = jnp.zeros_like(dw)
-            small[...] = jnp.zeros_like(small)
-        else:
-            copies = [
-                pltpu.make_async_copy(dw_before, dw, sem.at[2]),
-                pltpu.make_async_copy(small_before, small, sem.at[3]),
-            ]
-            for copy in copies:
-                copy.start()
-            for copy in copies:
-                copy.wait()
-        wait_bytes([weight], sem.at[0])
-        wait_bytes([vec], sem.at[1])
-        pieces = natural_rows(vec)
-        per = width // LANE
-        for line in range(lines.shape[0]):
-            lines[line : line + 1, :] = jnp.concatenate(pieces[line * per : (line + 1) * per], axis=1)
+        place(
+            info, frames + 1, halves(blocks), [(0, 3 * width, ROWS, weight, sem.at[0])], vec, sem.at[1]
+        )
+        dw[...] = jnp.zeros_like(dw)
+        small[...] = jnp.zeros_like(small)
+        if ends:
+            for i, (source, target) in enumerate(zip(earlier, loaded)):
+                pltpu.make_async_copy(source, target, sem.at[2 + i]).start()
 
     items = [
         (slice(w * CELLS, (w + 1) * CELLS), g * LANES)
@@ -386,6 +383,16 @@
     for (r, at, _), dq, dk, dv in zip(items, dqs, dks, dvs):
         for part, grad in enumerate((dq, dk, dv)):
             d_s[r, part * width + at : part * width + at + LANES] = grad
+
+    @pl.when(local == 0)
+    def _():
+        wait_bytes(weight, sem.at[0])
+        wait_bytes(vec, sem.at[1])
+        pieces = natural_rows(vec)
+        per = width // LANE
+        for line in range(lines.shape[0]):
+            lines[line : line + 1, :] = jnp.concatenate(pieces[line * per : (line + 1) * per], axis=1)
+
     bottom = jnp.where(step < frames, own[...], halo[...])
     x = jnp.concatenate([top[...], bottom], axis=0).astype(F32)
     normed, inverse = normalize(to_window_order(x, columns))
@@ -401,10 +408,13 @@
     store_rows(g_out, g_halo, held, out_sem, local, count, step, frames, grad)
 
     if ends:
-        keep, send = outs[1 + with_halo : 3 + with_halo]
 
         @pl.when(local == count - 1)
         def _():
+            for i, target in enumerate(loaded):
+                wait_bytes(target, sem.at[2 + i])
+                total = dw if i % 2 == 0 else small
+                total[...] += target[...]
             pieces = [small[1:2, :width], small[2:3, :width], small[0:1, :width], small[0:1, 2 * width :]]
             flat = jnp.concatenate(pieces, axis=1)
             tail = jnp.concatenate([flat[:, i * LANE : (i + 1) * LANE] for i in range(ROWS)], axis=0)
@@ -480,7 +490,7 @@
     )(index, *vectors, qkv, proj, up, down)
 
 
-def grid_specs(frames, cells, width, first=0):
+def grid_specs(frames, cells, width, first=0, which=0):
     top = pl.BlockSpec(
         (None, None, cells, width),
         lambda s, *_: ((s + first) % frames, 1 + 2 * ((s + first) % (2 * frames) // frames), 0, 0),
@@ -490,7 +500,8 @@
         lambda s, *_: (jnp.minimum((s + first) % (2 * frames), frames - 1), 2, 0, 0),
     )
     halo = pl.BlockSpec(
-        (None, cells, width), lambda s, *_: (jnp.maximum((s + first) % (2 * frames) - frames, 0), 0, 0)
+        (None, None, cells, width),
+        lambda s, *_: (which, jnp.maximum((s + first) % (2 * frames) - frames, 0), 0, 0),
     )
     return [top, own, halo]
 
@@ -507,19 +518,18 @@
     return pltpu.CompilerParams(vmem_limit_bytes=VMEM_LIMIT, dimension_semantics=("arbitrary",))
 
 
-def attend(info, tokens4, halo, blocks, previous, first, height, columns):
+def attend(info, tokens4, halo, blocks, height, columns):
     frames, groups, cells, width = tokens4.shape
     steps, block = 2 * frames, 2 * cells
-    row = pl.BlockSpec((None, block, width), lambda s, *_: (s + first, 0, 0))
+    row = pl.BlockSpec((None, block, width), lambda s, *_: (s, 0, 0))
     shape = jax.ShapeDtypeStruct((steps, block, width), BF16)
-    held = 6
     return pl.pallas_call(
-        functools.partial(attend_kernel, frames, columns, height, groups * HALF, first),
+        functools.partial(attend_kernel, frames, columns, height, groups * HALF),
         out_shape=[shape] * 5,
         grid_spec=pltpu.PrefetchScalarGridSpec(
             num_scalar_prefetch=1,
-            grid=(frames,),
-            in_specs=grid_specs(frames, cells, width, first) + [ANYWHERE] * (2 + len(previous)),
+            grid=(steps,),
+            in_specs=grid_specs(frames, cells, width) + [ANYWHERE] * len(blocks),
             out_specs=[row] * 5,
             scratch_shapes=[
                 pltpu.VMEM((width, 3 * width), BF16),
@@ -528,24 +538,23 @@
                 pltpu.SemaphoreType.DMA((2,)),
             ],
         ),
-        input_output_aliases={held + i: i for i in range(len(previous))},
         compiler_params=params(),
-        cost_estimate=pl.CostEstimate(flops=3 * 10**10, bytes_accessed=2 * 10**7, transcendentals=10**6),
+        cost_estimate=pl.CostEstimate(flops=3 * 10**10, bytes_accessed=3 * 10**7, transcendentals=10**6),
         name="attend",
-    )(info, tokens4, tokens4, halo, *blocks, *previous)
-
-
-def middle(info, tokens4, halo, d4, dhalo, o, blocks, hidden_width, columns, chunk=256):
+    )(info, tokens4, tokens4, halo, *blocks)
+
+
+def middle(info, tokens4, halo, d4, o, blocks, hidden_width, columns, chunk=256):
     frames, groups, cells, width = tokens4.shape
     steps, block = 2 * frames, 2 * cells
     row = pl.BlockSpec((None, block, width), lambda s, *_: (s, 0, 0))
-    ins = grid_specs(frames, cells, width)
-    mine = blocks[0].shape
+    ins = grid_specs(frames, cells, width) + grid_specs(frames, cells, width, which=1)
+    mine = (16,) + blocks[0].shape[1:]
     return pl.pallas_call(
         functools.partial(middle_kernel, frames, columns, chunk),
         out_shape=[
             jax.ShapeDtypeStruct(tokens4.shape, BF16),
-            jax.ShapeDtypeStruct(halo.shape, BF16),
+            jax.ShapeDtypeStruct(halo.shape[1:], BF16),
             jax.ShapeDtypeStruct((steps, block, width), F32),
             jax.ShapeDtypeStruct((steps, block, width), BF16),
             jax.ShapeDtypeStruct(mine, BF16),
@@ -554,7 +563,7 @@
         grid_spec=pltpu.PrefetchScalarGridSpec(
             num_scalar_prefetch=1,
             grid=(steps,),
-            in_specs=ins + ins + [row, ANYWHERE, ANYWHERE],
+            in_specs=ins + [row] + [ANYWHERE] * len(blocks),
             out_specs=[ANYWHERE, ANYWHERE, row, row, whole_out(mine), whole_out(mine)],
             scratch_shapes=[
                 pltpu.VMEM((width, width), BF16),
@@ -571,33 +580,32 @@
                 pltpu.VMEM((block, hidden_width), BF16),
                 pltpu.VMEM((block, hidden_width), BF16),
                 pltpu.VMEM((2, block, width), BF16),
-                pltpu.SemaphoreType.DMA((2,)),
+                pltpu.SemaphoreType.DMA((4,)),
                 pltpu.SemaphoreType.DMA((2, 2)),
             ],
         ),
         compiler_params=params(),
         cost_estimate=pl.CostEstimate(flops=9 * 10**10, bytes_accessed=4 * 10**7, transcendentals=10**7),
         name="middle",
-    )(info, tokens4, tokens4, halo, d4, d4, dhalo, o, *blocks)
+    )(info, tokens4, tokens4, halo, d4, d4, halo, o, *blocks)
 
 
 def back(info, tokens4, halo, q, k, v, p, do, dx, blocks, columns, before, first, count, ends):
     frames, groups, cells, width = tokens4.shape
     steps, block = 2 * frames, 2 * cells
     row = pl.BlockSpec((None, block, width), lambda s, *_: ((s + first) % steps, 0, 0))
-    mine = blocks[0].shape
+    mine = (16,) + blocks[0].shape[1:]
     dw, small = (width, 3 * width), (8, 3 * width)
     handed = [jax.ShapeDtypeStruct(mine, BF16)] * 2
     sums = [jax.ShapeDtypeStruct(dw, F32), jax.ShapeDtypeStruct(small, F32)]
-    held = 12
+    in_vmem = [pltpu.VMEM(dw, F32), pltpu.VMEM(small, F32)]
+    held = 10 + len(blocks)
     with_halo = first + count > frames
-    g_shapes = [jax.ShapeDtypeStruct(tokens4.shape, BF16), jax.ShapeDtypeStruct(halo.shape, BF16)]
+    g_shapes = [jax.ShapeDtypeStruct(tokens4.shape, BF16), jax.ShapeDtypeStruct(halo.shape[1:], BF16)]
     g_shapes = g_shapes[: 1 + with_halo]
-    if before:
-        before = (before[0], *(before[1:2] if with_halo else ()), *before[-2:])
     return pl.pallas_call(
         functools.partial(
-            back_kernel, frames, columns, first, count, with_halo, not before, ends
+            back_kernel, frames, columns, first, count, with_halo, len(blocks), len(before), ends
         ),
         out_shape=g_shapes + (handed if ends else sums),
         grid_spec=pltpu.PrefetchScalarGridSpec(
@@ -605,17 +613,17 @@
             grid=(count,),
             in_specs=grid_specs(frames, cells, width, first)
             + [row] * 6
-            + [ANYWHERE] * (2 + len(before)),
+            + [ANYWHERE] * (len(blocks) + len(before)),
             out_specs=[ANYWHERE] * len(g_shapes)
             + ([whole_out(mine)] * 2 if ends else [whole_out(dw), whole_out(small)]),
-            scratch_shapes=([pltpu.VMEM(dw, F32), pltpu.VMEM(small, F32)] if ends else [])
+            scratch_shapes=(in_vmem * ((len(before) - len(g_shapes)) // 2 + 1) if ends else [])
             + [
                 pltpu.VMEM((block, 3 * width), BF16),
                 pltpu.VMEM((width, 3 * width), BF16),
                 pltpu.VMEM((32, ROWS, LANE), BF16),
                 pltpu.VMEM((4, width), F32),
                 pltpu.VMEM((2, block, width), BF16),
-                pltpu.SemaphoreType.DMA((4,)),
+                pltpu.SemaphoreType.DMA((8,)),
                 pltpu.SemaphoreType.DMA((2, 2)),
             ],
         ),
@@ -760,34 +768,28 @@
         )
         own_a, own_b = pack(me[None], vectors, qkv_weight, proj_weight, fc1_weight, fc2_weight)
         z_a = along_z(own_a)
-        own_b = after(own_b, *z_a)
-        z_b = along_z(own_b)
+        halo = from_behind(jnp.stack([tokens4[:, 0], d4[:, 0]]), "rows", -1)
         column_a = join(own_a[None], *(z[None] for z in z_a))
-        halo = from_behind(after(tokens4[:, 0], column_a), "rows", -1)
-        plane_a = over_plane(column_a)
-        mine_a = join(column_a, *plane_a)
-        attend_blocks = (mine_a, flipped(mine_a, "rows", 1))
+        z_b = along_z(after(own_b, *z_a))
+        mine_a = (column_a, *over_plane(column_a))
         column_b = join(own_b[None], *(z[None] for z in z_b))
-        column_b = after(column_b, mine_a)
-        plane_b = over_plane(column_b)
-        dhalo = from_behind(after(d4[:, 0], mine_a), "rows", -1)
+        *mine_a, column_b = lax.optimization_barrier((*mine_a, column_b))
+        attend_blocks = (*mine_a, *(flipped(piece, "rows", 1) for piece in mine_a))
+        mine_b = (column_b, *over_plane(column_b))
     else:
         me = jnp.int32(0)
         attend_blocks = gather_blocks((qkv_weight,), (ln1_gain, ln1_bias, qv_bias))
         middle_blocks = gather_blocks(
             (proj_weight, fc1_weight, fc2_weight), (proj_bias, ln2_gain, ln2_bias, fc2_bias, fc1_bias)
         )
-        halo = from_behind(tokens4[:, 0], "rows", -1)
-        dhalo = from_behind(d4[:, 0], "rows", -1)
+        halo = from_behind(jnp.stack([tokens4[:, 0], d4[:, 0]]), "rows", -1)
     info = jnp.concatenate([frame_level, jnp.stack([lax.axis_index("rows").astype(jnp.int32), me])])
-    early = attend(info, tokens4, halo, attend_blocks, (), 0, height, columns)
+    q, k, v, p, o = attend(info, tokens4, halo, attend_blocks, height, columns)
     if is_cube():
-        plane_b = lax.optimization_barrier((*plane_b, early[0]))[:3]
-        mine_b = join(column_b, *plane_b)
-        middle_blocks = (mine_b, flipped(mine_b, "rows", 1))
-    q, k, v, p, o = attend(info, tokens4, halo, attend_blocks, early, frames, height, columns)
+        *mine_b, o = lax.optimization_barrier((*mine_b, o))
+        middle_blocks = (*mine_b, *(flipped(piece, "rows", 1) for piece in mine_b))
     m_out, m_halo, dx, do, keep, send = middle(
-        info, tokens4, halo, d4, dhalo, o, middle_blocks, hidden_width, columns
+        info, tokens4, halo, d4, o, middle_blocks, hidden_width, columns
     )
     m_back = from_behind(m_halo, "rows", 1)
     states = (info, tokens4, halo, q, k, v, p, do, dx, attend_blocks, columns)
@@ -796,22 +798,24 @@
     if is_cube():
         shards = lax.axis_size("dp") * lax.axis_size("rows")
         cores_b = sum_cores(keep, send)
-        before = back(*states, (), frames, 2, False)
-        *before, cores_b, m_back = lax.optimization_barrier((*before, cores_b, m_back))
+        part_a = back(*states, (), frames, 2, False)
+        *part_a, cores_b, m_back = lax.optimization_barrier((*part_a, cores_b, m_back))
         plane_b = sum_plane(*cores_b)
-        before = back(*states, before, frames + 2, frames, False)
-        g_back = from_behind(before[1], "rows", 1)
-        g_out, keep, send = back(*states, before, 2, frames - 2, True)
+        part_b = back(*states, part_a[:2], frames + 2, frames, False)
+        g_back = from_behind(part_b[1], "rows", 1)
+        sums = (*part_a[2:], *part_b[2:])
+        g_out, keep, send = back(*states, (part_b[0], *sums), 2, frames - 2, True)
         plane_b, send = lax.optimization_barrier((plane_b, send))
-        cores_a = sum_cores(keep, send)
-        sums_b, flat_b = own_rows(sum_line(*plane_b), shapes_b, shards)
-        cores_a, g_back = lax.optimization_barrier((cores_a, g_back))
-        sums_a, flat_a = own_rows(sum_line(*sum_plane(*cores_a)), shapes_a, shards)
+        plane_a = sum_plane(*sum_cores(keep, send))
+        line_b = [flipped(plane_b[1][z - 1], "dp", 2 * z) for z in (1, 2, 3)]
+        line_b, plane_a = lax.optimization_barrier((line_b, plane_a))
+        sums_b, flat_b = own_rows(plane_b[0] + sum(wide(x) for x in line_b), shapes_b, shards)
+        sums_a, flat_a = own_rows(sum_line(*plane_a), shapes_a, shards)
     else:
         sums_b, flat_b = scatter_sums(keep, send, shapes_b)
         before = back(*states, (), frames, frames, False)
         g_back = from_behind(before[1], "rows", 1)
-        g_out, keep, send = back(*states, before, 0, frames, True)
+        g_out, keep, send = back(*states, (before[0], *before[2:]), 0, frames, True)
         sums_a, flat_a = scatter_sums(keep, send, shapes_a)
     dw_proj, dw_up, dw_down = sums_b
     db_proj, dg_two, db_two, db_down, db_up = own_vectors(

time: 294 us -> 261 us (0.89)
  waiting for transfers between devices: 59 us -> 33.2 us
  Pallas kernels: 178 us -> 166 us
  starting transfers between devices: 32.7 us -> 38 us
    ppermute x24 -> x30, waiting for transfers between devices: 50.4 us -> 31 us  [flipped(): return lax.ppermute(x, axis, flip_perm(axis, bits))]
    ppermute x4, waiting for transfers between devices: 8.66 us -> 2.14 us  [flipped_both(): return lax.ppermute(x, AXES, pairs)]
    pallas_call x4 -> x2, Pallas kernels: 9.04 us -> 3.6 us  [join(): pl.pallas_call(join_kernel, out_shape=jax.ShapeDtypeStruct(shape, parts[0...]
    pallas_call x2 -> x1, Pallas kernels: 26.2 us -> 22.4 us  [attend(): pl.pallas_call(functools.partial(attend_kernel, frames, columns, height,...]
    ppermute x24 -> x30, starting transfers between devices: 24.6 us -> 26.6 us  [flipped(): return lax.ppermute(x, axis, flip_perm(axis, bits))]
    unnamed x36 -> x50, local copies, waits for them, and re-layouts: 6.15 us -> 5.23 us
  transfers between devices with their start and end apart: 32 -> 37, of which waited for: 18 -> 18; matrix products, arithmetic and copies ran while one was open for 4% -> 4% of each run, Pallas kernels for 31% -> 32%
where the time goes in v4:
time: 261 us
  Pallas kernels  166 us (64%)
  starting transfers between devices  38 us (15%)
  waiting for transfers between devices  33.2 us (13%)
  local copies, waits for them, and re-layouts  15.2 us (6%)
  other arithmetic  7.35 us (3%)
    pallas_call x1, Pallas kernels, middle(): pl.pallas_call(functools.partial(middle_kernel, frames, columns, chunk),...  82.5 us
    pallas_call x3, Pallas kernels, back(): pl.pallas_call(functools.partial(back_kernel, frames, columns, first, cou...  55.5 us
    ppermute x30, waiting for transfers between devices, flipped(): return lax.ppermute(x, axis, flip_perm(axis, bits))  31 us
    ppermute x30, starting transfers between devices, flipped(): return lax.ppermute(x, axis, flip_perm(axis, bits))  26.6 us
    pallas_call x1, Pallas kernels, attend(): pl.pallas_call(functools.partial(attend_kernel, frames, columns, height,...  22.4 us
    ppermute x4, starting transfers between devices, flipped_both(): return lax.ppermute(x, AXES, pairs)  7.84 us
    unnamed x50, local copies, waits for them, and re-layouts  5.23 us
  transfers between devices with their start and end apart: 37, of which 18 were waited for; matrix products, arithmetic and copies ran while one was open for 4% of the time, Pallas kernels for 32%

profile of v4, /device:TPU:0, one launch (start us, length us, event | category | flops | bytes accessed | tf_op | source)
XLA Modules:
  0.0 260.6 jit_solution(14024856991968674329)
XLA Ops:
  0.6 1.8 slice_bitcast_fusion
  2.4 1.5 pad_maximum_fusion
  3.9 2.4 collective-permute-start
  6.3 1.8 pack.1
  8.1 3.6 %collective-permute-start.3 = (bf16[16,1664]{1,0:T(8,128)(2,1)}, bf16[16,1664]{1,0:T(8,128)(2,1)S(1)}, u32[]{:S(2)}, u32[]{:S(2)}) collective-permute-start(bf16[16,1664]{1,0:T(8,128)(2,1)} %get-tuple-element.88), channel_id=1, source_target_pairs={{0,24},{4,28},{8,16},{12,20},{16,8},{20,12},{24,0},{28,4},{1,25},{... | collective-permute-start | bytes 159752 | tf_op jit(solution)/shard_map/ppermute | solution.py:647
  12.5 2.4 collective-permute-done.3
  14.9 2.1 collective-permute-done.2
  17.0 2.1 collective-permute-start.9
  19.1 1.6 join.2.rest_0_
  20.7 2.4 collective-permute-start.6
  23.6 1.5 collective-permute-done.9
  25.1 1.8 collective-permute-start.4
  26.9 5.0 %collective-permute-done.8 = bf16[16,4864]{1,0:T(8,128)(2,1)S(1)} collective-permute-done((bf16[16,4864]{1,0:T(8,128)(2,1)}, bf16[16,4864]{1,0:T(8,128)(2,1)S(1)}, u32[]{:S(2)}, u32[]{:S(2)}) %collective-permute-start.8) | collective-permute-done | bytes 155680 | tf_op jit(solution)/shard_map/ppermute | solution.py:647
  31.9 0.9 collective-permute-start.7
  32.7 4.6 %collective-permute-done.7 = bf16[16,4864]{1,0:T(8,128)(2,1)S(1)} collective-permute-done((bf16[16,4864]{1,0:T(8,128)(2,1)}, bf16[16,4864]{1,0:T(8,128)(2,1)S(1)}, u32[]{:S(2)}, u32[]{:S(2)}) %collective-permute-start.7) | collective-permute-done | bytes 155680 | tf_op jit(solution)/shard_map/ppermute | solution.py:647
  38.0 2.0 join.3.rest_0_
  42.2 3.1 %collective-permute-start.12 = (bf16[4,16,4864]{2,1,0:T(8,128)(2,1)}, bf16[4,16,4864]{2,1,0:T(8,128)(2,1)}, u32[]{:S(2)}, u32[]{:S(2)}) collective-permute-start(bf16[4,16,4864]{2,1,0:T(8,128)(2,1)} %join.3.rest_0_), channel_id=1, source_target_pairs={{0,6},{1,7},{2,4},{3,5},{4,2},{5,3},{6,0},{7,1},{8,14},{9,15},{10,... | collective-permute-start | bytes 1867784 | tf_op jit(solution)/shard_map/ppermute | solution.py:655
  47.2 1.3 copy-done.2
  48.5 22.4 %attend.1 = (bf16[8,512,512]{2,1,0:T(8,128)(2,1)}, bf16[8,512,512]{2,1,0:T(8,128)(2,1)}, bf16[8,512,512]{2,1,0:T(8,128)(2,1)}, bf16[8,512,512]{2,1,0:T(8,128)(2,1)}, bf16[8,512,512]{2,1,0:T(8,128)(2,1)}) custom-call(s32[6]{0:T(128)} %pad_add_fusion.info, bf16[4,4,256,512]{3,2,1,0:T(8,128)(2,1)} %bitcast.50, bf16[4,4,256,512]{3,2,1,0:T(8,128)(2,1)} %bitcast.51, ...), custom_call_target="tpu_custom_call" | custom-call | flops 30000001024 | bytes 30000000 | tf_op jit(solution)/shard_map/attend/pallas_call | solution.py:526
  70.9 2.3 collective-permute-done.11.rest_2_
  74.2 1.2 collective-permute-done.17.rest_4_
  75.4 0.9 collective-permute-done.18.rest_5_
  76.4 0.9 collective-permute-done.19.rest_6_
  77.3 0.9 collective-permute-done.20.rest_7_
  78.2 0.9 copy-done.23
  79.0 82.5 %middle.1 = (bf16[4,4,256,512]{3,2,1,0:T(8,128)(2,1)}, bf16[4,256,512]{2,1,0:T(8,128)(2,1)}, f32[8,512,512]{2,1,0:T(8,128)}, bf16[8,512,512]{2,1,0:T(8,128)(2,1)...) custom-call(s32[6]{0:T(128)} %pad_add_fusion.info, bf16[4,4,256,512]{3,2,1,0:T(8,128)(2,1)} %bitcast.52, ...), custom_call_target="tpu_custom_call" | custom-call | flops 89999998976 | bytes 40000000 | tf_op jit(solution)/shard_map/middle/pallas_call | solution.py:553
  162.1 15.4 %back.3 = (bf16[4,4,256,512]{3,2,1,0:T(8,128)(2,1)}, bf16[4,256,512]{2,1,0:T(8,128)(2,1)}, f32[512,1536]{1,0:T(8,128)}, f32[8,1536]{1,0:T(8,128)}) custom-call(s32[6]{0:T(128)} %pad_add_fusion.info, bf16[4,4,256,512]{3,2,1,0:T(8,128)(2,1)} %bitcast.54, bf16[4,4,256,512]{3,2,1,0:T(8,128)(2,1)} %bitcast.55, bf16[2,4,256,512]{3,2,1,0:T(8,128)(2,1)} %copy-done.2, ...), custom_call_target="tpu_custom_call" | custom-call | flops 12000000000 | bytes 10000000 | tf_op jit(solution)/shard_map/back/pallas_call | solution.py:606
  177.5 2.3 convert_add_fusion
  180.1 1.5 fusion.3
  181.5 1.1 copy-done
  182.6 1.8 collective-permute-start.24
  185.2 0.9 collective-permute-start.25
  186.1 24.4 %back.4 = (bf16[4,4,256,512]{3,2,1,0:T(8,128)(2,1)}, bf16[4,256,512]{2,1,0:T(8,128)(2,1)}, f32[512,1536]{1,0:T(8,128)}, f32[8,1536]{1,0:T(8,128)}) custom-call(s32[6]{0:T(128)} %pad_add_fusion.info, bf16[4,4,256,512]{3,2,1,0:T(8,128)(2,1)} %bitcast.56, bf16[4,4,256,512]{3,2,1,0:T(8,128)(2,1)} %bitcast.57, ...), custom_call_target="tpu_custom_call", output_to_operand_aliasing={{0}: (18, {}), {1}: (19, {})} | custom-call | flops 24000000000 | bytes 20000000 | tf_op jit(solution)/shard_map/back/pallas_call | solution.py:606
  211.2 15.8 %back.5 = (bf16[4,4,256,512]{3,2,1,0:T(8,128)(2,1)}, bf16[16,16,1664]{2,1,0:T(8,128)(2,1)}, bf16[16,16,1664]{2,1,0:T(8,128)(2,1)}) custom-call(s32[6]{0:T(128)} %pad_add_fusion.info, bf16[4,4,256,512]{3,2,1,0:T(8,128)(2,1)} %bitcast.58, bf16[4,4,256,512]{3,2,1,0:T(8,128)(2,1)} %bitcast.59, ...), custom_call_target="tpu_custom_call", output_to_operand_aliasing={{0}: (18, {})} | custom-call | flops 12000000000 | bytes 10000000 | tf_op jit(solution)/shard_map/back/pallas_call | solution.py:606
  227.0 1.0 bitcast_dynamic-update-slice_fusion
  228.1 1.8 convert_add_fusion.2
  230.0 1.3 collective-permute-start.30
  231.3 3.0 %collective-permute-start.29 = (bf16[16,4864]{1,0:T(8,128)(2,1)S(1)}, bf16[16,4864]{1,0:T(8,128)(2,1)S(1)}, u32[]{:S(2)}, u32[]{:S(2)}) collective-permute-start(bf16[16,4864]{1,0:T(8,128)(2,1)S(1)} %get-tuple-element.146), channel_id=1, source_target_pairs={{0,24},{4,28},{8,16},{12,20},{16,8},{20,12},{24,0},{28,4},{1,25},{... | collective-permute-start | bytes 466952 | tf_op jit(solution)/shard_map/ppermute | solution.py:647
  235.3 1.7 collective-permute-start.33
  236.9 1.3 collective-permute-start.32
  238.2 1.0 bitcast_dynamic-update-slice_fusion.1
  239.2 3.6 %collective-permute-done.31 = bf16[4,16,1664]{2,1,0:T(8,128)(2,1)S(1)} collective-permute-done((bf16[4,16,1664]{2,1,0:T(8,128)(2,1)S(1)}, bf16[4,16,1664]{2,1,0:T(8,128)(2,1)S(1)}, u32[]{:S(2)}, u32[]{:S(2)}) %collective-permute-start.31) | collective-permute-done | bytes 213024 | tf_op jit(solution)/shard_map/ppermute | solution.py:647
  242.9 1.5 collective-permute-start.27
  244.3 2.1 collective-permute-done.33
  246.5 1.4 collective-permute-done.32
  248.0 1.7 collective-permute-done.27
  250.6 3.1 %collective-permute-start.36 = (bf16[16,1664]{1,0:T(8,128)(2,1)S(1)}, bf16[16,1664]{1,0:T(8,128)(2,1)S(1)}, u32[]{:S(2)}, u32[]{:S(2)}) collective-permute-start(bf16[16,1664]{1,0:T(8,128)(2,1)S(1)} %get-tuple-element.155), channel_id=1, source_target_pairs={{0,24},{4,28},{8,16},{12,20},{16,8},{20,12},{24,0},{28,4},{1,25},{... | collective-permute-start | bytes 159752 | tf_op jit(solution)/shard_map/ppermute | solution.py:647
  256.9 1.8 collective-permute-done.35
  (115 shorter events, 16.5 us)
Async XLA Ops:
  2.4 38.8 %copy-start.18 = (s32[4]{0:T(128)S(1)}, s32[4]{0:T(128)}, u32[]{:S(2)}) copy-start(s32[4]{0:T(128)} %param.20) | copy-start | bytes 52
  3.9 43.2 %collective-permute-start = (bf16[2,4,256,512]{3,2,1,0:T(8,128)(2,1)}, bf16[2,4,256,512]{3,2,1,0:T(8,128)(2,1)S(1)}, u32[]{:S(2)}, u32[]{:S(2)}) collective-permute-start(bf16[2,4,256,512]{3,2,1,0:T(8,128)(2,1)} %pad_maximum_fusion), channel_id=1, source_target_pairs={{0,3},{1,0},{2,1},{3,2},{4,7},{5,4},{6,5},{7,6},{8,11},{9,8},{10,9... | collective-permute-start | bytes 6291464 | tf_op jit(solution)/shard_map/ppermute | solution.py:27
  8.1 6.8 %collective-permute-start.3 = (bf16[16,1664]{1,0:T(8,128)(2,1)}, bf16[16,1664]{1,0:T(8,128)(2,1)S(1)}, u32[]{:S(2)}, u32[]{:S(2)}) collective-permute-start(bf16[16,1664]{1,0:T(8,128)(2,1)} %get-tuple-element.88), channel_id=1, source_target_pairs={{0,24},{4,28},{8,16},{12,20},{16,8},{20,12},{24,0},{28,4},{1,25},{... | collective-permute-start | bytes 159752 | tf_op jit(solution)/shard_map/ppermute | solution.py:647
  11.7 5.2 %collective-permute-start.2 = (bf16[16,1664]{1,0:T(8,128)(2,1)}, bf16[16,1664]{1,0:T(8,128)(2,1)S(1)}, u32[]{:S(2)}, u32[]{:S(2)}) collective-permute-start(bf16[16,1664]{1,0:T(8,128)(2,1)} %get-tuple-element.88), channel_id=1, source_target_pairs={{0,16},{4,20},{8,24},{12,28},{16,0},{20,4},{24,8},{28,12},{1,17},{... | collective-permute-start | bytes 159752 | tf_op jit(solution)/shard_map/ppermute | solution.py:647
  11.7 5.2 %collective-permute-start.1 = (bf16[16,1664]{1,0:T(8,128)(2,1)}, bf16[16,1664]{1,0:T(8,128)(2,1)S(1)}, u32[]{:S(2)}, u32[]{:S(2)}) collective-permute-start(bf16[16,1664]{1,0:T(8,128)(2,1)} %get-tuple-element.88), channel_id=1, source_target_pairs={{0,8},{4,12},{8,0},{12,4},{16,24},{20,28},{24,16},{28,20},{1,9},{5... | collective-permute-start | bytes 159752 | tf_op jit(solution)/shard_map/ppermute | solution.py:647
  17.0 8.1 %collective-permute-start.9 = (bf16[16,4864]{1,0:T(8,128)(2,1)}, bf16[16,4864]{1,0:T(8,128)(2,1)S(1)}, u32[]{:S(2)}, u32[]{:S(2)}) collective-permute-start(bf16[16,4864]{1,0:T(8,128)(2,1)} %get-tuple-element.90), channel_id=1, source_target_pairs={{0,24},{4,28},{8,16},{12,20},{16,8},{20,12},{24,0},{28,4},{1,25},{... | collective-permute-start | bytes 466952 | tf_op jit(solution)/shard_map/ppermute | solution.py:647
  19.1 12.8 %collective-permute-start.8 = (bf16[16,4864]{1,0:T(8,128)(2,1)}, bf16[16,4864]{1,0:T(8,128)(2,1)S(1)}, u32[]{:S(2)}, u32[]{:S(2)}) collective-permute-start(bf16[16,4864]{1,0:T(8,128)(2,1)} %get-tuple-element.90), channel_id=1, source_target_pairs={{0,16},{4,20},{8,24},{12,28},{16,0},{20,4},{24,8},{28,12},{1,17},{... | collective-permute-start | bytes 466952 | tf_op jit(solution)/shard_map/ppermute | solution.py:647
  20.7 19.2 %collective-permute-start.6 = (bf16[4,16,1664]{2,1,0:T(8,128)(2,1)}, bf16[4,16,1664]{2,1,0:T(8,128)(2,1)S(1)}, u32[]{:S(2)}, u32[]{:S(2)}) collective-permute-start(bf16[4,16,1664]{2,1,0:T(8,128)(2,1)} %join.2.rest_0_), channel_id=1, source_target_pairs={{0,6},{1,7},{2,4},{3,5},{4,2},{5,3},{6,0},{7,1},{8,14},{9,15},{10,... | collective-permute-start | bytes 638984 | tf_op jit(solution)/shard_map/ppermute | solution.py:655
  23.1 16.9 %collective-permute-start.5 = (bf16[4,16,1664]{2,1,0:T(8,128)(2,1)}, bf16[4,16,1664]{2,1,0:T(8,128)(2,1)S(1)}, u32[]{:S(2)}, u32[]{:S(2)}) collective-permute-start(bf16[4,16,1664]{2,1,0:T(8,128)(2,1)} %join.2.rest_0_), channel_id=1, source_target_pairs={{0,4},{4,0},{8,12},{12,8},{16,20},{20,16},{24,28},{28,24},{1,5},{5... | collective-permute-start | bytes 638984 | tf_op jit(solution)/shard_map/ppermute | solution.py:647
  25.1 12.3 %copy-start.12 = (bf16[16,4864]{1,0:T(8,128)(2,1)}, bf16[16,4864]{1,0:T(8,128)(2,1)S(1)}, u32[]{:S(2)}) copy-start(bf16[16,4864]{1,0:T(8,128)(2,1)S(1)} %collective-permute-done.9) | copy-start | bytes 466948
  25.1 15.2 %collective-permute-start.4 = (bf16[4,16,1664]{2,1,0:T(8,128)(2,1)}, bf16[4,16,1664]{2,1,0:T(8,128)(2,1)S(1)}, u32[]{:S(2)}, u32[]{:S(2)}) collective-permute-start(bf16[4,16,1664]{2,1,0:T(8,128)(2,1)} %join.2.rest_0_), channel_id=1, source_target_pairs={{0,2},{1,3},{2,0},{3,1},{4,6},{5,7},{6,4},{7,5},{8,10},{9,11},{10,... | collective-permute-start | bytes 638984 | tf_op jit(solution)/shard_map/ppermute | solution.py:647
  31.9 5.5 %copy-start.13 = (bf16[16,4864]{1,0:T(8,128)(2,1)}, bf16[16,4864]{1,0:T(8,128)(2,1)S(1)}, u32[]{:S(2)}) copy-start(bf16[16,4864]{1,0:T(8,128)(2,1)S(1)} %collective-permute-done.8) | copy-start | bytes 466948
  31.9 5.4 %collective-permute-start.7 = (bf16[16,4864]{1,0:T(8,128)(2,1)}, bf16[16,4864]{1,0:T(8,128)(2,1)S(1)}, u32[]{:S(2)}, u32[]{:S(2)}) collective-permute-start(bf16[16,4864]{1,0:T(8,128)(2,1)} %get-tuple-element.90), channel_id=1, source_target_pairs={{0,8},{4,12},{8,0},{12,4},{16,24},{20,28},{24,16},{28,20},{1,9},{5... | collective-permute-start | bytes 466952 | tf_op jit(solution)/shard_map/ppermute | solution.py:647
  40.0 7.2 %copy-start.5 = (bf16[4,16,1664]{2,1,0:T(8,128)(2,1)}, bf16[4,16,1664]{2,1,0:T(8,128)(2,1)S(1)}, u32[]{:S(2)}) copy-start(bf16[4,16,1664]{2,1,0:T(8,128)(2,1)S(1)} %collective-permute-done.6.rest_3_) | copy-start | bytes 638980
  40.0 7.2 %copy-start.6 = (bf16[4,16,1664]{2,1,0:T(8,128)(2,1)}, bf16[4,16,1664]{2,1,0:T(8,128)(2,1)S(1)}, u32[]{:S(2)}) copy-start(bf16[4,16,1664]{2,1,0:T(8,128)(2,1)S(1)} %collective-permute-done.5.rest_2_) | copy-start | bytes 638980
  40.2 6.9 %copy-start.7 = (bf16[4,16,1664]{2,1,0:T(8,128)(2,1)}, bf16[4,16,1664]{2,1,0:T(8,128)(2,1)S(1)}, u32[]{:S(2)}) copy-start(bf16[4,16,1664]{2,1,0:T(8,128)(2,1)S(1)} %collective-permute-done.4.rest_1_) | copy-start | bytes 638980
  40.2 1.9 collective-permute-start.13
  40.2 5.0 %collective-permute-start.14 = (bf16[4,16,1664]{2,1,0:T(8,128)(2,1)S(1)}, bf16[4,16,1664]{2,1,0:T(8,128)(2,1)S(1)}, u32[]{:S(2)}, u32[]{:S(2)}) collective-permute-start(bf16[4,16,1664]{2,1,0:T(8,128)(2,1)S(1)} %collective-permute-done.4.rest_1_), channel_id=1, source_target_pairs={{0,1},{1,0},{2,3},{3,2},{4,5},{5,4},{6,7},{7,6},{8,9},{9,8},{10,11... | collective-permute-start | bytes 638984 | tf_op jit(solution)/shard_map/ppermute | solution.py:647
  40.7 5.0 %collective-permute-start.15 = (bf16[4,16,1664]{2,1,0:T(8,128)(2,1)S(1)}, bf16[4,16,1664]{2,1,0:T(8,128)(2,1)S(1)}, u32[]{:S(2)}, u32[]{:S(2)}) collective-permute-start(bf16[4,16,1664]{2,1,0:T(8,128)(2,1)S(1)} %collective-permute-done.5.rest_2_), channel_id=1, source_target_pairs={{0,1},{1,0},{2,3},{3,2},{4,5},{5,4},{6,7},{7,6},{8,9},{9,8},{10,11... | collective-permute-start | bytes 638984 | tf_op jit(solution)/shard_map/ppermute | solution.py:647
  40.7 5.2 %collective-permute-start.16 = (bf16[4,16,1664]{2,1,0:T(8,128)(2,1)S(1)}, bf16[4,16,1664]{2,1,0:T(8,128)(2,1)S(1)}, u32[]{:S(2)}, u32[]{:S(2)}) collective-permute-start(bf16[4,16,1664]{2,1,0:T(8,128)(2,1)S(1)} %collective-permute-done.6.rest_3_), channel_id=1, source_target_pairs={{0,1},{1,0},{2,3},{3,2},{4,5},{5,4},{6,7},{7,6},{8,9},{9,8},{10,11... | collective-permute-start | bytes 638984 | tf_op jit(solution)/shard_map/ppermute | solution.py:647
  41.8 31.4 %copy-start.4 = (bf16[4,16,4864]{2,1,0:T(8,128)(2,1)S(1)}, bf16[4,16,4864]{2,1,0:T(8,128)(2,1)}, u32[]{:S(2)}) copy-start(bf16[4,16,4864]{2,1,0:T(8,128)(2,1)} %join.3.rest_0_) | copy-start | bytes 1867780
  42.2 5.0 %copy-start.8 = (bf16[4,16,1664]{2,1,0:T(8,128)(2,1)}, bf16[4,16,1664]{2,1,0:T(8,128)(2,1)S(1)}, u32[]{:S(2)}) copy-start(bf16[4,16,1664]{2,1,0:T(8,128)(2,1)S(1)} %collective-permute-done.13.rest_4_) | copy-start | bytes 638980
  42.2 28.8 %collective-permute-start.12 = (bf16[4,16,4864]{2,1,0:T(8,128)(2,1)}, bf16[4,16,4864]{2,1,0:T(8,128)(2,1)}, u32[]{:S(2)}, u32[]{:S(2)}) collective-permute-start(bf16[4,16,4864]{2,1,0:T(8,128)(2,1)} %join.3.rest_0_), channel_id=1, source_target_pairs={{0,6},{1,7},{2,4},{3,5},{4,2},{5,3},{6,0},{7,1},{8,14},{9,15},{10,... | collective-permute-start | bytes 1867784 | tf_op jit(solution)/shard_map/ppermute | solution.py:655
  45.2 28.0 %collective-permute-start.11 = (bf16[4,16,4864]{2,1,0:T(8,128)(2,1)}, bf16[4,16,4864]{2,1,0:T(8,128)(2,1)}, u32[]{:S(2)}, u32[]{:S(2)}) collective-permute-start(bf16[4,16,4864]{2,1,0:T(8,128)(2,1)} %join.3.rest_0_), channel_id=1, source_target_pairs={{0,4},{4,0},{8,12},{12,8},{16,20},{20,16},{24,28},{28,24},{1,5},{5... | collective-permute-start | bytes 1867784 | tf_op jit(solution)/shard_map/ppermute | solution.py:647
  45.7 27.5 %collective-permute-start.10 = (bf16[4,16,4864]{2,1,0:T(8,128)(2,1)}, bf16[4,16,4864]{2,1,0:T(8,128)(2,1)}, u32[]{:S(2)}, u32[]{:S(2)}) collective-permute-start(bf16[4,16,4864]{2,1,0:T(8,128)(2,1)} %join.3.rest_0_), channel_id=1, source_target_pairs={{0,2},{1,3},{2,0},{3,1},{4,6},{5,7},{6,4},{7,5},{8,10},{9,11},{10,... | collective-permute-start | bytes 1867784 | tf_op jit(solution)/shard_map/ppermute | solution.py:647
  73.2 2.2 collective-permute-start.17
  73.2 3.1 %collective-permute-start.18 = (bf16[4,16,4864]{2,1,0:T(8,128)(2,1)}, bf16[4,16,4864]{2,1,0:T(8,128)(2,1)S(1)}, u32[]{:S(2)}, u32[]{:S(2)}) collective-permute-start(bf16[4,16,4864]{2,1,0:T(8,128)(2,1)} %collective-permute-done.10.rest_1_), channel_id=1, source_target_pairs={{0,1},{1,0},{2,3},{3,2},{4,5},{5,4},{6,7},{7,6},{8,9},{9,8},{10,11... | collective-permute-start | bytes 1867784 | tf_op jit(solution)/shard_map/ppermute | solution.py:647
  73.7 3.5 %collective-permute-start.19 = (bf16[4,16,4864]{2,1,0:T(8,128)(2,1)}, bf16[4,16,4864]{2,1,0:T(8,128)(2,1)S(1)}, u32[]{:S(2)}, u32[]{:S(2)}) collective-permute-start(bf16[4,16,4864]{2,1,0:T(8,128)(2,1)} %collective-permute-done.11.rest_2_), channel_id=1, source_target_pairs={{0,1},{1,0},{2,3},{3,2},{4,5},{5,4},{6,7},{7,6},{8,9},{9,8},{10,11... | collective-permute-start | bytes 1867784 | tf_op jit(solution)/shard_map/ppermute | solution.py:647
  73.8 4.3 %collective-permute-start.20 = (bf16[4,16,4864]{2,1,0:T(8,128)(2,1)}, bf16[4,16,4864]{2,1,0:T(8,128)(2,1)S(1)}, u32[]{:S(2)}, u32[]{:S(2)}) collective-permute-start(bf16[4,16,4864]{2,1,0:T(8,128)(2,1)} %collective-permute-done.12.rest_3_), channel_id=1, source_target_pairs={{0,1},{1,0},{2,3},{3,2},{4,5},{5,4},{6,7},{7,6},{8,9},{9,8},{10,11... | collective-permute-start | bytes 1867784 | tf_op jit(solution)/shard_map/ppermute | solution.py:647
  161.5 16.0 %collective-permute-start.21 = (bf16[16,16,4864]{2,1,0:T(8,128)(2,1)}, bf16[16,16,4864]{2,1,0:T(8,128)(2,1)}, u32[]{:S(2)}, u32[]{:S(2)}) collective-permute-start(bf16[16,16,4864]{2,1,0:T(8,128)(2,1)} %get-tuple-element.114), channel_id=1, source_target_pairs={{0,1},{1,0},{2,3},{3,2},{4,5},{5,4},{6,7},{7,6},{8,9},{9,8},{10,11... | collective-permute-start | bytes 7471112 | tf_op jit(solution)/shard_map/ppermute | solution.py:647
  161.7 18.3 %collective-permute-start.22 = (bf16[4,256,512]{2,1,0:T(8,128)(2,1)}, bf16[4,256,512]{2,1,0:T(8,128)(2,1)S(1)}, u32[]{:S(2)}, u32[]{:S(2)}) collective-permute-start(bf16[4,256,512]{2,1,0:T(8,128)(2,1)} %get-tuple-element.115), channel_id=1, source_target_pairs={{0,1},{1,2},{2,3},{3,0},{4,5},{5,6},{6,7},{7,4},{8,9},{9,10},{10,1... | collective-permute-start | bytes 3145736 | tf_op jit(solution)/shard_map/ppermute | solution.py:27
  162.1 15.4 %copy-start.1 = (bf16[16,16,4864]{2,1,0:T(8,128)(2,1)S(1)}, bf16[16,16,4864]{2,1,0:T(8,128)(2,1)}, u32[]{:S(2)}) copy-start(bf16[16,16,4864]{2,1,0:T(8,128)(2,1)} %get-tuple-element.113) | copy-start | bytes 7471108
  182.6 45.4 %collective-permute-start.24 = (bf16[4,16,4864]{2,1,0:T(8,128)(2,1)}, bf16[4,16,4864]{2,1,0:T(8,128)(2,1)}, u32[]{:S(2)}, u32[]{:S(2)}) collective-permute-start(bf16[4,16,4864]{2,1,0:T(8,128)(2,1)} %get-tuple-element.138), channel_id=1, source_target_pairs={{0,2},{1,3},{2,0},{3,1},{4,6},{5,7},{6,4},{7,5},{8,10},{9,11},{10,... | collective-permute-start | bytes 1867784 | tf_op jit(solution)/shard_map/ppermute | solution.py:647
  184.4 43.7 %collective-permute-start.26 = (bf16[4,16,4864]{2,1,0:T(8,128)(2,1)}, bf16[4,16,4864]{2,1,0:T(8,128)(2,1)}, u32[]{:S(2)}, u32[]{:S(2)}) collective-permute-start(bf16[4,16,4864]{2,1,0:T(8,128)(2,1)} %get-tuple-element.139), channel_id=1, source_target_pairs={{0,6},{1,7},{2,4},{3,5},{4,2},{5,3},{6,0},{7,1},{8,14},{9,15},{10,... | collective-permute-start | bytes 1867784 | tf_op jit(solution)/shard_map/ppermute | solution.py:655
  185.2 42.9 %collective-permute-start.25 = (bf16[4,16,4864]{2,1,0:T(8,128)(2,1)}, bf16[4,16,4864]{2,1,0:T(8,128)(2,1)}, u32[]{:S(2)}, u32[]{:S(2)}) collective-permute-start(bf16[4,16,4864]{2,1,0:T(8,128)(2,1)} %get-tuple-element.140), channel_id=1, source_target_pairs={{0,4},{4,0},{8,12},{12,8},{16,20},{20,16},{24,28},{28,24},{1,5},{5... | collective-permute-start | bytes 1867784 | tf_op jit(solution)/shard_map/ppermute | solution.py:647
  210.5 26.5 %collective-permute-start.23 = (bf16[4,256,512]{2,1,0:T(8,128)(2,1)}, bf16[4,256,512]{2,1,0:T(8,128)(2,1)S(1)}, u32[]{:S(2)}, u32[]{:S(2)}) collective-permute-start(bf16[4,256,512]{2,1,0:T(8,128)(2,1)} %get-tuple-element.125), channel_id=1, source_target_pairs={{0,1},{1,2},{2,3},{3,0},{4,5},{5,6},{6,7},{7,4},{8,9},{9,10},{10,1... | collective-permute-start | bytes 3145736 | tf_op jit(solution)/shard_map/ppermute | solution.py:27
  211.2 16.9 %slice-start = ((f32[16,16,4864]{2,1,0:T(8,128)}), f32[4,16,4864]{2,1,0:T(8,128)S(1)}, s32[]{:S(2)}) async-start(f32[16,16,4864]{2,1,0:T(8,128)} %copy-done), calls=%async_computation | async-start | bytes 2490368 | tf_op jit(solution)/shard_map/slice | solution.py:710
  228.1 6.3 %copy-start.3 = (bf16[16,16,1664]{2,1,0:T(8,128)(2,1)S(1)}, bf16[16,16,1664]{2,1,0:T(8,128)(2,1)}, u32[]{:S(2)}) copy-start(bf16[16,16,1664]{2,1,0:T(8,128)(2,1)} %get-tuple-element.130) | copy-start | bytes 2555908
  230.0 4.3 %collective-permute-start.30 = (bf16[16,16,1664]{2,1,0:T(8,128)(2,1)S(1)}, bf16[16,16,1664]{2,1,0:T(8,128)(2,1)S(1)}, u32[]{:S(2)}, u32[]{:S(2)}) collective-permute-start(bf16[16,16,1664]{2,1,0:T(8,128)(2,1)S(1)} %copy-done.19), channel_id=1, source_target_pairs={{0,1},{1,0},{2,3},{3,2},{4,5},{5,4},{6,7},{7,6},{8,9},{9,8},{10,11... | collective-permute-start | bytes 2555912 | tf_op jit(solution)/shard_map/ppermute | solution.py:647
  231.3 16.7 %collective-permute-start.29 = (bf16[16,4864]{1,0:T(8,128)(2,1)S(1)}, bf16[16,4864]{1,0:T(8,128)(2,1)S(1)}, u32[]{:S(2)}, u32[]{:S(2)}) collective-permute-start(bf16[16,4864]{1,0:T(8,128)(2,1)S(1)} %get-tuple-element.146), channel_id=1, source_target_pairs={{0,24},{4,28},{8,16},{12,20},{16,8},{20,12},{24,0},{28,4},{1,25},{... | collective-permute-start | bytes 466952 | tf_op jit(solution)/shard_map/ppermute | solution.py:647
  234.3 13.7 %collective-permute-start.28 = (bf16[16,4864]{1,0:T(8,128)(2,1)S(1)}, bf16[16,4864]{1,0:T(8,128)(2,1)S(1)}, u32[]{:S(2)}, u32[]{:S(2)}) collective-permute-start(bf16[16,4864]{1,0:T(8,128)(2,1)S(1)} %get-tuple-element.147), channel_id=1, source_target_pairs={{0,16},{4,20},{8,24},{12,28},{16,0},{20,4},{24,8},{28,12},{1,17},{... | collective-permute-start | bytes 466952 | tf_op jit(solution)/shard_map/ppermute | solution.py:647
  234.7 8.2 %collective-permute-start.31 = (bf16[4,16,1664]{2,1,0:T(8,128)(2,1)S(1)}, bf16[4,16,1664]{2,1,0:T(8,128)(2,1)S(1)}, u32[]{:S(2)}, u32[]{:S(2)}) collective-permute-start(bf16[4,16,1664]{2,1,0:T(8,128)(2,1)S(1)} %get-tuple-element.143), channel_id=1, source_target_pairs={{0,2},{1,3},{2,0},{3,1},{4,6},{5,7},{6,4},{7,5},{8,10},{9,11},{10,... | collective-permute-start | bytes 638984 | tf_op jit(solution)/shard_map/ppermute | solution.py:647
  235.3 11.2 %collective-permute-start.33 = (bf16[4,16,1664]{2,1,0:T(8,128)(2,1)S(1)}, bf16[4,16,1664]{2,1,0:T(8,128)(2,1)S(1)}, u32[]{:S(2)}, u32[]{:S(2)}) collective-permute-start(bf16[4,16,1664]{2,1,0:T(8,128)(2,1)S(1)} %get-tuple-element.144), channel_id=1, source_target_pairs={{0,6},{1,7},{2,4},{3,5},{4,2},{5,3},{6,0},{7,1},{8,14},{9,15},{10,... | collective-permute-start | bytes 638984 | tf_op jit(solution)/shard_map/ppermute | solution.py:655
  236.9 10.9 %collective-permute-start.32 = (bf16[4,16,1664]{2,1,0:T(8,128)(2,1)S(1)}, bf16[4,16,1664]{2,1,0:T(8,128)(2,1)S(1)}, u32[]{:S(2)}, u32[]{:S(2)}) collective-permute-start(bf16[4,16,1664]{2,1,0:T(8,128)(2,1)S(1)} %get-tuple-element.145), channel_id=1, source_target_pairs={{0,4},{4,0},{8,12},{12,8},{16,20},{20,16},{24,28},{28,24},{1,5},{5... | collective-permute-start | bytes 638984 | tf_op jit(solution)/shard_map/ppermute | solution.py:647
  242.9 6.9 %collective-permute-start.27 = (bf16[16,4864]{1,0:T(8,128)(2,1)S(1)}, bf16[16,4864]{1,0:T(8,128)(2,1)S(1)}, u32[]{:S(2)}, u32[]{:S(2)}) collective-permute-start(bf16[16,4864]{1,0:T(8,128)(2,1)S(1)} %get-tuple-element.148), channel_id=1, source_target_pairs={{0,8},{4,12},{8,0},{12,4},{16,24},{20,28},{24,16},{28,20},{1,9},{5... | collective-permute-start | bytes 466952 | tf_op jit(solution)/shard_map/ppermute | solution.py:647
  250.5 6.2 %collective-permute-start.34 = (bf16[16,1664]{1,0:T(8,128)(2,1)S(1)}, bf16[16,1664]{1,0:T(8,128)(2,1)S(1)}, u32[]{:S(2)}, u32[]{:S(2)}) collective-permute-start(bf16[16,1664]{1,0:T(8,128)(2,1)S(1)} %get-tuple-element.154), channel_id=1, source_target_pairs={{0,8},{4,12},{8,0},{12,4},{16,24},{20,28},{24,16},{28,20},{1,9},{5... | collective-permute-start | bytes 159752 | tf_op jit(solution)/shard_map/ppermute | solution.py:647
  250.6 6.4 %collective-permute-start.36 = (bf16[16,1664]{1,0:T(8,128)(2,1)S(1)}, bf16[16,1664]{1,0:T(8,128)(2,1)S(1)}, u32[]{:S(2)}, u32[]{:S(2)}) collective-permute-start(bf16[16,1664]{1,0:T(8,128)(2,1)S(1)} %get-tuple-element.155), channel_id=1, source_target_pairs={{0,24},{4,28},{8,16},{12,20},{16,8},{20,12},{24,0},{28,4},{1,25},{... | collective-permute-start | bytes 159752 | tf_op jit(solution)/shard_map/ppermute | solution.py:647
  253.7 5.0 %collective-permute-start.35 = (bf16[16,1664]{1,0:T(8,128)(2,1)S(1)}, bf16[16,1664]{1,0:T(8,128)(2,1)S(1)}, u32[]{:S(2)}, u32[]{:S(2)}) collective-permute-start(bf16[16,1664]{1,0:T(8,128)(2,1)S(1)} %get-tuple-element.156), channel_id=1, source_target_pairs={{0,16},{4,20},{8,24},{12,28},{16,0},{20,4},{24,8},{28,12},{1,17},{... | collective-permute-start | bytes 159752 | tf_op jit(solution)/shard_map/ppermute | solution.py:647
  (14 other events, 24.8 us)

commit v5 on v4

--- a/solution.py
+++ b/solution.py
@@ -159,12 +159,13 @@
             out[j, :, out.shape[-1] - tail.shape[-1] :] = tail.astype(out.dtype)
 
 
-def store_rows(out, halo, held, sem, local, total, step, frames, value):
+def store_rows(out, halo, held, sem, local, total, window_row, frame, value):
     slot = lax.rem(local, 2)
-    half = value.shape[0] // 2
+    half = out.shape[2]
+    count = value.shape[0] // (2 * half)
 
     def finish(slot):
-        for part in range(2):
+        for part in range(2 * count):
             rows = held.at[slot, pl.ds(part * half, half)]
             pltpu.make_async_copy(rows, rows, sem.at[slot, part]).wait()
 
@@ -173,19 +174,21 @@
         finish(slot)
 
     held[slot] = value
-    frame, window_row = lax.rem(step, frames), step // frames
-    top, bottom = (held.at[slot, pl.ds(part * half, half)] for part in range(2))
-    pltpu.make_async_copy(top, out.at[frame, 1 + 2 * window_row], sem.at[slot, 0]).start()
-
-    @pl.when(step < frames)
-    def _():
-        pltpu.make_async_copy(bottom, out.at[frame, 2], sem.at[slot, 1]).start()
-
-    if halo is not None:
-
-        @pl.when(step >= frames)
+    for i in range(count):
+        at = frame + i
+        top, bottom = (held.at[slot, pl.ds((2 * i + part) * half, half)] for part in range(2))
+        top_sem, bottom_sem = sem.at[slot, 2 * i], sem.at[slot, 2 * i + 1]
+        pltpu.make_async_copy(top, out.at[at, 1 + 2 * window_row], top_sem).start()
+
+        @pl.when(window_row == 0)
         def _():
-            pltpu.make_async_copy(bottom, halo.at[frame], sem.at[slot, 1]).start()
+            pltpu.make_async_copy(bottom, out.at[at, 2], bottom_sem).start()
+
+        if halo is not None:
+
+            @pl.when(window_row == 1)
+            def _():
+                pltpu.make_async_copy(bottom, halo.at[at], bottom_sem).start()
 
     @pl.when(local == total - 1)
     def _():
@@ -273,56 +276,73 @@
         dw_down_t[...] = jnp.zeros_like(dw_down_t)
         small[...] = jnp.zeros_like(small)
 
-    bottom = jnp.where(step < frames, own[...], halo[...])
-    dbottom = jnp.where(step < frames, down[...], dhalo[...])
-    x = to_window_order(jnp.concatenate([top[...], bottom], axis=0).astype(F32), columns)
-    dy = to_window_order(jnp.concatenate([dtop[...], dbottom], axis=0).astype(F32), columns)
+    count = top.shape[0]
+    pairs = frames // count
+    window_row = step // pairs
+
+    def rows_of(top, own, halo):
+        out = []
+        for i in range(count):
+            bottom = jnp.where(window_row == 0, own[i], halo[i])
+            rows = jnp.concatenate([top[i], bottom], axis=0).astype(F32)
+            out.append(to_window_order(rows, columns))
+        return jnp.concatenate(out, axis=0)
+
+    dy = rows_of(dtop, down, dhalo)
     dy_low = dy.astype(BF16)
-    x2 = x + dot(o_in[...], w_proj[...]) + b_proj[...]
+    o_rows = o_in[...].reshape(-1, width)
+    x2 = rows_of(top, own, halo) + dot(o_rows, w_proj[...]) + b_proj[...]
+    parts = [slice(start, start + chunk) for start in range(0, hidden_width, chunk)]
+    dgs = {0: dot_t(dy_low, w_down[parts[0], :])}
     normed, inverse = normalize(x2)
     h2 = (normed * g_two[...] + b_two[...]).astype(BF16)
     h2_t = h2.T
     dy_t = dy_low.T
     total = x2 + b_down[...]
     dh2 = jnp.zeros_like(x2)
-    parts = [slice(start, start + chunk) for start in range(0, hidden_width, chunk)]
-
-    def enter(part):
-        return dot(h2, w_up[:, part]) + b_up[:, part], dot_t(dy_low, w_down[part, :])
-
-    ahead = enter(parts[0])
-    for index, part in enumerate(parts + [None]):
-        if part is not None:
-            u, dg = ahead
+
+    def enter(index):
+        if index not in dgs:
+            dgs[index] = dot_t(dy_low, w_down[parts[index], :])
+        return dot(h2, w_up[:, parts[index]]) + b_up[:, parts[index]]
+
+    ahead = enter(0)
+    for index in range(len(parts) + 1):
+        if index < len(parts):
+            u, part = ahead, parts[index]
             if index + 1 < len(parts):
-                ahead = enter(parts[index + 1])
+                ahead = enter(index + 1)
             phi = 0.5 * (1.0 + lax.erf(u * INV_ROOT_TWO))
-            g_s[:, part] = (u * phi).astype(BF16)
-            du = dg * (phi + u * jnp.exp(-0.5 * u * u) * INV_ROOT_TWO_PI)
-            du_s[:, part] = du.astype(BF16)
+            g_s[index % 2] = (u * phi).astype(BF16)
+            du = dgs[index] * (phi + u * jnp.exp(-0.5 * u * u) * INV_ROOT_TWO_PI)
+            du_s[index % 2] = du.astype(BF16)
             small[0:1, part] += jnp.sum(du, axis=0, keepdims=True)
         if index > 0:
-            old = parts[index - 1]
-            total += dot(g_s[:, old], w_down[old, :])
-            dh2 += dot_t(du_s[:, old], w_up[:, old])
-            dw_up[:, old] += dot(h2_t, du_s[:, old])
-            dw_down_t[:, old] += dot(dy_t, g_s[:, old])
-    mixed = from_window_order(total, columns).astype(BF16)
-    store_rows(m_out, m_halo, held, out_sem, step, pl.num_programs(0), step, frames, mixed)
+            old, slot = parts[index - 1], (index - 1) % 2
+            total += dot(g_s[slot], w_down[old, :])
+            dh2 += dot_t(du_s[slot], w_up[:, old])
+            dw_up[:, old] += dot(h2_t, du_s[slot])
+            dw_down_t[:, old] += dot(dy_t, g_s[slot])
+    block = total.shape[0] // count
+    mixed = [from_window_order(total[i * block : (i + 1) * block], columns) for i in range(count)]
+    mixed = jnp.concatenate(mixed, axis=0).astype(BF16)
+    store_rows(
+        m_out, m_halo, held, out_sem, step, pl.num_programs(0), window_row, lax.rem(step, pairs) * count, mixed
+    )
     small[1:2, :width] += jnp.sum(dy, axis=0, keepdims=True)
     small[2:3, :width] += jnp.sum(dh2 * normed, axis=0, keepdims=True)
     small[3:4, :width] += jnp.sum(dh2, axis=0, keepdims=True)
     dx2 = dy + norm_back(dh2 * g_two[...], normed, inverse)
     da = dx2.astype(BF16)
     small[4:5, :width] += jnp.sum(dx2, axis=0, keepdims=True)
-    dx_out[...] = dx2
-    dw_proj[...] += dot(o_in[...].T, da)
-    do_out[...] = dot_t(da, w_proj[...]).astype(BF16)
+    dx_out[...] = dx2.reshape(dx_out.shape)
+    dw_proj[...] += dot(o_rows.T, da)
+    do_out[...] = dot_t(da, w_proj[...]).astype(BF16).reshape(do_out.shape)
 
     @pl.when(step == pl.num_programs(0) - 1)
     def _():
         for lane in range(0, hidden_width, LANE):
-            dw_down[lane : lane + LANE, :] = dw_down_t[:, lane : lane + LANE].T
+            dw_down[lane : lane + LANE, :] = dw_down_t[:, lane : lane + LANE].astype(BF16).T
         order = (4, 2, 3, 1)
         flat = jnp.concatenate([small[r : r + 1, :width] for r in order] + [small[0:1, :]], axis=1)
         lines_of = keep.shape[-1] - width - 2 * hidden_width
@@ -405,7 +425,9 @@
     small[2:3, :width] += jnp.sum(dh, axis=0, keepdims=True)
     grad = dx_in[...] + norm_back(dh * gain[...], normed, inverse)
     grad = from_window_order(grad, columns).astype(BF16)
-    store_rows(g_out, g_halo, held, out_sem, local, count, step, frames, grad)
+    store_rows(
+        g_out, g_halo, held, out_sem, local, count, step // frames, lax.rem(step, frames), grad
+    )
 
     if ends:
 
@@ -490,18 +512,17 @@
     )(index, *vectors, qkv, proj, up, down)
 
 
-def grid_specs(frames, cells, width, first=0, which=0):
+def grid_specs(frames, cells, width, first=0, which=0, count=None):
+    turns = frames // (count or 1)
+    at = lambda s: (s + first) % (2 * turns)
     top = pl.BlockSpec(
-        (None, None, cells, width),
-        lambda s, *_: ((s + first) % frames, 1 + 2 * ((s + first) % (2 * frames) // frames), 0, 0),
+        (count, None, cells, width), lambda s, *_: (at(s) % turns, 1 + 2 * (at(s) // turns), 0, 0)
     )
     own = pl.BlockSpec(
-        (None, None, cells, width),
-        lambda s, *_: (jnp.minimum((s + first) % (2 * frames), frames - 1), 2, 0, 0),
+        (count, None, cells, width), lambda s, *_: (jnp.minimum(at(s), turns - 1), 2, 0, 0)
     )
     halo = pl.BlockSpec(
-        (None, None, cells, width),
-        lambda s, *_: (which, jnp.maximum((s + first) % (2 * frames) - frames, 0), 0, 0),
+        (None, count, cells, width), lambda s, *_: (which, jnp.maximum(at(s) - turns, 0), 0, 0)
     )
     return [top, own, halo]
 
@@ -544,11 +565,12 @@
     )(info, tokens4, tokens4, halo, *blocks)
 
 
-def middle(info, tokens4, halo, d4, o, blocks, hidden_width, columns, chunk=256):
+def middle(info, tokens4, halo, d4, o, blocks, hidden_width, columns, chunk=256, count=1):
     frames, groups, cells, width = tokens4.shape
     steps, block = 2 * frames, 2 * cells
-    row = pl.BlockSpec((None, block, width), lambda s, *_: (s, 0, 0))
-    ins = grid_specs(frames, cells, width) + grid_specs(frames, cells, width, which=1)
+    row = pl.BlockSpec((count, block, width), lambda s, *_: (s, 0, 0))
+    ins = grid_specs(frames, cells, width, count=count)
+    ins += grid_specs(frames, cells, width, which=1, count=count)
     mine = (16,) + blocks[0].shape[1:]
     return pl.pallas_call(
         functools.partial(middle_kernel, frames, columns, chunk),
@@ -562,7 +584,7 @@
         ],
         grid_spec=pltpu.PrefetchScalarGridSpec(
             num_scalar_prefetch=1,
-            grid=(steps,),
+            grid=(steps // count,),
             in_specs=ins + [row] + [ANYWHERE] * len(blocks),
             out_specs=[ANYWHERE, ANYWHERE, row, row, whole_out(mine), whole_out(mine)],
             scratch_shapes=[
@@ -575,13 +597,13 @@
                 pltpu.VMEM((width, width), F32),
                 pltpu.VMEM((width, hidden_width), F32),
                 pltpu.VMEM((width, hidden_width), F32),
-                pltpu.VMEM((hidden_width, width), F32),
+                pltpu.VMEM((hidden_width, width), BF16),
                 pltpu.VMEM((8, hidden_width), F32),
-                pltpu.VMEM((block, hidden_width), BF16),
-                pltpu.VMEM((block, hidden_width), BF16),
-                pltpu.VMEM((2, block, width), BF16),
+                pltpu.VMEM((2, count * block, chunk), BF16),
+                pltpu.VMEM((2, count * block, chunk), BF16),
+                pltpu.VMEM((2, count * block, width), BF16),
                 pltpu.SemaphoreType.DMA((4,)),
-                pltpu.SemaphoreType.DMA((2, 2)),
+                pltpu.SemaphoreType.DMA((2, 2 * count)),
             ],
         ),
         compiler_params=params(),
@@ -772,6 +794,7 @@
         column_a = join(own_a[None], *(z[None] for z in z_a))
         z_b = along_z(after(own_b, *z_a))
         mine_a = (column_a, *over_plane(column_a))
+        z_b, halo = lax.optimization_barrier((z_b, halo))
         column_b = join(own_b[None], *(z[None] for z in z_b))
         *mine_a, column_b = lax.optimization_barrier((*mine_a, column_b))
         attend_blocks = (*mine_a, *(flipped(piece, "rows", 1) for piece in mine_a))
@@ -786,8 +809,9 @@
     info = jnp.concatenate([frame_level, jnp.stack([lax.axis_index("rows").astype(jnp.int32), me])])
     q, k, v, p, o = attend(info, tokens4, halo, attend_blocks, height, columns)
     if is_cube():
-        *mine_b, o = lax.optimization_barrier((*mine_b, o))
-        middle_blocks = (*mine_b, *(flipped(piece, "rows", 1) for piece in mine_b))
+        first_piece = flipped(mine_b[0], "rows", 1)
+        *mine_b, o, first_piece = lax.optimization_barrier((*mine_b, o, first_piece))
+        middle_blocks = (*mine_b, first_piece, *(flipped(piece, "rows", 1) for piece in mine_b[1:]))
     m_out, m_halo, dx, do, keep, send = middle(
         info, tokens4, halo, d4, o, middle_blocks, hidden_width, columns
     )
@@ -798,13 +822,11 @@
     if is_cube():
         shards = lax.axis_size("dp") * lax.axis_size("rows")
         cores_b = sum_cores(keep, send)
-        part_a = back(*states, (), frames, 2, False)
+        part_a = back(*states, (), frames, 4, False)
         *part_a, cores_b, m_back = lax.optimization_barrier((*part_a, cores_b, m_back))
         plane_b = sum_plane(*cores_b)
-        part_b = back(*states, part_a[:2], frames + 2, frames, False)
-        g_back = from_behind(part_b[1], "rows", 1)
-        sums = (*part_a[2:], *part_b[2:])
-        g_out, keep, send = back(*states, (part_b[0], *sums), 2, frames - 2, True)
+        g_back = from_behind(part_a[1], "rows", 1)
+        g_out, keep, send = back(*states, (part_a[0], *part_a[2:]), 0, 4, True)
         plane_b, send = lax.optimization_barrier((plane_b, send))
         plane_a = sum_plane(*sum_cores(keep, send))
         line_b = [flipped(plane_b[1][z - 1], "dp", 2 * z) for z in (1, 2, 3)]

time: 261 us -> 257 us (0.985)
  Pallas kernels: 166 us -> 160 us
  waiting for transfers between devices: 33.2 us -> 37.3 us
    pallas_call x3 -> x2, Pallas kernels: 55.5 us -> 49.1 us  [back(): pl.pallas_call(functools.partial(back_kernel, frames, columns, first, cou...]
    ppermute x30, starting transfers between devices: 26.6 us -> 29.9 us  [flipped(): return lax.ppermute(x, axis, flip_perm(axis, bits))]
    unnamed x50 -> x46, local copies, waits for them, and re-layouts: 5.23 us -> 3.41 us
  transfers between devices with their start and end apart: 37 -> 37, of which waited for: 18 -> 16; matrix products, arithmetic and copies ran while one was open for 4% -> 4% of each run, Pallas kernels for 32% -> 30%
where the time goes in v5:
time: 257 us
  Pallas kernels  160 us (62%)
  starting transfers between devices  39.9 us (16%)
  waiting for transfers between devices  37.3 us (15%)
  local copies, waits for them, and re-layouts  12.9 us (5%)
  other arithmetic  5.97 us (2%)
    pallas_call x1, Pallas kernels, middle(): pl.pallas_call(functools.partial(middle_kernel, frames, columns, chunk),...  82.7 us
    pallas_call x2, Pallas kernels, back(): pl.pallas_call(functools.partial(back_kernel, frames, columns, first, cou...  49.1 us
    ppermute x30, waiting for transfers between devices, flipped(): return lax.ppermute(x, axis, flip_perm(axis, bits))  31.2 us
    ppermute x30, starting transfers between devices, flipped(): return lax.ppermute(x, axis, flip_perm(axis, bits))  29.9 us
    pallas_call x1, Pallas kernels, attend(): pl.pallas_call(functools.partial(attend_kernel, frames, columns, height,...  22.3 us
    ppermute x4, starting transfers between devices, flipped_both(): return lax.ppermute(x, AXES, pairs)  7.25 us
  transfers between devices with their start and end apart: 37, of which 16 were waited for; matrix products, arithmetic and copies ran while one was open for 4% of the time, Pallas kernels for 30%

profile of v5, /device:TPU:0, one launch (start us, length us, event | category | flops | bytes accessed | tf_op | source)
XLA Modules:
  0.0 256.7 jit_solution(6706498759086641387)
XLA Ops:
  0.6 1.8 slice_bitcast_fusion
  2.6 2.4 collective-permute-start.6
  5.1 1.8 pack.1
  6.9 1.6 collective-permute-start
  8.5 2.6 %collective-permute-start.1 = (bf16[16,1664]{1,0:T(8,128)(2,1)}, bf16[16,1664]{1,0:T(8,128)(2,1)S(1)}, u32[]{:S(2)}, u32[]{:S(2)}) collective-permute-start(bf16[16,1664]{1,0:T(8,128)(2,1)} %get-tuple-element.90), channel_id=1, source_target_pairs={{0,16},{4,20},{8,24},{12,28},{16,0},{20,4},{24,8},{28,12},{1,17},{... | collective-permute-start | bytes 159752 | tf_op jit(solution)/shard_map/ppermute | solution.py:669
  11.3 3.2 %collective-permute-done.1 = bf16[16,1664]{1,0:T(8,128)(2,1)S(1)} collective-permute-done((bf16[16,1664]{1,0:T(8,128)(2,1)}, bf16[16,1664]{1,0:T(8,128)(2,1)S(1)}, u32[]{:S(2)}, u32[]{:S(2)}) %collective-permute-start.1) | collective-permute-done | bytes 53280 | tf_op jit(solution)/shard_map/ppermute | solution.py:669
  14.5 2.7 %collective-permute-done.2 = bf16[16,1664]{1,0:T(8,128)(2,1)S(1)} collective-permute-done((bf16[16,1664]{1,0:T(8,128)(2,1)}, bf16[16,1664]{1,0:T(8,128)(2,1)S(1)}, u32[]{:S(2)}, u32[]{:S(2)}) %collective-permute-start.2) | collective-permute-done | bytes 53280 | tf_op jit(solution)/shard_map/ppermute | solution.py:669
  17.2 1.4 collective-permute-start.4
  18.6 1.6 join.2.rest_0_
  20.1 1.5 collective-permute-start.7
  21.6 1.5 collective-permute-start.8
  23.2 1.1 collective-permute-done.3
  24.3 2.8 %collective-permute-start.9 = (bf16[4,16,1664]{2,1,0:T(8,128)(2,1)}, bf16[4,16,1664]{2,1,0:T(8,128)(2,1)S(1)}, u32[]{:S(2)}, u32[]{:S(2)}) collective-permute-start(bf16[4,16,1664]{2,1,0:T(8,128)(2,1)} %join.2.rest_0_), channel_id=1, source_target_pairs={{0,6},{1,7},{2,4},{3,5},{4,2},{5,3},{6,0},{7,1},{8,14},{9,15},{10,... | collective-permute-start | bytes 638984 | tf_op jit(solution)/shard_map/ppermute | solution.py:677
  27.4 7.0 %collective-permute-done.5 = bf16[16,4864]{1,0:T(8,128)(2,1)S(1)} collective-permute-done((bf16[16,4864]{1,0:T(8,128)(2,1)}, bf16[16,4864]{1,0:T(8,128)(2,1)S(1)}, u32[]{:S(2)}, u32[]{:S(2)}) %collective-permute-start.5) | collective-permute-done | bytes 155680 | tf_op jit(solution)/shard_map/ppermute | solution.py:669
  35.1 2.0 join.3.rest_0_
  37.2 2.6 collective-permute-done.9.rest_3_
  41.3 1.5 collective-permute-start.10
  43.3 1.5 collective-permute-start.12
  44.9 22.3 %attend.1 = (bf16[8,512,512]{2,1,0:T(8,128)(2,1)}, bf16[8,512,512]{2,1,0:T(8,128)(2,1)}, bf16[8,512,512]{2,1,0:T(8,128)(2,1)}, bf16[8,512,512]{2,1,0:T(8,128)(2,1)}, bf16[8,512,512]{2,1,0:T(8,128)(2,1)}) custom-call(s32[6]{0:T(128)} %pad_add_fusion.info, bf16[4,4,256,512]{3,2,1,0:T(8,128)(2,1)} %bitcast.53, bf16[4,4,256,512]{3,2,1,0:T(8,128)(2,1)} %bitcast.54, ...), custom_call_target="tpu_custom_call" | custom-call | flops 30000001024 | bytes 30000000 | tf_op jit(solution)/shard_map/attend/pallas_call | solution.py:547
  67.3 4.8 %collective-permute-done.11.rest_2_ = bf16[4,16,4864]{2,1,0:T(8,128)(2,1)S(1)} collective-permute-done((bf16[4,16,4864]{2,1,0:T(8,128)(2,1)}, bf16[4,16,4864]{2,1,0:T(8,128)(2,1)S(1)}, u32[]{:S(2)}, u32[]{:S(2)}) %collective-permute-start.11) | collective-permute-done | bytes 622624 | tf_op jit(solution)/shard_map/ppermute | solution.py:669
  72.7 1.5 collective-permute-done.18.rest_5_
  74.2 1.8 collective-permute-done.19.rest_6_
  76.8 82.7 %middle.1 = (bf16[4,4,256,512]{3,2,1,0:T(8,128)(2,1)}, bf16[4,256,512]{2,1,0:T(8,128)(2,1)}, f32[8,512,512]{2,1,0:T(8,128)}, bf16[8,512,512]{2,1,0:T(8,128)(2,1)...) custom-call(s32[6]{0:T(128)} %pad_add_fusion.info, bf16[4,4,256,512]{3,2,1,0:T(8,128)(2,1)} %bitcast.55, ...), custom_call_target="tpu_custom_call" | custom-call | flops 89999998976 | bytes 40000000 | tf_op jit(solution)/shard_map/middle/pallas_call | solution.py:575
  160.1 24.8 %back.2 = (bf16[4,4,256,512]{3,2,1,0:T(8,128)(2,1)}, bf16[4,256,512]{2,1,0:T(8,128)(2,1)}, f32[512,1536]{1,0:T(8,128)}, f32[8,1536]{1,0:T(8,128)}) custom-call(s32[6]{0:T(128)} %pad_add_fusion.info, bf16[4,4,256,512]{3,2,1,0:T(8,128)(2,1)} %bitcast.57, bf16[4,4,256,512]{3,2,1,0:T(8,128)(2,1)} %bitcast.58, ...), custom_call_target="tpu_custom_call" | custom-call | flops 24000000000 | bytes 20000000 | tf_op jit(solution)/shard_map/back/pallas_call | solution.py:628
  184.9 2.3 convert_add_fusion
  187.4 2.0 copy-done
  189.4 1.0 fusion.3
  191.1 1.0 collective-permute-start.25
  192.1 1.8 collective-permute-start.26
  193.9 24.4 %back.3 = (bf16[4,4,256,512]{3,2,1,0:T(8,128)(2,1)}, bf16[16,16,1664]{2,1,0:T(8,128)(2,1)}, bf16[16,16,1664]{2,1,0:T(8,128)(2,1)}) custom-call(s32[6]{0:T(128)} %pad_add_fusion.info, bf16[4,4,256,512]{3,2,1,0:T(8,128)(2,1)} %bitcast.59, bf16[4,4,256,512]{3,2,1,0:T(8,128)(2,1)} %bitcast.60, ...), custom_call_target="tpu_custom_call", output_to_operand_aliasing={{0}: (18, {})} | custom-call | flops 24000000000 | bytes 20000000 | tf_op jit(solution)/shard_map/back/pallas_call | solution.py:628
  218.3 1.0 bitcast_dynamic-update-slice_fusion
  219.3 1.9 collective-permute-done.25
  221.3 1.7 convert_add_fusion.2
  223.2 1.6 collective-permute-start.27
  224.9 2.6 %collective-permute-start.28 = (bf16[16,4864]{1,0:T(8,128)(2,1)S(1)}, bf16[16,4864]{1,0:T(8,128)(2,1)S(1)}, u32[]{:S(2)}, u32[]{:S(2)}) collective-permute-start(bf16[16,4864]{1,0:T(8,128)(2,1)S(1)} %get-tuple-element.149), channel_id=1, source_target_pairs={{0,16},{4,20},{8,24},{12,28},{16,0},{20,4},{24,8},{28,12},{1,17},{... | collective-permute-start | bytes 466952 | tf_op jit(solution)/shard_map/ppermute | solution.py:669
  228.6 1.2 collective-permute-start.32
  229.8 1.9 collective-permute-done.23
  231.7 1.2 collective-permute-start.33
  232.9 1.0 bitcast_dynamic-update-slice_fusion.1
  233.9 2.1 collective-permute-done.31
  236.0 3.5 %collective-permute-start.29 = (bf16[16,4864]{1,0:T(8,128)(2,1)S(1)}, bf16[16,4864]{1,0:T(8,128)(2,1)S(1)}, u32[]{:S(2)}, u32[]{:S(2)}) collective-permute-start(bf16[16,4864]{1,0:T(8,128)(2,1)S(1)} %get-tuple-element.148), channel_id=1, source_target_pairs={{0,24},{4,28},{8,16},{12,20},{16,8},{20,12},{24,0},{28,4},{1,25},{... | collective-permute-start | bytes 466952 | tf_op jit(solution)/shard_map/ppermute | solution.py:669
  239.5 1.6 collective-permute-done.33
  241.3 2.7 %collective-permute-done.29 = bf16[16,4864]{1,0:T(8,128)(2,1)S(1)} collective-permute-done((bf16[16,4864]{1,0:T(8,128)(2,1)S(1)}, bf16[16,4864]{1,0:T(8,128)(2,1)S(1)}, u32[]{:S(2)}, u32[]{:S(2)}) %collective-permute-start.29) | collective-permute-done | bytes 155680 | tf_op jit(solution)/shard_map/ppermute | solution.py:669
  244.7 2.9 %collective-permute-start.34 = (bf16[16,1664]{1,0:T(8,128)(2,1)S(1)}, bf16[16,1664]{1,0:T(8,128)(2,1)S(1)}, u32[]{:S(2)}, u32[]{:S(2)}) collective-permute-start(bf16[16,1664]{1,0:T(8,128)(2,1)S(1)} %get-tuple-element.156), channel_id=1, source_target_pairs={{0,8},{4,12},{8,0},{12,4},{16,24},{20,28},{24,16},{28,20},{1,9},{5... | collective-permute-start | bytes 159752 | tf_op jit(solution)/shard_map/ppermute | solution.py:669
  247.6 1.2 collective-permute-start.35
  248.8 1.3 collective-permute-start.36
  252.6 1.2 collective-permute-done.35
  253.9 1.0 collective-permute-done.36
  (110 shorter events, 13.1 us)
Async XLA Ops:
  2.4 38.3 %copy-start.9 = (s32[4]{0:T(128)S(1)}, s32[4]{0:T(128)}, u32[]{:S(2)}) copy-start(s32[4]{0:T(128)} %param.20) | copy-start | bytes 52
  2.6 31.8 %collective-permute-start.6 = (bf16[2,4,256,512]{3,2,1,0:T(8,128)(2,1)S(1)}, bf16[2,4,256,512]{3,2,1,0:T(8,128)(2,1)}, u32[]{:S(2)}, u32[]{:S(2)}) collective-permute-start(bf16[2,4,256,512]{3,2,1,0:T(8,128)(2,1)S(1)} %pad_maximum_fusion), channel_id=1, source_target_pairs={{0,3},{1,0},{2,1},{3,2},{4,7},{5,4},{6,5},{7,6},{8,11},{9,8},{10,9... | collective-permute-start | bytes 6291464 | tf_op jit(solution)/shard_map/ppermute | solution.py:27
  6.9 4.4 %collective-permute-start = (bf16[16,1664]{1,0:T(8,128)(2,1)}, bf16[16,1664]{1,0:T(8,128)(2,1)S(1)}, u32[]{:S(2)}, u32[]{:S(2)}) collective-permute-start(bf16[16,1664]{1,0:T(8,128)(2,1)} %get-tuple-element.90), channel_id=1, source_target_pairs={{0,8},{4,12},{8,0},{12,4},{16,24},{20,28},{24,16},{28,20},{1,9},{5... | collective-permute-start | bytes 159752 | tf_op jit(solution)/shard_map/ppermute | solution.py:669
  8.5 6.0 %collective-permute-start.1 = (bf16[16,1664]{1,0:T(8,128)(2,1)}, bf16[16,1664]{1,0:T(8,128)(2,1)S(1)}, u32[]{:S(2)}, u32[]{:S(2)}) collective-permute-start(bf16[16,1664]{1,0:T(8,128)(2,1)} %get-tuple-element.90), channel_id=1, source_target_pairs={{0,16},{4,20},{8,24},{12,28},{16,0},{20,4},{24,8},{28,12},{1,17},{... | collective-permute-start | bytes 159752 | tf_op jit(solution)/shard_map/ppermute | solution.py:669
  11.0 6.1 %collective-permute-start.2 = (bf16[16,1664]{1,0:T(8,128)(2,1)}, bf16[16,1664]{1,0:T(8,128)(2,1)S(1)}, u32[]{:S(2)}, u32[]{:S(2)}) collective-permute-start(bf16[16,1664]{1,0:T(8,128)(2,1)} %get-tuple-element.90), channel_id=1, source_target_pairs={{0,24},{4,28},{8,16},{12,20},{16,8},{20,12},{24,0},{28,4},{1,25},{... | collective-permute-start | bytes 159752 | tf_op jit(solution)/shard_map/ppermute | solution.py:669
  11.3 7.3 %copy-start.6 = (bf16[16,1664]{1,0:T(8,128)(2,1)}, bf16[16,1664]{1,0:T(8,128)(2,1)S(1)}, u32[]{:S(2)}) copy-start(bf16[16,1664]{1,0:T(8,128)(2,1)S(1)} %collective-permute-done) | copy-start | bytes 159748
  14.5 4.1 %copy-start.7 = (bf16[16,1664]{1,0:T(8,128)(2,1)}, bf16[16,1664]{1,0:T(8,128)(2,1)S(1)}, u32[]{:S(2)}) copy-start(bf16[16,1664]{1,0:T(8,128)(2,1)S(1)} %collective-permute-done.1) | copy-start | bytes 159748
  17.2 7.1 %collective-permute-start.3 = (bf16[16,4864]{1,0:T(8,128)(2,1)}, bf16[16,4864]{1,0:T(8,128)(2,1)S(1)}, u32[]{:S(2)}, u32[]{:S(2)}) collective-permute-start(bf16[16,4864]{1,0:T(8,128)(2,1)} %get-tuple-element.91), channel_id=1, source_target_pairs={{0,8},{4,12},{8,0},{12,4},{16,24},{20,28},{24,16},{28,20},{1,9},{5... | collective-permute-start | bytes 466952 | tf_op jit(solution)/shard_map/ppermute | solution.py:669
  17.2 9.9 %collective-permute-start.4 = (bf16[16,4864]{1,0:T(8,128)(2,1)}, bf16[16,4864]{1,0:T(8,128)(2,1)S(1)}, u32[]{:S(2)}, u32[]{:S(2)}) collective-permute-start(bf16[16,4864]{1,0:T(8,128)(2,1)} %get-tuple-element.91), channel_id=1, source_target_pairs={{0,16},{4,20},{8,24},{12,28},{16,0},{20,4},{24,8},{28,12},{1,17},{... | collective-permute-start | bytes 466952 | tf_op jit(solution)/shard_map/ppermute | solution.py:669
  20.1 17.0 %collective-permute-start.7 = (bf16[4,16,1664]{2,1,0:T(8,128)(2,1)}, bf16[4,16,1664]{2,1,0:T(8,128)(2,1)S(1)}, u32[]{:S(2)}, u32[]{:S(2)}) collective-permute-start(bf16[4,16,1664]{2,1,0:T(8,128)(2,1)} %join.2.rest_0_), channel_id=1, source_target_pairs={{0,2},{1,3},{2,0},{3,1},{4,6},{5,7},{6,4},{7,5},{8,10},{9,11},{10,... | collective-permute-start | bytes 638984 | tf_op jit(solution)/shard_map/ppermute | solution.py:669
  21.6 15.5 %collective-permute-start.8 = (bf16[4,16,1664]{2,1,0:T(8,128)(2,1)}, bf16[4,16,1664]{2,1,0:T(8,128)(2,1)S(1)}, u32[]{:S(2)}, u32[]{:S(2)}) collective-permute-start(bf16[4,16,1664]{2,1,0:T(8,128)(2,1)} %join.2.rest_0_), channel_id=1, source_target_pairs={{0,4},{4,0},{8,12},{12,8},{16,20},{20,16},{24,28},{28,24},{1,5},{5... | collective-permute-start | bytes 638984 | tf_op jit(solution)/shard_map/ppermute | solution.py:669
  24.3 10.2 %copy-start.3 = (bf16[16,4864]{1,0:T(8,128)(2,1)}, bf16[16,4864]{1,0:T(8,128)(2,1)S(1)}, u32[]{:S(2)}) copy-start(bf16[16,4864]{1,0:T(8,128)(2,1)S(1)} %collective-permute-done.3) | copy-start | bytes 466948
  24.3 15.4 %collective-permute-start.9 = (bf16[4,16,1664]{2,1,0:T(8,128)(2,1)}, bf16[4,16,1664]{2,1,0:T(8,128)(2,1)S(1)}, u32[]{:S(2)}, u32[]{:S(2)}) collective-permute-start(bf16[4,16,1664]{2,1,0:T(8,128)(2,1)} %join.2.rest_0_), channel_id=1, source_target_pairs={{0,6},{1,7},{2,4},{3,5},{4,2},{5,3},{6,0},{7,1},{8,14},{9,15},{10,... | collective-permute-start | bytes 638984 | tf_op jit(solution)/shard_map/ppermute | solution.py:677
  27.1 7.4 %copy-start.4 = (bf16[16,4864]{1,0:T(8,128)(2,1)}, bf16[16,4864]{1,0:T(8,128)(2,1)S(1)}, u32[]{:S(2)}) copy-start(bf16[16,4864]{1,0:T(8,128)(2,1)S(1)} %collective-permute-done.4) | copy-start | bytes 466948
  27.1 7.3 %collective-permute-start.5 = (bf16[16,4864]{1,0:T(8,128)(2,1)}, bf16[16,4864]{1,0:T(8,128)(2,1)S(1)}, u32[]{:S(2)}, u32[]{:S(2)}) collective-permute-start(bf16[16,4864]{1,0:T(8,128)(2,1)} %get-tuple-element.91), channel_id=1, source_target_pairs={{0,24},{4,28},{8,16},{12,20},{16,8},{20,12},{24,0},{28,4},{1,25},{... | collective-permute-start | bytes 466952 | tf_op jit(solution)/shard_map/ppermute | solution.py:669
  37.1 7.7 %copy-start.17 = (bf16[4,16,1664]{2,1,0:T(8,128)(2,1)}, bf16[4,16,1664]{2,1,0:T(8,128)(2,1)S(1)}, u32[]{:S(2)}) copy-start(bf16[4,16,1664]{2,1,0:T(8,128)(2,1)S(1)} %collective-permute-done.7.rest_1_) | copy-start | bytes 638980
  37.1 7.7 %copy-start.18 = (bf16[4,16,1664]{2,1,0:T(8,128)(2,1)}, bf16[4,16,1664]{2,1,0:T(8,128)(2,1)S(1)}, u32[]{:S(2)}) copy-start(bf16[4,16,1664]{2,1,0:T(8,128)(2,1)S(1)} %collective-permute-done.8.rest_2_) | copy-start | bytes 638980
  39.7 5.1 %copy-start.19 = (bf16[4,16,1664]{2,1,0:T(8,128)(2,1)}, bf16[4,16,1664]{2,1,0:T(8,128)(2,1)S(1)}, u32[]{:S(2)}) copy-start(bf16[4,16,1664]{2,1,0:T(8,128)(2,1)S(1)} %collective-permute-done.9.rest_3_) | copy-start | bytes 638980
  39.7 3.1 %collective-permute-start.13 = (bf16[4,16,1664]{2,1,0:T(8,128)(2,1)}, bf16[4,16,1664]{2,1,0:T(8,128)(2,1)S(1)}, u32[]{:S(2)}, u32[]{:S(2)}) collective-permute-start(bf16[4,16,1664]{2,1,0:T(8,128)(2,1)} %join.2.rest_0_), channel_id=1, source_target_pairs={{0,1},{1,0},{2,3},{3,2},{4,5},{5,4},{6,7},{7,6},{8,9},{9,8},{10,11... | collective-permute-start | bytes 638984 | tf_op jit(solution)/shard_map/ppermute | solution.py:669
  39.7 3.6 %collective-permute-start.14 = (bf16[4,16,1664]{2,1,0:T(8,128)(2,1)S(1)}, bf16[4,16,1664]{2,1,0:T(8,128)(2,1)S(1)}, u32[]{:S(2)}, u32[]{:S(2)}) collective-permute-start(bf16[4,16,1664]{2,1,0:T(8,128)(2,1)S(1)} %collective-permute-done.7.rest_1_), channel_id=1, source_target_pairs={{0,1},{1,0},{2,3},{3,2},{4,5},{5,4},{6,7},{7,6},{8,9},{9,8},{10,11... | collective-permute-start | bytes 638984 | tf_op jit(solution)/shard_map/ppermute | solution.py:669
  40.2 4.6 %collective-permute-start.15 = (bf16[4,16,1664]{2,1,0:T(8,128)(2,1)S(1)}, bf16[4,16,1664]{2,1,0:T(8,128)(2,1)}, u32[]{:S(2)}, u32[]{:S(2)}) collective-permute-start(bf16[4,16,1664]{2,1,0:T(8,128)(2,1)S(1)} %collective-permute-done.8.rest_2_), channel_id=1, source_target_pairs={{0,1},{1,0},{2,3},{3,2},{4,5},{5,4},{6,7},{7,6},{8,9},{9,8},{10,11... | collective-permute-start | bytes 638984 | tf_op jit(solution)/shard_map/ppermute | solution.py:669
  40.2 4.6 %collective-permute-start.16 = (bf16[4,16,1664]{2,1,0:T(8,128)(2,1)S(1)}, bf16[4,16,1664]{2,1,0:T(8,128)(2,1)}, u32[]{:S(2)}, u32[]{:S(2)}) collective-permute-start(bf16[4,16,1664]{2,1,0:T(8,128)(2,1)S(1)} %collective-permute-done.9.rest_3_), channel_id=1, source_target_pairs={{0,1},{1,0},{2,3},{3,2},{4,5},{5,4},{6,7},{7,6},{8,9},{9,8},{10,11... | collective-permute-start | bytes 638984 | tf_op jit(solution)/shard_map/ppermute | solution.py:669
  41.3 25.9 %collective-permute-start.10 = (bf16[4,16,4864]{2,1,0:T(8,128)(2,1)}, bf16[4,16,4864]{2,1,0:T(8,128)(2,1)S(1)}, u32[]{:S(2)}, u32[]{:S(2)}) collective-permute-start(bf16[4,16,4864]{2,1,0:T(8,128)(2,1)} %join.3.rest_0_), channel_id=1, source_target_pairs={{0,2},{1,3},{2,0},{3,1},{4,6},{5,7},{6,4},{7,5},{8,10},{9,11},{10,... | collective-permute-start | bytes 1867784 | tf_op jit(solution)/shard_map/ppermute | solution.py:669
  42.8 29.2 %collective-permute-start.11 = (bf16[4,16,4864]{2,1,0:T(8,128)(2,1)}, bf16[4,16,4864]{2,1,0:T(8,128)(2,1)S(1)}, u32[]{:S(2)}, u32[]{:S(2)}) collective-permute-start(bf16[4,16,4864]{2,1,0:T(8,128)(2,1)} %join.3.rest_0_), channel_id=1, source_target_pairs={{0,4},{4,0},{8,12},{12,8},{16,20},{20,16},{24,28},{28,24},{1,5},{5... | collective-permute-start | bytes 1867784 | tf_op jit(solution)/shard_map/ppermute | solution.py:669
  43.3 28.7 %collective-permute-start.12 = (bf16[4,16,4864]{2,1,0:T(8,128)(2,1)}, bf16[4,16,4864]{2,1,0:T(8,128)(2,1)S(1)}, u32[]{:S(2)}, u32[]{:S(2)}) collective-permute-start(bf16[4,16,4864]{2,1,0:T(8,128)(2,1)} %join.3.rest_0_), channel_id=1, source_target_pairs={{0,6},{1,7},{2,4},{3,5},{4,2},{5,3},{6,0},{7,1},{8,14},{9,15},{10,... | collective-permute-start | bytes 1867784 | tf_op jit(solution)/shard_map/ppermute | solution.py:677
  44.8 27.2 %collective-permute-start.17 = (bf16[4,16,4864]{2,1,0:T(8,128)(2,1)}, bf16[4,16,4864]{2,1,0:T(8,128)(2,1)S(1)}, u32[]{:S(2)}, u32[]{:S(2)}) collective-permute-start(bf16[4,16,4864]{2,1,0:T(8,128)(2,1)} %join.3.rest_0_), channel_id=1, source_target_pairs={{0,1},{1,0},{2,3},{3,2},{4,5},{5,4},{6,7},{7,6},{8,9},{9,8},{10,11... | collective-permute-start | bytes 1867784 | tf_op jit(solution)/shard_map/ppermute | solution.py:669
  67.2 8.8 %copy-start.11 = (bf16[4,16,4864]{2,1,0:T(8,128)(2,1)}, bf16[4,16,4864]{2,1,0:T(8,128)(2,1)S(1)}, u32[]{:S(2)}) copy-start(bf16[4,16,4864]{2,1,0:T(8,128)(2,1)S(1)} %collective-permute-done.10.rest_1_) | copy-start | bytes 1867780
  72.0 2.1 collective-permute-start.18
  72.1 3.8 %collective-permute-start.19 = (bf16[4,16,4864]{2,1,0:T(8,128)(2,1)S(1)}, bf16[4,16,4864]{2,1,0:T(8,128)(2,1)S(1)}, u32[]{:S(2)}, u32[]{:S(2)}) collective-permute-start(bf16[4,16,4864]{2,1,0:T(8,128)(2,1)S(1)} %collective-permute-done.11.rest_2_), channel_id=1, source_target_pairs={{0,1},{1,0},{2,3},{3,2},{4,5},{5,4},{6,7},{7,6},{8,9},{9,8},{10,11... | collective-permute-start | bytes 1867784 | tf_op jit(solution)/shard_map/ppermute | solution.py:669
  72.6 3.5 %collective-permute-start.20 = (bf16[4,16,4864]{2,1,0:T(8,128)(2,1)S(1)}, bf16[4,16,4864]{2,1,0:T(8,128)(2,1)}, u32[]{:S(2)}, u32[]{:S(2)}) collective-permute-start(bf16[4,16,4864]{2,1,0:T(8,128)(2,1)S(1)} %collective-permute-done.12.rest_3_), channel_id=1, source_target_pairs={{0,1},{1,0},{2,3},{3,2},{4,5},{5,4},{6,7},{7,6},{8,9},{9,8},{10,11... | collective-permute-start | bytes 1867784 | tf_op jit(solution)/shard_map/ppermute | solution.py:669
  159.5 25.3 %collective-permute-start.21 = (bf16[16,16,4864]{2,1,0:T(8,128)(2,1)}, bf16[16,16,4864]{2,1,0:T(8,128)(2,1)}, u32[]{:S(2)}, u32[]{:S(2)}) collective-permute-start(bf16[16,16,4864]{2,1,0:T(8,128)(2,1)} %get-tuple-element.120), channel_id=1, source_target_pairs={{0,1},{1,0},{2,3},{3,2},{4,5},{5,4},{6,7},{7,6},{8,9},{9,8},{10,11... | collective-permute-start | bytes 7471112 | tf_op jit(solution)/shard_map/ppermute | solution.py:669
  159.7 29.7 %collective-permute-start.22 = (bf16[4,256,512]{2,1,0:T(8,128)(2,1)}, bf16[4,256,512]{2,1,0:T(8,128)(2,1)S(1)}, u32[]{:S(2)}, u32[]{:S(2)}) collective-permute-start(bf16[4,256,512]{2,1,0:T(8,128)(2,1)} %get-tuple-element.121), channel_id=1, source_target_pairs={{0,1},{1,2},{2,3},{3,0},{4,5},{5,6},{6,7},{7,4},{8,9},{9,10},{10,1... | collective-permute-start | bytes 3145736 | tf_op jit(solution)/shard_map/ppermute | solution.py:27
  160.1 24.8 %copy-start.1 = (bf16[16,16,4864]{2,1,0:T(8,128)(2,1)S(1)}, bf16[16,16,4864]{2,1,0:T(8,128)(2,1)}, u32[]{:S(2)}) copy-start(bf16[16,16,4864]{2,1,0:T(8,128)(2,1)} %get-tuple-element.119) | copy-start | bytes 7471108
  190.4 28.9 %collective-permute-start.24 = (bf16[4,16,4864]{2,1,0:T(8,128)(2,1)}, bf16[4,16,4864]{2,1,0:T(8,128)(2,1)}, u32[]{:S(2)}, u32[]{:S(2)}) collective-permute-start(bf16[4,16,4864]{2,1,0:T(8,128)(2,1)} %get-tuple-element.140), channel_id=1, source_target_pairs={{0,2},{1,3},{2,0},{3,1},{4,6},{5,7},{6,4},{7,5},{8,10},{9,11},{10,... | collective-permute-start | bytes 1867784 | tf_op jit(solution)/shard_map/ppermute | solution.py:669
  191.1 30.1 %collective-permute-start.25 = (bf16[4,16,4864]{2,1,0:T(8,128)(2,1)S(1)}, bf16[4,16,4864]{2,1,0:T(8,128)(2,1)}, u32[]{:S(2)}, u32[]{:S(2)}) collective-permute-start(bf16[4,16,4864]{2,1,0:T(8,128)(2,1)S(1)} %get-tuple-element.142), channel_id=1, source_target_pairs={{0,4},{4,0},{8,12},{12,8},{16,20},{20,16},{24,28},{28,24},{1,5},{5... | collective-permute-start | bytes 1867784 | tf_op jit(solution)/shard_map/ppermute | solution.py:669
  192.1 29.1 %collective-permute-start.26 = (bf16[4,16,4864]{2,1,0:T(8,128)(2,1)S(1)}, bf16[4,16,4864]{2,1,0:T(8,128)(2,1)}, u32[]{:S(2)}, u32[]{:S(2)}) collective-permute-start(bf16[4,16,4864]{2,1,0:T(8,128)(2,1)S(1)} %get-tuple-element.141), channel_id=1, source_target_pairs={{0,6},{1,7},{2,4},{3,5},{4,2},{5,3},{6,0},{7,1},{8,14},{9,15},{10,... | collective-permute-start | bytes 1867784 | tf_op jit(solution)/shard_map/ppermute | solution.py:677
  193.9 37.8 %collective-permute-start.23 = (bf16[4,256,512]{2,1,0:T(8,128)(2,1)}, bf16[4,256,512]{2,1,0:T(8,128)(2,1)S(1)}, u32[]{:S(2)}, u32[]{:S(2)}) collective-permute-start(bf16[4,256,512]{2,1,0:T(8,128)(2,1)} %get-tuple-element.127), channel_id=1, source_target_pairs={{0,1},{1,2},{2,3},{3,0},{4,5},{5,6},{6,7},{7,4},{8,9},{9,10},{10,1... | collective-permute-start | bytes 3145736 | tf_op jit(solution)/shard_map/ppermute | solution.py:27
  219.3 8.2 %copy-start.2 = (bf16[16,16,1664]{2,1,0:T(8,128)(2,1)S(1)}, bf16[16,16,1664]{2,1,0:T(8,128)(2,1)}, u32[]{:S(2)}) copy-start(bf16[16,16,1664]{2,1,0:T(8,128)(2,1)} %get-tuple-element.132) | copy-start | bytes 2555908
  223.1 4.4 %collective-permute-start.30 = (bf16[16,16,1664]{2,1,0:T(8,128)(2,1)S(1)}, bf16[16,16,1664]{2,1,0:T(8,128)(2,1)S(1)}, u32[]{:S(2)}, u32[]{:S(2)}) collective-permute-start(bf16[16,16,1664]{2,1,0:T(8,128)(2,1)S(1)} %copy-done.10), channel_id=1, source_target_pairs={{0,1},{1,0},{2,3},{3,2},{4,5},{5,4},{6,7},{7,6},{8,9},{9,8},{10,11... | collective-permute-start | bytes 2555912 | tf_op jit(solution)/shard_map/ppermute | solution.py:669
  223.2 18.0 %collective-permute-start.27 = (bf16[16,4864]{1,0:T(8,128)(2,1)S(1)}, bf16[16,4864]{1,0:T(8,128)(2,1)S(1)}, u32[]{:S(2)}, u32[]{:S(2)}) collective-permute-start(bf16[16,4864]{1,0:T(8,128)(2,1)S(1)} %get-tuple-element.150), channel_id=1, source_target_pairs={{0,8},{4,12},{8,0},{12,4},{16,24},{20,28},{24,16},{28,20},{1,9},{5... | collective-permute-start | bytes 466952 | tf_op jit(solution)/shard_map/ppermute | solution.py:669
  224.9 16.4 %collective-permute-start.28 = (bf16[16,4864]{1,0:T(8,128)(2,1)S(1)}, bf16[16,4864]{1,0:T(8,128)(2,1)S(1)}, u32[]{:S(2)}, u32[]{:S(2)}) collective-permute-start(bf16[16,4864]{1,0:T(8,128)(2,1)S(1)} %get-tuple-element.149), channel_id=1, source_target_pairs={{0,16},{4,20},{8,24},{12,28},{16,0},{20,4},{24,8},{28,12},{1,17},{... | collective-permute-start | bytes 466952 | tf_op jit(solution)/shard_map/ppermute | solution.py:669
  227.8 8.3 %collective-permute-start.31 = (bf16[4,16,1664]{2,1,0:T(8,128)(2,1)S(1)}, bf16[4,16,1664]{2,1,0:T(8,128)(2,1)S(1)}, u32[]{:S(2)}, u32[]{:S(2)}) collective-permute-start(bf16[4,16,1664]{2,1,0:T(8,128)(2,1)S(1)} %get-tuple-element.145), channel_id=1, source_target_pairs={{0,2},{1,3},{2,0},{3,1},{4,6},{5,7},{6,4},{7,5},{8,10},{9,11},{10,... | collective-permute-start | bytes 638984 | tf_op jit(solution)/shard_map/ppermute | solution.py:669
  228.6 10.9 %collective-permute-start.32 = (bf16[4,16,1664]{2,1,0:T(8,128)(2,1)S(1)}, bf16[4,16,1664]{2,1,0:T(8,128)(2,1)S(1)}, u32[]{:S(2)}, u32[]{:S(2)}) collective-permute-start(bf16[4,16,1664]{2,1,0:T(8,128)(2,1)S(1)} %get-tuple-element.147), channel_id=1, source_target_pairs={{0,4},{4,0},{8,12},{12,8},{16,20},{20,16},{24,28},{28,24},{1,5},{5... | collective-permute-start | bytes 638984 | tf_op jit(solution)/shard_map/ppermute | solution.py:669
  231.7 9.4 %collective-permute-start.33 = (bf16[4,16,1664]{2,1,0:T(8,128)(2,1)S(1)}, bf16[4,16,1664]{2,1,0:T(8,128)(2,1)S(1)}, u32[]{:S(2)}, u32[]{:S(2)}) collective-permute-start(bf16[4,16,1664]{2,1,0:T(8,128)(2,1)S(1)} %get-tuple-element.146), channel_id=1, source_target_pairs={{0,6},{1,7},{2,4},{3,5},{4,2},{5,3},{6,0},{7,1},{8,14},{9,15},{10,... | collective-permute-start | bytes 638984 | tf_op jit(solution)/shard_map/ppermute | solution.py:677
  236.0 7.9 %collective-permute-start.29 = (bf16[16,4864]{1,0:T(8,128)(2,1)S(1)}, bf16[16,4864]{1,0:T(8,128)(2,1)S(1)}, u32[]{:S(2)}, u32[]{:S(2)}) collective-permute-start(bf16[16,4864]{1,0:T(8,128)(2,1)S(1)} %get-tuple-element.148), channel_id=1, source_target_pairs={{0,24},{4,28},{8,16},{12,20},{16,8},{20,12},{24,0},{28,4},{1,25},{... | collective-permute-start | bytes 466952 | tf_op jit(solution)/shard_map/ppermute | solution.py:669
  244.7 7.9 %collective-permute-start.34 = (bf16[16,1664]{1,0:T(8,128)(2,1)S(1)}, bf16[16,1664]{1,0:T(8,128)(2,1)S(1)}, u32[]{:S(2)}, u32[]{:S(2)}) collective-permute-start(bf16[16,1664]{1,0:T(8,128)(2,1)S(1)} %get-tuple-element.156), channel_id=1, source_target_pairs={{0,8},{4,12},{8,0},{12,4},{16,24},{20,28},{24,16},{28,20},{1,9},{5... | collective-permute-start | bytes 159752 | tf_op jit(solution)/shard_map/ppermute | solution.py:669
  247.6 6.2 %collective-permute-start.35 = (bf16[16,1664]{1,0:T(8,128)(2,1)S(1)}, bf16[16,1664]{1,0:T(8,128)(2,1)S(1)}, u32[]{:S(2)}, u32[]{:S(2)}) collective-permute-start(bf16[16,1664]{1,0:T(8,128)(2,1)S(1)} %get-tuple-element.158), channel_id=1, source_target_pairs={{0,16},{4,20},{8,24},{12,28},{16,0},{20,4},{24,8},{28,12},{1,17},{... | collective-permute-start | bytes 159752 | tf_op jit(solution)/shard_map/ppermute | solution.py:669
  248.8 6.0 %collective-permute-start.36 = (bf16[16,1664]{1,0:T(8,128)(2,1)S(1)}, bf16[16,1664]{1,0:T(8,128)(2,1)S(1)}, u32[]{:S(2)}, u32[]{:S(2)}) collective-permute-start(bf16[16,1664]{1,0:T(8,128)(2,1)S(1)} %get-tuple-element.157), channel_id=1, source_target_pairs={{0,24},{4,28},{8,16},{12,20},{16,8},{20,12},{24,0},{28,4},{1,25},{... | collective-permute-start | bytes 159752 | tf_op jit(solution)/shard_map/ppermute | solution.py:669
  (12 other events, 29.6 us)

commit v6 on v5

--- a/solution.py
+++ b/solution.py
@@ -385,25 +385,6 @@
             for i, (source, target) in enumerate(zip(earlier, loaded)):
                 pltpu.make_async_copy(source, target, sem.at[2 + i]).start()
 
-    items = [
-        (slice(w * CELLS, (w + 1) * CELLS), g * LANES)
-        for w in range(columns // WIN)
-        for g in range(width // LANES)
-    ]
-    items = [(r, at, slice(at, at + LANES)) for r, at in items]
-    diags = [block_diag(do_in[r, l]) for r, _, l in items]
-    dps = [dot_t(v_in[r, l], diag) for (r, _, l), diag in zip(items, diags)]
-    dvs = [dot(p_in[r, l], diag).astype(BF16) for (r, _, l), diag in zip(items, diags)]
-    dss = []
-    for (r, _, l), dp in zip(items, dps):
-        full = p_in[r, l].astype(F32)
-        dss.append((full * (dp - jnp.sum(dp * full, axis=0, keepdims=True))).astype(BF16))
-    dks = [dot(ds, block_diag(q_in[r, l])).astype(BF16) for (r, _, l), ds in zip(items, dss)]
-    dqs = [(dot_down(ds, k_in[r, l]) * 0.125).astype(BF16) for (r, _, l), ds in zip(items, dss)]
-    for (r, at, _), dq, dk, dv in zip(items, dqs, dks, dvs):
-        for part, grad in enumerate((dq, dk, dv)):
-            d_s[r, part * width + at : part * width + at + LANES] = grad
-
     @pl.when(local == 0)
     def _():
         wait_bytes(weight, sem.at[0])
@@ -417,10 +398,27 @@
     x = jnp.concatenate([top[...], bottom], axis=0).astype(F32)
     normed, inverse = normalize(to_window_order(x, columns))
     hidden = (normed * gain[...] + bias[...]).astype(BF16)
-    d = d_s[...]
-    dw[...] += dot(hidden.T, d)
-    small[0:1, :] += jnp.sum(d.astype(F32), axis=0, keepdims=True)
-    dh = dot_t(d, weight[...])
+    hidden_t = hidden.T
+    dh = jnp.zeros_like(normed)
+    for at in range(0, width, LANES):
+        l = slice(at, at + LANES)
+        items = [slice(w * CELLS, (w + 1) * CELLS) for w in range(columns // WIN)]
+        diags = [block_diag(do_in[r, l]) for r in items]
+        dps = [dot_t(v_in[r, l], diag) for r, diag in zip(items, diags)]
+        dvs = [dot(p_in[r, l], diag).astype(BF16) for r, diag in zip(items, diags)]
+        dss = []
+        for r, dp in zip(items, dps):
+            full = p_in[r, l].astype(F32)
+            dss.append((full * (dp - jnp.sum(dp * full, axis=0, keepdims=True))).astype(BF16))
+        dks = [dot(ds, block_diag(q_in[r, l])).astype(BF16) for r, ds in zip(items, dss)]
+        dqs = [(dot_down(ds, k_in[r, l]) * 0.125).astype(BF16) for r, ds in zip(items, dss)]
+        for part, grads in enumerate((dqs, dks, dvs)):
+            lane = slice(part * width + at, part * width + at + LANES)
+            d = jnp.concatenate(grads, axis=0)
+            dw[:, lane] += dot(hidden_t, d)
+            small[0:1, lane] += jnp.sum(d.astype(F32), axis=0, keepdims=True)
+            dh = dh + dot_t(d, weight[:, lane])
+
     small[1:2, :width] += jnp.sum(dh * normed, axis=0, keepdims=True)
     small[2:3, :width] += jnp.sum(dh, axis=0, keepdims=True)
     grad = dx_in[...] + norm_back(dh * gain[...], normed, inverse)

time: 257 us -> 257 us (level)
  no operation moved by 1% of the time
where the time goes in v6:
time: 257 us
  Pallas kernels  160 us (62%)
  starting transfers between devices  39.9 us (16%)
  waiting for transfers between devices  37.2 us (14%)
  local copies, waits for them, and re-layouts  12.9 us (5%)
  other arithmetic  5.97 us (2%)
    pallas_call x1, Pallas kernels, middle(): pl.pallas_call(functools.partial(middle_kernel, frames, columns, chunk),...  82.7 us
    pallas_call x2, Pallas kernels, back(): pl.pallas_call(functools.partial(back_kernel, frames, columns, first, cou...  49.2 us
    ppermute x30, waiting for transfers between devices, flipped(): return lax.ppermute(x, axis, flip_perm(axis, bits))  31.2 us
    ppermute x30, starting transfers between devices, flipped(): return lax.ppermute(x, axis, flip_perm(axis, bits))  29.9 us
    pallas_call x1, Pallas kernels, attend(): pl.pallas_call(functools.partial(attend_kernel, frames, columns, height,...  22.3 us
    ppermute x4, starting transfers between devices, flipped_both(): return lax.ppermute(x, AXES, pairs)  7.25 us
  transfers between devices with their start and end apart: 37, of which 16 were waited for; matrix products, arithmetic and copies ran while one was open for 4% of the time, Pallas kernels for 30%

profile of v6, /device:TPU:0, one launch (start us, length us, event | category | flops | bytes accessed | tf_op | source)
XLA Modules:
  0.0 256.7 jit_solution(2905406964062060266)
XLA Ops:
  0.6 1.8 slice_bitcast_fusion
  2.6 2.4 collective-permute-start.6
  5.1 1.8 pack.1
  6.9 1.6 collective-permute-start
  8.5 2.6 %collective-permute-start.1 = (bf16[16,1664]{1,0:T(8,128)(2,1)}, bf16[16,1664]{1,0:T(8,128)(2,1)S(1)}, u32[]{:S(2)}, u32[]{:S(2)}) collective-permute-start(bf16[16,1664]{1,0:T(8,128)(2,1)} %get-tuple-element.90), channel_id=1, source_target_pairs={{0,16},{4,20},{8,24},{12,28},{16,0},{20,4},{24,8},{28,12},{1,17},{... | collective-permute-start | bytes 159752 | tf_op jit(solution)/shard_map/ppermute | solution.py:667
  11.3 3.2 %collective-permute-done.1 = bf16[16,1664]{1,0:T(8,128)(2,1)S(1)} collective-permute-done((bf16[16,1664]{1,0:T(8,128)(2,1)}, bf16[16,1664]{1,0:T(8,128)(2,1)S(1)}, u32[]{:S(2)}, u32[]{:S(2)}) %collective-permute-start.1) | collective-permute-done | bytes 53280 | tf_op jit(solution)/shard_map/ppermute | solution.py:667
  14.5 2.7 %collective-permute-done.2 = bf16[16,1664]{1,0:T(8,128)(2,1)S(1)} collective-permute-done((bf16[16,1664]{1,0:T(8,128)(2,1)}, bf16[16,1664]{1,0:T(8,128)(2,1)S(1)}, u32[]{:S(2)}, u32[]{:S(2)}) %collective-permute-start.2) | collective-permute-done | bytes 53280 | tf_op jit(solution)/shard_map/ppermute | solution.py:667
  17.2 1.4 collective-permute-start.4
  18.6 1.6 join.2.rest_0_
  20.1 1.5 collective-permute-start.7
  21.6 1.5 collective-permute-start.8
  23.2 1.1 collective-permute-done.3
  24.3 2.8 %collective-permute-start.9 = (bf16[4,16,1664]{2,1,0:T(8,128)(2,1)}, bf16[4,16,1664]{2,1,0:T(8,128)(2,1)S(1)}, u32[]{:S(2)}, u32[]{:S(2)}) collective-permute-start(bf16[4,16,1664]{2,1,0:T(8,128)(2,1)} %join.2.rest_0_), channel_id=1, source_target_pairs={{0,6},{1,7},{2,4},{3,5},{4,2},{5,3},{6,0},{7,1},{8,14},{9,15},{10,... | collective-permute-start | bytes 638984 | tf_op jit(solution)/shard_map/ppermute | solution.py:675
  27.4 7.0 %collective-permute-done.5 = bf16[16,4864]{1,0:T(8,128)(2,1)S(1)} collective-permute-done((bf16[16,4864]{1,0:T(8,128)(2,1)}, bf16[16,4864]{1,0:T(8,128)(2,1)S(1)}, u32[]{:S(2)}, u32[]{:S(2)}) %collective-permute-start.5) | collective-permute-done | bytes 155680 | tf_op jit(solution)/shard_map/ppermute | solution.py:667
  35.1 2.0 join.3.rest_0_
  37.2 2.6 collective-permute-done.9.rest_3_
  41.3 1.5 collective-permute-start.10
  43.3 1.5 collective-permute-start.12
  44.9 22.3 %attend.1 = (bf16[8,512,512]{2,1,0:T(8,128)(2,1)}, bf16[8,512,512]{2,1,0:T(8,128)(2,1)}, bf16[8,512,512]{2,1,0:T(8,128)(2,1)}, bf16[8,512,512]{2,1,0:T(8,128)(2,1)}, bf16[8,512,512]{2,1,0:T(8,128)(2,1)}) custom-call(s32[6]{0:T(128)} %pad_add_fusion.info, bf16[4,4,256,512]{3,2,1,0:T(8,128)(2,1)} %bitcast.53, bf16[4,4,256,512]{3,2,1,0:T(8,128)(2,1)} %bitcast.54, ...), custom_call_target="tpu_custom_call" | custom-call | flops 30000001024 | bytes 30000000 | tf_op jit(solution)/shard_map/attend/pallas_call | solution.py:545
  67.3 4.8 %collective-permute-done.11.rest_2_ = bf16[4,16,4864]{2,1,0:T(8,128)(2,1)S(1)} collective-permute-done((bf16[4,16,4864]{2,1,0:T(8,128)(2,1)}, bf16[4,16,4864]{2,1,0:T(8,128)(2,1)S(1)}, u32[]{:S(2)}, u32[]{:S(2)}) %collective-permute-start.11) | collective-permute-done | bytes 622624 | tf_op jit(solution)/shard_map/ppermute | solution.py:667
  72.7 1.5 collective-permute-done.18.rest_5_
  74.2 1.8 collective-permute-done.19.rest_6_
  76.8 82.7 %middle.1 = (bf16[4,4,256,512]{3,2,1,0:T(8,128)(2,1)}, bf16[4,256,512]{2,1,0:T(8,128)(2,1)}, f32[8,512,512]{2,1,0:T(8,128)}, bf16[8,512,512]{2,1,0:T(8,128)(2,1)...) custom-call(s32[6]{0:T(128)} %pad_add_fusion.info, bf16[4,4,256,512]{3,2,1,0:T(8,128)(2,1)} %bitcast.55, ...), custom_call_target="tpu_custom_call" | custom-call | flops 89999998976 | bytes 40000000 | tf_op jit(solution)/shard_map/middle/pallas_call | solution.py:573
  160.1 24.8 %back.2 = (bf16[4,4,256,512]{3,2,1,0:T(8,128)(2,1)}, bf16[4,256,512]{2,1,0:T(8,128)(2,1)}, f32[512,1536]{1,0:T(8,128)}, f32[8,1536]{1,0:T(8,128)}) custom-call(s32[6]{0:T(128)} %pad_add_fusion.info, bf16[4,4,256,512]{3,2,1,0:T(8,128)(2,1)} %bitcast.57, bf16[4,4,256,512]{3,2,1,0:T(8,128)(2,1)} %bitcast.58, ...), custom_call_target="tpu_custom_call" | custom-call | flops 24000000000 | bytes 20000000 | tf_op jit(solution)/shard_map/back/pallas_call | solution.py:626
  184.9 2.3 convert_add_fusion
  187.4 2.0 copy-done
  189.4 1.0 fusion.3
  191.1 1.0 collective-permute-start.25
  192.1 1.8 collective-permute-start.26
  193.9 24.4 %back.3 = (bf16[4,4,256,512]{3,2,1,0:T(8,128)(2,1)}, bf16[16,16,1664]{2,1,0:T(8,128)(2,1)}, bf16[16,16,1664]{2,1,0:T(8,128)(2,1)}) custom-call(s32[6]{0:T(128)} %pad_add_fusion.info, bf16[4,4,256,512]{3,2,1,0:T(8,128)(2,1)} %bitcast.59, bf16[4,4,256,512]{3,2,1,0:T(8,128)(2,1)} %bitcast.60, ...), custom_call_target="tpu_custom_call", output_to_operand_aliasing={{0}: (18, {})} | custom-call | flops 24000000000 | bytes 20000000 | tf_op jit(solution)/shard_map/back/pallas_call | solution.py:626
  218.3 1.0 bitcast_dynamic-update-slice_fusion
  219.3 1.9 collective-permute-done.25
  221.3 1.7 convert_add_fusion.2
  223.2 1.6 collective-permute-start.27
  224.9 2.6 %collective-permute-start.28 = (bf16[16,4864]{1,0:T(8,128)(2,1)S(1)}, bf16[16,4864]{1,0:T(8,128)(2,1)S(1)}, u32[]{:S(2)}, u32[]{:S(2)}) collective-permute-start(bf16[16,4864]{1,0:T(8,128)(2,1)S(1)} %get-tuple-element.149), channel_id=1, source_target_pairs={{0,16},{4,20},{8,24},{12,28},{16,0},{20,4},{24,8},{28,12},{1,17},{... | collective-permute-start | bytes 466952 | tf_op jit(solution)/shard_map/ppermute | solution.py:667
  228.6 1.2 collective-permute-start.32
  229.8 1.9 collective-permute-done.23
  231.7 1.2 collective-permute-start.33
  232.9 1.0 bitcast_dynamic-update-slice_fusion.1
  233.9 2.1 collective-permute-done.31
  236.0 3.5 %collective-permute-start.29 = (bf16[16,4864]{1,0:T(8,128)(2,1)S(1)}, bf16[16,4864]{1,0:T(8,128)(2,1)S(1)}, u32[]{:S(2)}, u32[]{:S(2)}) collective-permute-start(bf16[16,4864]{1,0:T(8,128)(2,1)S(1)} %get-tuple-element.148), channel_id=1, source_target_pairs={{0,24},{4,28},{8,16},{12,20},{16,8},{20,12},{24,0},{28,4},{1,25},{... | collective-permute-start | bytes 466952 | tf_op jit(solution)/shard_map/ppermute | solution.py:667
  239.6 1.6 collective-permute-done.33
  241.3 2.7 %collective-permute-done.29 = bf16[16,4864]{1,0:T(8,128)(2,1)S(1)} collective-permute-done((bf16[16,4864]{1,0:T(8,128)(2,1)S(1)}, bf16[16,4864]{1,0:T(8,128)(2,1)S(1)}, u32[]{:S(2)}, u32[]{:S(2)}) %collective-permute-start.29) | collective-permute-done | bytes 155680 | tf_op jit(solution)/shard_map/ppermute | solution.py:667
  244.7 2.9 %collective-permute-start.34 = (bf16[16,1664]{1,0:T(8,128)(2,1)S(1)}, bf16[16,1664]{1,0:T(8,128)(2,1)S(1)}, u32[]{:S(2)}, u32[]{:S(2)}) collective-permute-start(bf16[16,1664]{1,0:T(8,128)(2,1)S(1)} %get-tuple-element.156), channel_id=1, source_target_pairs={{0,8},{4,12},{8,0},{12,4},{16,24},{20,28},{24,16},{28,20},{1,9},{5... | collective-permute-start | bytes 159752 | tf_op jit(solution)/shard_map/ppermute | solution.py:667
  247.6 1.2 collective-permute-start.35
  248.8 1.3 collective-permute-start.36
  252.6 1.2 collective-permute-done.35
  253.9 1.0 collective-permute-done.36
  (110 shorter events, 13.1 us)
Async XLA Ops:
  2.4 38.3 %copy-start.9 = (s32[4]{0:T(128)S(1)}, s32[4]{0:T(128)}, u32[]{:S(2)}) copy-start(s32[4]{0:T(128)} %param.20) | copy-start | bytes 52
  2.6 31.8 %collective-permute-start.6 = (bf16[2,4,256,512]{3,2,1,0:T(8,128)(2,1)S(1)}, bf16[2,4,256,512]{3,2,1,0:T(8,128)(2,1)}, u32[]{:S(2)}, u32[]{:S(2)}) collective-permute-start(bf16[2,4,256,512]{3,2,1,0:T(8,128)(2,1)S(1)} %pad_maximum_fusion), channel_id=1, source_target_pairs={{0,3},{1,0},{2,1},{3,2},{4,7},{5,4},{6,5},{7,6},{8,11},{9,8},{10,9... | collective-permute-start | bytes 6291464 | tf_op jit(solution)/shard_map/ppermute | solution.py:27
  6.9 4.4 %collective-permute-start = (bf16[16,1664]{1,0:T(8,128)(2,1)}, bf16[16,1664]{1,0:T(8,128)(2,1)S(1)}, u32[]{:S(2)}, u32[]{:S(2)}) collective-permute-start(bf16[16,1664]{1,0:T(8,128)(2,1)} %get-tuple-element.90), channel_id=1, source_target_pairs={{0,8},{4,12},{8,0},{12,4},{16,24},{20,28},{24,16},{28,20},{1,9},{5... | collective-permute-start | bytes 159752 | tf_op jit(solution)/shard_map/ppermute | solution.py:667
  8.5 6.0 %collective-permute-start.1 = (bf16[16,1664]{1,0:T(8,128)(2,1)}, bf16[16,1664]{1,0:T(8,128)(2,1)S(1)}, u32[]{:S(2)}, u32[]{:S(2)}) collective-permute-start(bf16[16,1664]{1,0:T(8,128)(2,1)} %get-tuple-element.90), channel_id=1, source_target_pairs={{0,16},{4,20},{8,24},{12,28},{16,0},{20,4},{24,8},{28,12},{1,17},{... | collective-permute-start | bytes 159752 | tf_op jit(solution)/shard_map/ppermute | solution.py:667
  11.0 6.1 %collective-permute-start.2 = (bf16[16,1664]{1,0:T(8,128)(2,1)}, bf16[16,1664]{1,0:T(8,128)(2,1)S(1)}, u32[]{:S(2)}, u32[]{:S(2)}) collective-permute-start(bf16[16,1664]{1,0:T(8,128)(2,1)} %get-tuple-element.90), channel_id=1, source_target_pairs={{0,24},{4,28},{8,16},{12,20},{16,8},{20,12},{24,0},{28,4},{1,25},{... | collective-permute-start | bytes 159752 | tf_op jit(solution)/shard_map/ppermute | solution.py:667
  11.3 7.3 %copy-start.6 = (bf16[16,1664]{1,0:T(8,128)(2,1)}, bf16[16,1664]{1,0:T(8,128)(2,1)S(1)}, u32[]{:S(2)}) copy-start(bf16[16,1664]{1,0:T(8,128)(2,1)S(1)} %collective-permute-done) | copy-start | bytes 159748
  14.5 4.1 %copy-start.7 = (bf16[16,1664]{1,0:T(8,128)(2,1)}, bf16[16,1664]{1,0:T(8,128)(2,1)S(1)}, u32[]{:S(2)}) copy-start(bf16[16,1664]{1,0:T(8,128)(2,1)S(1)} %collective-permute-done.1) | copy-start | bytes 159748
  17.2 7.1 %collective-permute-start.3 = (bf16[16,4864]{1,0:T(8,128)(2,1)}, bf16[16,4864]{1,0:T(8,128)(2,1)S(1)}, u32[]{:S(2)}, u32[]{:S(2)}) collective-permute-start(bf16[16,4864]{1,0:T(8,128)(2,1)} %get-tuple-element.91), channel_id=1, source_target_pairs={{0,8},{4,12},{8,0},{12,4},{16,24},{20,28},{24,16},{28,20},{1,9},{5... | collective-permute-start | bytes 466952 | tf_op jit(solution)/shard_map/ppermute | solution.py:667
  17.2 9.9 %collective-permute-start.4 = (bf16[16,4864]{1,0:T(8,128)(2,1)}, bf16[16,4864]{1,0:T(8,128)(2,1)S(1)}, u32[]{:S(2)}, u32[]{:S(2)}) collective-permute-start(bf16[16,4864]{1,0:T(8,128)(2,1)} %get-tuple-element.91), channel_id=1, source_target_pairs={{0,16},{4,20},{8,24},{12,28},{16,0},{20,4},{24,8},{28,12},{1,17},{... | collective-permute-start | bytes 466952 | tf_op jit(solution)/shard_map/ppermute | solution.py:667
  20.1 17.0 %collective-permute-start.7 = (bf16[4,16,1664]{2,1,0:T(8,128)(2,1)}, bf16[4,16,1664]{2,1,0:T(8,128)(2,1)S(1)}, u32[]{:S(2)}, u32[]{:S(2)}) collective-permute-start(bf16[4,16,1664]{2,1,0:T(8,128)(2,1)} %join.2.rest_0_), channel_id=1, source_target_pairs={{0,2},{1,3},{2,0},{3,1},{4,6},{5,7},{6,4},{7,5},{8,10},{9,11},{10,... | collective-permute-start | bytes 638984 | tf_op jit(solution)/shard_map/ppermute | solution.py:667
  21.6 15.5 %collective-permute-start.8 = (bf16[4,16,1664]{2,1,0:T(8,128)(2,1)}, bf16[4,16,1664]{2,1,0:T(8,128)(2,1)S(1)}, u32[]{:S(2)}, u32[]{:S(2)}) collective-permute-start(bf16[4,16,1664]{2,1,0:T(8,128)(2,1)} %join.2.rest_0_), channel_id=1, source_target_pairs={{0,4},{4,0},{8,12},{12,8},{16,20},{20,16},{24,28},{28,24},{1,5},{5... | collective-permute-start | bytes 638984 | tf_op jit(solution)/shard_map/ppermute | solution.py:667
  24.3 10.2 %copy-start.3 = (bf16[16,4864]{1,0:T(8,128)(2,1)}, bf16[16,4864]{1,0:T(8,128)(2,1)S(1)}, u32[]{:S(2)}) copy-start(bf16[16,4864]{1,0:T(8,128)(2,1)S(1)} %collective-permute-done.3) | copy-start | bytes 466948
  24.3 15.4 %collective-permute-start.9 = (bf16[4,16,1664]{2,1,0:T(8,128)(2,1)}, bf16[4,16,1664]{2,1,0:T(8,128)(2,1)S(1)}, u32[]{:S(2)}, u32[]{:S(2)}) collective-permute-start(bf16[4,16,1664]{2,1,0:T(8,128)(2,1)} %join.2.rest_0_), channel_id=1, source_target_pairs={{0,6},{1,7},{2,4},{3,5},{4,2},{5,3},{6,0},{7,1},{8,14},{9,15},{10,... | collective-permute-start | bytes 638984 | tf_op jit(solution)/shard_map/ppermute | solution.py:675
  27.1 7.4 %copy-start.4 = (bf16[16,4864]{1,0:T(8,128)(2,1)}, bf16[16,4864]{1,0:T(8,128)(2,1)S(1)}, u32[]{:S(2)}) copy-start(bf16[16,4864]{1,0:T(8,128)(2,1)S(1)} %collective-permute-done.4) | copy-start | bytes 466948
  27.1 7.3 %collective-permute-start.5 = (bf16[16,4864]{1,0:T(8,128)(2,1)}, bf16[16,4864]{1,0:T(8,128)(2,1)S(1)}, u32[]{:S(2)}, u32[]{:S(2)}) collective-permute-start(bf16[16,4864]{1,0:T(8,128)(2,1)} %get-tuple-element.91), channel_id=1, source_target_pairs={{0,24},{4,28},{8,16},{12,20},{16,8},{20,12},{24,0},{28,4},{1,25},{... | collective-permute-start | bytes 466952 | tf_op jit(solution)/shard_map/ppermute | solution.py:667
  37.1 7.7 %copy-start.17 = (bf16[4,16,1664]{2,1,0:T(8,128)(2,1)}, bf16[4,16,1664]{2,1,0:T(8,128)(2,1)S(1)}, u32[]{:S(2)}) copy-start(bf16[4,16,1664]{2,1,0:T(8,128)(2,1)S(1)} %collective-permute-done.7.rest_1_) | copy-start | bytes 638980
  37.1 7.7 %copy-start.18 = (bf16[4,16,1664]{2,1,0:T(8,128)(2,1)}, bf16[4,16,1664]{2,1,0:T(8,128)(2,1)S(1)}, u32[]{:S(2)}) copy-start(bf16[4,16,1664]{2,1,0:T(8,128)(2,1)S(1)} %collective-permute-done.8.rest_2_) | copy-start | bytes 638980
  39.7 5.1 %copy-start.19 = (bf16[4,16,1664]{2,1,0:T(8,128)(2,1)}, bf16[4,16,1664]{2,1,0:T(8,128)(2,1)S(1)}, u32[]{:S(2)}) copy-start(bf16[4,16,1664]{2,1,0:T(8,128)(2,1)S(1)} %collective-permute-done.9.rest_3_) | copy-start | bytes 638980
  39.7 3.1 %collective-permute-start.13 = (bf16[4,16,1664]{2,1,0:T(8,128)(2,1)}, bf16[4,16,1664]{2,1,0:T(8,128)(2,1)S(1)}, u32[]{:S(2)}, u32[]{:S(2)}) collective-permute-start(bf16[4,16,1664]{2,1,0:T(8,128)(2,1)} %join.2.rest_0_), channel_id=1, source_target_pairs={{0,1},{1,0},{2,3},{3,2},{4,5},{5,4},{6,7},{7,6},{8,9},{9,8},{10,11... | collective-permute-start | bytes 638984 | tf_op jit(solution)/shard_map/ppermute | solution.py:667
  39.7 3.6 %collective-permute-start.14 = (bf16[4,16,1664]{2,1,0:T(8,128)(2,1)S(1)}, bf16[4,16,1664]{2,1,0:T(8,128)(2,1)S(1)}, u32[]{:S(2)}, u32[]{:S(2)}) collective-permute-start(bf16[4,16,1664]{2,1,0:T(8,128)(2,1)S(1)} %collective-permute-done.7.rest_1_), channel_id=1, source_target_pairs={{0,1},{1,0},{2,3},{3,2},{4,5},{5,4},{6,7},{7,6},{8,9},{9,8},{10,11... | collective-permute-start | bytes 638984 | tf_op jit(solution)/shard_map/ppermute | solution.py:667
  40.2 4.6 %collective-permute-start.15 = (bf16[4,16,1664]{2,1,0:T(8,128)(2,1)S(1)}, bf16[4,16,1664]{2,1,0:T(8,128)(2,1)}, u32[]{:S(2)}, u32[]{:S(2)}) collective-permute-start(bf16[4,16,1664]{2,1,0:T(8,128)(2,1)S(1)} %collective-permute-done.8.rest_2_), channel_id=1, source_target_pairs={{0,1},{1,0},{2,3},{3,2},{4,5},{5,4},{6,7},{7,6},{8,9},{9,8},{10,11... | collective-permute-start | bytes 638984 | tf_op jit(solution)/shard_map/ppermute | solution.py:667
  40.2 4.6 %collective-permute-start.16 = (bf16[4,16,1664]{2,1,0:T(8,128)(2,1)S(1)}, bf16[4,16,1664]{2,1,0:T(8,128)(2,1)}, u32[]{:S(2)}, u32[]{:S(2)}) collective-permute-start(bf16[4,16,1664]{2,1,0:T(8,128)(2,1)S(1)} %collective-permute-done.9.rest_3_), channel_id=1, source_target_pairs={{0,1},{1,0},{2,3},{3,2},{4,5},{5,4},{6,7},{7,6},{8,9},{9,8},{10,11... | collective-permute-start | bytes 638984 | tf_op jit(solution)/shard_map/ppermute | solution.py:667
  41.3 25.9 %collective-permute-start.10 = (bf16[4,16,4864]{2,1,0:T(8,128)(2,1)}, bf16[4,16,4864]{2,1,0:T(8,128)(2,1)S(1)}, u32[]{:S(2)}, u32[]{:S(2)}) collective-permute-start(bf16[4,16,4864]{2,1,0:T(8,128)(2,1)} %join.3.rest_0_), channel_id=1, source_target_pairs={{0,2},{1,3},{2,0},{3,1},{4,6},{5,7},{6,4},{7,5},{8,10},{9,11},{10,... | collective-permute-start | bytes 1867784 | tf_op jit(solution)/shard_map/ppermute | solution.py:667
  42.8 29.2 %collective-permute-start.11 = (bf16[4,16,4864]{2,1,0:T(8,128)(2,1)}, bf16[4,16,4864]{2,1,0:T(8,128)(2,1)S(1)}, u32[]{:S(2)}, u32[]{:S(2)}) collective-permute-start(bf16[4,16,4864]{2,1,0:T(8,128)(2,1)} %join.3.rest_0_), channel_id=1, source_target_pairs={{0,4},{4,0},{8,12},{12,8},{16,20},{20,16},{24,28},{28,24},{1,5},{5... | collective-permute-start | bytes 1867784 | tf_op jit(solution)/shard_map/ppermute | solution.py:667
  43.3 28.7 %collective-permute-start.12 = (bf16[4,16,4864]{2,1,0:T(8,128)(2,1)}, bf16[4,16,4864]{2,1,0:T(8,128)(2,1)S(1)}, u32[]{:S(2)}, u32[]{:S(2)}) collective-permute-start(bf16[4,16,4864]{2,1,0:T(8,128)(2,1)} %join.3.rest_0_), channel_id=1, source_target_pairs={{0,6},{1,7},{2,4},{3,5},{4,2},{5,3},{6,0},{7,1},{8,14},{9,15},{10,... | collective-permute-start | bytes 1867784 | tf_op jit(solution)/shard_map/ppermute | solution.py:675
  44.8 27.2 %collective-permute-start.17 = (bf16[4,16,4864]{2,1,0:T(8,128)(2,1)}, bf16[4,16,4864]{2,1,0:T(8,128)(2,1)S(1)}, u32[]{:S(2)}, u32[]{:S(2)}) collective-permute-start(bf16[4,16,4864]{2,1,0:T(8,128)(2,1)} %join.3.rest_0_), channel_id=1, source_target_pairs={{0,1},{1,0},{2,3},{3,2},{4,5},{5,4},{6,7},{7,6},{8,9},{9,8},{10,11... | collective-permute-start | bytes 1867784 | tf_op jit(solution)/shard_map/ppermute | solution.py:667
  67.2 8.8 %copy-start.11 = (bf16[4,16,4864]{2,1,0:T(8,128)(2,1)}, bf16[4,16,4864]{2,1,0:T(8,128)(2,1)S(1)}, u32[]{:S(2)}) copy-start(bf16[4,16,4864]{2,1,0:T(8,128)(2,1)S(1)} %collective-permute-done.10.rest_1_) | copy-start | bytes 1867780
  72.0 2.1 collective-permute-start.18
  72.1 3.8 %collective-permute-start.19 = (bf16[4,16,4864]{2,1,0:T(8,128)(2,1)S(1)}, bf16[4,16,4864]{2,1,0:T(8,128)(2,1)S(1)}, u32[]{:S(2)}, u32[]{:S(2)}) collective-permute-start(bf16[4,16,4864]{2,1,0:T(8,128)(2,1)S(1)} %collective-permute-done.11.rest_2_), channel_id=1, source_target_pairs={{0,1},{1,0},{2,3},{3,2},{4,5},{5,4},{6,7},{7,6},{8,9},{9,8},{10,11... | collective-permute-start | bytes 1867784 | tf_op jit(solution)/shard_map/ppermute | solution.py:667
  72.6 3.5 %collective-permute-start.20 = (bf16[4,16,4864]{2,1,0:T(8,128)(2,1)S(1)}, bf16[4,16,4864]{2,1,0:T(8,128)(2,1)}, u32[]{:S(2)}, u32[]{:S(2)}) collective-permute-start(bf16[4,16,4864]{2,1,0:T(8,128)(2,1)S(1)} %collective-permute-done.12.rest_3_), channel_id=1, source_target_pairs={{0,1},{1,0},{2,3},{3,2},{4,5},{5,4},{6,7},{7,6},{8,9},{9,8},{10,11... | collective-permute-start | bytes 1867784 | tf_op jit(solution)/shard_map/ppermute | solution.py:667
  159.5 25.4 %collective-permute-start.21 = (bf16[16,16,4864]{2,1,0:T(8,128)(2,1)}, bf16[16,16,4864]{2,1,0:T(8,128)(2,1)}, u32[]{:S(2)}, u32[]{:S(2)}) collective-permute-start(bf16[16,16,4864]{2,1,0:T(8,128)(2,1)} %get-tuple-element.120), channel_id=1, source_target_pairs={{0,1},{1,0},{2,3},{3,2},{4,5},{5,4},{6,7},{7,6},{8,9},{9,8},{10,11... | collective-permute-start | bytes 7471112 | tf_op jit(solution)/shard_map/ppermute | solution.py:667
  159.7 29.7 %collective-permute-start.22 = (bf16[4,256,512]{2,1,0:T(8,128)(2,1)}, bf16[4,256,512]{2,1,0:T(8,128)(2,1)S(1)}, u32[]{:S(2)}, u32[]{:S(2)}) collective-permute-start(bf16[4,256,512]{2,1,0:T(8,128)(2,1)} %get-tuple-element.121), channel_id=1, source_target_pairs={{0,1},{1,2},{2,3},{3,0},{4,5},{5,6},{6,7},{7,4},{8,9},{9,10},{10,1... | collective-permute-start | bytes 3145736 | tf_op jit(solution)/shard_map/ppermute | solution.py:27
  160.1 24.8 %copy-start.1 = (bf16[16,16,4864]{2,1,0:T(8,128)(2,1)S(1)}, bf16[16,16,4864]{2,1,0:T(8,128)(2,1)}, u32[]{:S(2)}) copy-start(bf16[16,16,4864]{2,1,0:T(8,128)(2,1)} %get-tuple-element.119) | copy-start | bytes 7471108
  190.4 28.9 %collective-permute-start.24 = (bf16[4,16,4864]{2,1,0:T(8,128)(2,1)}, bf16[4,16,4864]{2,1,0:T(8,128)(2,1)}, u32[]{:S(2)}, u32[]{:S(2)}) collective-permute-start(bf16[4,16,4864]{2,1,0:T(8,128)(2,1)} %get-tuple-element.140), channel_id=1, source_target_pairs={{0,2},{1,3},{2,0},{3,1},{4,6},{5,7},{6,4},{7,5},{8,10},{9,11},{10,... | collective-permute-start | bytes 1867784 | tf_op jit(solution)/shard_map/ppermute | solution.py:667
  191.1 30.1 %collective-permute-start.25 = (bf16[4,16,4864]{2,1,0:T(8,128)(2,1)S(1)}, bf16[4,16,4864]{2,1,0:T(8,128)(2,1)}, u32[]{:S(2)}, u32[]{:S(2)}) collective-permute-start(bf16[4,16,4864]{2,1,0:T(8,128)(2,1)S(1)} %get-tuple-element.142), channel_id=1, source_target_pairs={{0,4},{4,0},{8,12},{12,8},{16,20},{20,16},{24,28},{28,24},{1,5},{5... | collective-permute-start | bytes 1867784 | tf_op jit(solution)/shard_map/ppermute | solution.py:667
  192.1 29.2 %collective-permute-start.26 = (bf16[4,16,4864]{2,1,0:T(8,128)(2,1)S(1)}, bf16[4,16,4864]{2,1,0:T(8,128)(2,1)}, u32[]{:S(2)}, u32[]{:S(2)}) collective-permute-start(bf16[4,16,4864]{2,1,0:T(8,128)(2,1)S(1)} %get-tuple-element.141), channel_id=1, source_target_pairs={{0,6},{1,7},{2,4},{3,5},{4,2},{5,3},{6,0},{7,1},{8,14},{9,15},{10,... | collective-permute-start | bytes 1867784 | tf_op jit(solution)/shard_map/ppermute | solution.py:675
  193.9 37.8 %collective-permute-start.23 = (bf16[4,256,512]{2,1,0:T(8,128)(2,1)}, bf16[4,256,512]{2,1,0:T(8,128)(2,1)S(1)}, u32[]{:S(2)}, u32[]{:S(2)}) collective-permute-start(bf16[4,256,512]{2,1,0:T(8,128)(2,1)} %get-tuple-element.127), channel_id=1, source_target_pairs={{0,1},{1,2},{2,3},{3,0},{4,5},{5,6},{6,7},{7,4},{8,9},{9,10},{10,1... | collective-permute-start | bytes 3145736 | tf_op jit(solution)/shard_map/ppermute | solution.py:27
  219.3 8.1 %copy-start.2 = (bf16[16,16,1664]{2,1,0:T(8,128)(2,1)S(1)}, bf16[16,16,1664]{2,1,0:T(8,128)(2,1)}, u32[]{:S(2)}) copy-start(bf16[16,16,1664]{2,1,0:T(8,128)(2,1)} %get-tuple-element.132) | copy-start | bytes 2555908
  223.1 4.4 %collective-permute-start.30 = (bf16[16,16,1664]{2,1,0:T(8,128)(2,1)S(1)}, bf16[16,16,1664]{2,1,0:T(8,128)(2,1)S(1)}, u32[]{:S(2)}, u32[]{:S(2)}) collective-permute-start(bf16[16,16,1664]{2,1,0:T(8,128)(2,1)S(1)} %copy-done.10), channel_id=1, source_target_pairs={{0,1},{1,0},{2,3},{3,2},{4,5},{5,4},{6,7},{7,6},{8,9},{9,8},{10,11... | collective-permute-start | bytes 2555912 | tf_op jit(solution)/shard_map/ppermute | solution.py:667
  223.2 18.0 %collective-permute-start.27 = (bf16[16,4864]{1,0:T(8,128)(2,1)S(1)}, bf16[16,4864]{1,0:T(8,128)(2,1)S(1)}, u32[]{:S(2)}, u32[]{:S(2)}) collective-permute-start(bf16[16,4864]{1,0:T(8,128)(2,1)S(1)} %get-tuple-element.150), channel_id=1, source_target_pairs={{0,8},{4,12},{8,0},{12,4},{16,24},{20,28},{24,16},{28,20},{1,9},{5... | collective-permute-start | bytes 466952 | tf_op jit(solution)/shard_map/ppermute | solution.py:667
  224.9 16.4 %collective-permute-start.28 = (bf16[16,4864]{1,0:T(8,128)(2,1)S(1)}, bf16[16,4864]{1,0:T(8,128)(2,1)S(1)}, u32[]{:S(2)}, u32[]{:S(2)}) collective-permute-start(bf16[16,4864]{1,0:T(8,128)(2,1)S(1)} %get-tuple-element.149), channel_id=1, source_target_pairs={{0,16},{4,20},{8,24},{12,28},{16,0},{20,4},{24,8},{28,12},{1,17},{... | collective-permute-start | bytes 466952 | tf_op jit(solution)/shard_map/ppermute | solution.py:667
  227.8 8.3 %collective-permute-start.31 = (bf16[4,16,1664]{2,1,0:T(8,128)(2,1)S(1)}, bf16[4,16,1664]{2,1,0:T(8,128)(2,1)S(1)}, u32[]{:S(2)}, u32[]{:S(2)}) collective-permute-start(bf16[4,16,1664]{2,1,0:T(8,128)(2,1)S(1)} %get-tuple-element.145), channel_id=1, source_target_pairs={{0,2},{1,3},{2,0},{3,1},{4,6},{5,7},{6,4},{7,5},{8,10},{9,11},{10,... | collective-permute-start | bytes 638984 | tf_op jit(solution)/shard_map/ppermute | solution.py:667
  228.6 10.9 %collective-permute-start.32 = (bf16[4,16,1664]{2,1,0:T(8,128)(2,1)S(1)}, bf16[4,16,1664]{2,1,0:T(8,128)(2,1)S(1)}, u32[]{:S(2)}, u32[]{:S(2)}) collective-permute-start(bf16[4,16,1664]{2,1,0:T(8,128)(2,1)S(1)} %get-tuple-element.147), channel_id=1, source_target_pairs={{0,4},{4,0},{8,12},{12,8},{16,20},{20,16},{24,28},{28,24},{1,5},{5... | collective-permute-start | bytes 638984 | tf_op jit(solution)/shard_map/ppermute | solution.py:667
  231.7 9.4 %collective-permute-start.33 = (bf16[4,16,1664]{2,1,0:T(8,128)(2,1)S(1)}, bf16[4,16,1664]{2,1,0:T(8,128)(2,1)S(1)}, u32[]{:S(2)}, u32[]{:S(2)}) collective-permute-start(bf16[4,16,1664]{2,1,0:T(8,128)(2,1)S(1)} %get-tuple-element.146), channel_id=1, source_target_pairs={{0,6},{1,7},{2,4},{3,5},{4,2},{5,3},{6,0},{7,1},{8,14},{9,15},{10,... | collective-permute-start | bytes 638984 | tf_op jit(solution)/shard_map/ppermute | solution.py:675
  236.0 7.9 %collective-permute-start.29 = (bf16[16,4864]{1,0:T(8,128)(2,1)S(1)}, bf16[16,4864]{1,0:T(8,128)(2,1)S(1)}, u32[]{:S(2)}, u32[]{:S(2)}) collective-permute-start(bf16[16,4864]{1,0:T(8,128)(2,1)S(1)} %get-tuple-element.148), channel_id=1, source_target_pairs={{0,24},{4,28},{8,16},{12,20},{16,8},{20,12},{24,0},{28,4},{1,25},{... | collective-permute-start | bytes 466952 | tf_op jit(solution)/shard_map/ppermute | solution.py:667
  244.7 7.9 %collective-permute-start.34 = (bf16[16,1664]{1,0:T(8,128)(2,1)S(1)}, bf16[16,1664]{1,0:T(8,128)(2,1)S(1)}, u32[]{:S(2)}, u32[]{:S(2)}) collective-permute-start(bf16[16,1664]{1,0:T(8,128)(2,1)S(1)} %get-tuple-element.156), channel_id=1, source_target_pairs={{0,8},{4,12},{8,0},{12,4},{16,24},{20,28},{24,16},{28,20},{1,9},{5... | collective-permute-start | bytes 159752 | tf_op jit(solution)/shard_map/ppermute | solution.py:667
  247.6 6.2 %collective-permute-start.35 = (bf16[16,1664]{1,0:T(8,128)(2,1)S(1)}, bf16[16,1664]{1,0:T(8,128)(2,1)S(1)}, u32[]{:S(2)}, u32[]{:S(2)}) collective-permute-start(bf16[16,1664]{1,0:T(8,128)(2,1)S(1)} %get-tuple-element.158), channel_id=1, source_target_pairs={{0,16},{4,20},{8,24},{12,28},{16,0},{20,4},{24,8},{28,12},{1,17},{... | collective-permute-start | bytes 159752 | tf_op jit(solution)/shard_map/ppermute | solution.py:667
  248.8 6.0 %collective-permute-start.36 = (bf16[16,1664]{1,0:T(8,128)(2,1)S(1)}, bf16[16,1664]{1,0:T(8,128)(2,1)S(1)}, u32[]{:S(2)}, u32[]{:S(2)}) collective-permute-start(bf16[16,1664]{1,0:T(8,128)(2,1)S(1)} %get-tuple-element.157), channel_id=1, source_target_pairs={{0,24},{4,28},{8,16},{12,20},{16,8},{20,12},{24,0},{28,4},{1,25},{... | collective-permute-start | bytes 159752 | tf_op jit(solution)/shard_map/ppermute | solution.py:667
  (12 other events, 29.6 us)
